TPU v7x, 32 devices: a whole 2x2x4 slice. The times are simulated.
32 devices in a mesh: enc: 4 (over y, core), seq: 8 (over z, x).
Axes of the slice: x: 2, y: 2, z: 4, core: 2. Of those that a mesh axis runs over, the one named last changes fastest.
Arguments:
- clip_features: bfloat16 [4, 8, 4, 16, 16, 512], P('enc', 'seq'), may hold values from -6 to 6
- clip_shape: int32 [4, 8, 3], P('enc', 'seq'), may hold values from 0 to 16, as said below
- packing: int32 [4, 8, 2, 2], P('enc', 'seq'), may hold values from -1 to 3, as said below
- conv_weight: bfloat16 [27, 16, 512], replicated, may hold values from -0.0546875 to 0.0546875
- embed_weight: bfloat16 [64, 2048], replicated, may hold values from -0.75 to 0.75
- mod_shift: float32 [2048], replicated, may hold values from -3 to 3
- mod_scale: float32 [2048], replicated, may hold values from -2 to 2
- qkv_weight: bfloat16 [3, 2048, 2048], P(None, 'seq', 'enc'), may hold values from -0.125 to 0.125
- q_gain: float32 [128], replicated, may hold values from 0.9 to 1.8
- k_gain: float32 [128], replicated, may hold values from 0.9 to 1.8
Outputs:
- attended: bfloat16 [8, 512, 2048], P('seq', 'enc')
Inputs may be any that keep to these rules, and one draw needn't show every extreme that they name: `clip_shape`: Frames, height and width of each device's clip in latent pixels; height and width are even and at least 2, frames at most 4, height at most 16, width at most 16, and frames * height * width / 4 at most 256. Frames is 0 on some devices of every seq index; in every draw some device of each seq index has a clip of 4 x 16 x 16. `packing`: for each block slot: the enc index that owns it in its buffer and its block offset there, below the number of enc devices and below 1; both are -1 exactly for the slots past a clip's last token. Among the devices of one seq index no two blocks name the same owner and offset.
All inputs are finite; a program needn't handle non-finite values.
Results may differ from a plain program's by a relative error of at most 0.0075.
Values may be sent and summed in bfloat16 or wider, within the bound.
No kernel may reach another device: no remote copies, remote signals or barrier semaphores. Data moves between devices by JAX's collectives and lax.ppermute only.
A program may use at most 128 MiB of HBM per device.

v0:
```python
import functools
import math

import jax
import jax.numpy as jnp
from jax import lax
from jax.experimental import pallas as pl
from jax.experimental.pallas import tpu as pltpu
from jax.sharding import PartitionSpec as P

BLOCK = 128
NBS = 2
LANES = 128
APAD = 72
TAIL = 8
TOKEN_ROWS = 80
eps_norm = 1e-06
FAR = 2.0**20
VMEM_LIMIT = 48 * 1024 * 1024


def mm(a, b, dims=((1,), (0,)), precision=None):
    return lax.dot_general(a, b, (dims, ((), ())), preferred_element_type=jnp.float32, precision=precision)


def split_bf16(x):
    hi = x.astype(jnp.bfloat16)
    return hi, (x - hi.astype(jnp.float32)).astype(jnp.bfloat16)


def log2(n):
    bits = n.bit_length() - 1
    assert 1 << bits == n
    return bits


def fetch(pairs, sems):
    copies = [pltpu.make_async_copy(src, dst, sems.at[i]) for i, (src, dst) in enumerate(pairs)]
    for copy in copies:
        copy.start()
    return copies


def fold_kernel(count, embed_hbm, scale_hbm, shift_hbm, w_hbm, *refs):
    later_hbm, embed_ref, later, keep_ref, sends = refs[:count], refs[count], refs[count + 1 : 2 * count + 1], refs[2 * count + 1], refs[2 * count + 2 : -4]
    scale_ref, shift_ref, w_ref, sems = refs[-4:]
    copies = fetch(
        [(embed_hbm, embed_ref), (scale_hbm, scale_ref), (shift_hbm, shift_ref), (w_hbm, w_ref)]
        + list(zip(later_hbm, later)),
        sems,
    )
    me = lax.axis_index("seq")
    _, depth, cols = w_ref.shape
    feats = embed_ref.shape[0]
    heads = cols // LANES
    for copy in copies[:3]:
        copy.wait()
    mean = jnp.sum(embed_ref[...].astype(jnp.float32), axis=1, keepdims=True) / embed_ref.shape[1]
    span = max(depth, LANES)
    chunks = span // LANES
    first = (me * depth) // LANES
    emb = embed_ref[:, pl.ds(pl.multiple_of(first * LANES, LANES), span)].astype(jnp.float32) - mean
    scale = jnp.concatenate([scale_ref[pl.ds(first + i, 1), :] for i in range(chunks)], axis=1)
    shift = jnp.concatenate([shift_ref[pl.ds(first + i, 1), :] for i in range(chunks)], axis=1)
    left = jnp.concatenate(
        [emb * (1.0 + scale), shift, jnp.zeros((APAD - feats - 1, span), jnp.float32)], axis=0
    )
    if depth < LANES:
        low = me * depth - first * LANES
        lane = lax.broadcasted_iota(jnp.int32, left.shape, 1)
        left = jnp.where((lane >= low) & (lane < low + depth), left, 0.0)
    hi, lo = split_bf16(left)
    both = jnp.concatenate([hi, lo], axis=0)
    copies[3].wait()

    def product(head):
        start = pl.multiple_of(head * LANES, LANES)
        right = jnp.concatenate([w_ref[part, :, pl.ds(start, LANES)] for part in range(3)], axis=1)
        right = jnp.concatenate([right] * (span // depth), axis=0)
        total = mm(both, right)
        total = total[:APAD] + total[APAD:]
        parts = [total[:, part * LANES : (part + 1) * LANES] for part in range(3)]
        row = lax.broadcasted_iota(jnp.int32, (TAIL, LANES), 0)
        tail = jnp.zeros((TAIL, LANES), jnp.float32)
        for part in range(3):
            tail = jnp.where(row == part, parts[part][feats : feats + 1], tail)
        return jnp.concatenate([part[:feats] for part in parts] + [tail], axis=0)

    slot = me & (heads - 1)
    for k in range(1, heads):
        sends[k - 1][...] = product(slot ^ k).astype(jnp.bfloat16)
    total = product(slot)
    keep_ref[...] = total
    if heads == 1:
        sends[0][...] = total.astype(jnp.bfloat16)
    for copy in copies[4:]:
        copy.wait()


def add_kernel(count, keep_in, *refs):
    total = keep_in[...]
    for ref in refs[:count]:
        total = total + ref[...].astype(jnp.float32)
    refs[-2][...] = total
    refs[-1][...] = total.astype(jnp.bfloat16)


def last_add_kernel(count, keep_in, got_ref, *refs):
    total = (keep_in[...] + got_ref[...].astype(jnp.float32)).astype(jnp.bfloat16)
    out_ref, swap_ref = refs[-2:]
    out_ref[...] = total
    swap_ref[0] = total
    for i in range(count):
        block = refs[i][...]
        rest = jnp.zeros((total.shape[0] - block.shape[0], LANES), jnp.bfloat16)
        swap_ref[1 + i] = jnp.concatenate([block, rest], axis=0)


def pair_kernel(own_ref, swapped_ref, out_ref):
    out_ref[0] = own_ref[...]
    out_ref[1] = swapped_ref[0]


def gate_kernel(*refs):
    pass


def encode_kernel(caps, shape_hbm, plan_hbm, feat_ref, conv_ref, out_ref, shape_ref, plan_ref, sems):
    copies = fetch([(shape_hbm, shape_ref), (plan_hbm, plan_ref)], sems)
    frames_cap, height_cap, width_cap = caps
    spots = frames_cap * height_cap * width_cap
    frame_size = height_cap * width_cap
    latent_ch = conv_ref.shape[0] // 27
    feats = 4 * latent_ch
    taps = mm(conv_ref[...], feat_ref[...], ((1,), (1,)))
    copies[0].wait()
    copies[1].wait()
    frames, height, width = shape_ref[0, 0, 0], shape_ref[0, 0, 1], shape_ref[0, 0, 2]
    spot = lax.broadcasted_iota(jnp.int32, (1, spots), 1)
    frame_ix = spot // frame_size
    row_ix = (spot % frame_size) // width_cap
    col_ix = spot % width_cap
    inside = (frame_ix < frames) & (row_ix < height) & (col_ix < width)
    taps = jnp.where(inside, taps, 0.0)

    def tap(a, b, j):
        at = (9 * a + 3 * b + j) * latent_ch
        return taps[at : at + latent_ch]

    def later(x, by):
        zeros = jnp.zeros((latent_ch, by * frame_size), jnp.float32)
        return jnp.concatenate([zeros, x[:, : spots - by * frame_size]], axis=1)

    def over_frames(b, j):
        return tap(2, b, j) + later(tap(1, b, j), 1) + later(tap(0, b, j), 2)

    def over_rows(j):
        above = pltpu.roll(over_frames(0, j), width_cap, 1)
        below = pltpu.roll(over_frames(2, j), spots - width_cap, 1)
        return (
            over_frames(1, j)
            + jnp.where(row_ix >= 1, above, 0.0)
            + jnp.where(row_ix < height_cap - 1, below, 0.0)
        )

    latent = (
        over_rows(1)
        + jnp.where(col_ix >= 1, pltpu.roll(over_rows(0), 1, 1), 0.0)
        + jnp.where(col_ix < width_cap - 1, pltpu.roll(over_rows(2), spots - 1, 1), 0.0)
    )
    latent = latent.astype(jnp.bfloat16).astype(jnp.float32)
    shifted = [latent] + [pltpu.roll(latent, spots - by, 1) for by in (1, width_cap, width_cap + 1)]
    patches = jnp.concatenate(shifted, axis=0).astype(jnp.bfloat16)

    tokens = NBS * BLOCK
    half_w = (width // 2).astype(jnp.float32)
    per_frame_int = (height // 2) * (width // 2)
    per_frame = per_frame_int.astype(jnp.float32)
    live = frames * per_frame_int
    token_int = lax.broadcasted_iota(jnp.int32, (1, tokens), 1)
    token = token_int.astype(jnp.float32)
    frame_of = jnp.floor((token + 0.5) / jnp.full((1, tokens), per_frame))
    within = token - frame_of * per_frame
    row_of = jnp.floor((within + 0.5) / jnp.full((1, tokens), half_w))
    col_of = within - row_of * half_w
    source = (frame_of * frame_size + row_of * (2 * width_cap) + col_of * 2).astype(jnp.int32)
    source = jnp.where(token_int < live, source, -1)
    chosen = lax.broadcasted_iota(jnp.int32, (spots, tokens), 0) == source
    picked = mm(patches, jnp.where(chosen, 1.0, 0.0).astype(jnp.bfloat16))
    kind = lax.broadcasted_iota(jnp.int32, (TOKEN_ROWS - feats, BLOCK), 0)
    pieces = []
    for b in range(NBS):
        count = jnp.clip(live - b * BLOCK, 0, BLOCK)
        info = jnp.where(
            kind == 0,
            plan_ref[0, 0, b, 0],
            jnp.where(kind == 1, plan_ref[0, 0, b, 1], jnp.where(kind == 2, count, 0)),
        )
        pieces += [picked[:, b * BLOCK : (b + 1) * BLOCK], info.astype(jnp.float32)]
    out_ref[...] = jnp.concatenate(pieces, axis=0).astype(jnp.bfloat16)


def gram_kernel(embed_ref, first_ref, out_ref):
    feats, width = embed_ref.shape
    emb = embed_ref[...].astype(jnp.float32)
    emb = emb - jnp.sum(emb, axis=1, keepdims=True) / width
    both = jnp.concatenate(split_bf16(emb), axis=0)
    gram = mm(both, both, ((1,), (1,))) / width
    gram = gram[:feats] + gram[feats:]
    out_ref[...] = jnp.concatenate(split_bf16(gram[:, :feats] + gram[:, feats:]), axis=0)


def pack_kernel(evens, feats, q_gain_ref, k_gain_ref, gram_ref, *refs):
    here, near = refs[: len(evens)], refs[len(evens)]
    x_t_ref, x_ref, key_mask_ref, gain_ref, *row_refs, rows_t = refs[len(evens) + 1 :]
    n_enc = 2 * len(evens)
    mine = lax.axis_index("enc")
    rows = n_enc * BLOCK
    lane = lax.broadcasted_iota(jnp.int32, (1, BLOCK), 1).astype(jnp.float32)
    extra = lax.broadcasted_iota(jnp.int32, (APAD - feats, BLOCK), 0)
    found = []
    blocks = [(at, here[i][...]) for i, at in enumerate(evens)]
    blocks += [(at ^ 1, near[1 + i]) for i, at in enumerate(evens)]
    for distance, block in blocks:
        source = mine ^ distance
        for b in range(NBS):
            tile = block.astype(jnp.float32)[b * TOKEN_ROWS : (b + 1) * TOKEN_ROWS]
            owner, offset, count = (tile[feats + i : feats + i + 1] for i in range(3))
            owner = jnp.where(offset == 0.0, owner, -1.0)
            segment = jnp.where(lane < count, (source + 1).astype(jnp.float32), 0.0)
            found.append((owner, segment, tile[:feats]))
    at = lax.broadcasted_iota(jnp.int32, (feats, feats), 0)
    frm = lax.broadcasted_iota(jnp.int32, (feats, feats), 1)
    order = jnp.where(frm == (at % 4) * (feats // 4) + at // 4, 1.0, 0.0).astype(jnp.bfloat16)
    for o in range(n_enc):
        segment = jnp.zeros((1, BLOCK), jnp.float32)
        body = jnp.zeros((feats, BLOCK), jnp.float32)
        for owner, seg_of, tile in found:
            hit = owner == float(o)
            segment = segment + jnp.where(hit, seg_of, 0.0)
            body = body + jnp.where(hit, tile, 0.0)
        tail = jnp.where(extra == 0, 1.0, jnp.where(extra == 1, segment, 0.0))
        rows_t[:, o * BLOCK : (o + 1) * BLOCK] = jnp.concatenate(
            [body, tail, jnp.zeros((LANES - APAD, BLOCK), jnp.float32)], axis=0
        )
    picked = mm(order, rows_t[:feats].astype(jnp.bfloat16))
    spread = mm(gram_ref[...], picked.astype(jnp.bfloat16))
    variance = jnp.sum((spread[:feats] + spread[feats:]) * picked, axis=0, keepdims=True)
    rows_t[:feats] = picked * lax.rsqrt(jnp.maximum(variance, 0.0) + eps_norm)
    x_t = rows_t[...]
    x_t_ref[...] = x_t[:APAD].astype(jnp.bfloat16)
    x_ref[...] = x_t.T.astype(jnp.bfloat16)
    group_t = lax.broadcasted_iota(jnp.int32, (LANES, rows), 0).astype(jnp.float32)
    key_mask_ref[...] = jnp.where(x_t[feats + 1 : feats + 2] == group_t, 0.0, 1.0).astype(jnp.bfloat16)
    group = lax.broadcasted_iota(jnp.int32, (BLOCK, LANES), 1).astype(jnp.float32)
    for core in range(2):
        rows_ref, mask_ref = row_refs[2 * core : 2 * core + 2]
        own = rows_t[:, pl.ds(pl.multiple_of((mine ^ core) * BLOCK, BLOCK), BLOCK)].T
        rows_ref[...] = own.astype(jnp.bfloat16)
        mask_ref[...] = jnp.where(own[:, feats + 1 : feats + 2] == group, -FAR, 0.0).astype(jnp.bfloat16)
    head_dim = q_gain_ref.shape[1]
    gain_ref[...] = q_gain_ref[...] * k_gain_ref[...] * (head_dim**-0.5 * math.log2(math.e))


def attend_heads(folds, place, x_t_ref, x_ref, key_mask_ref, gain_ref, own_ref, own_mask_ref):
    folds = list(folds)
    heads = range(len(folds))
    feats = (folds[0].shape[0] - TAIL) // 3
    tails = jnp.concatenate([fold[3 * feats :].astype(jnp.float32) for fold in folds], axis=1)
    row = lax.broadcasted_iota(jnp.int32, tails.shape, 0)

    def side(part):
        body = jnp.concatenate([fold[part * feats : (part + 1) * feats] for fold in folds], axis=1)
        shift = jnp.where(row == 0, tails[part : part + 1], 0.0).astype(jnp.bfloat16)
        return jnp.concatenate([body, shift], axis=0)

    def of(i):
        return slice(i * LANES, (i + 1) * LANES)

    keys = mm(side(1), x_t_ref[...], ((0,), (0,)))
    queries = mm(own_ref[:, :APAD], side(0))
    values = mm(x_ref[:, :APAD], side(2)).astype(jnp.bfloat16)
    gain, own_mask, key_mask = gain_ref[...], own_mask_ref[...], key_mask_ref[...]
    left, right = [], []
    for i in heads:
        key = keys[of(i)]
        square = jnp.sum(key * key, axis=0, keepdims=True) / LANES
        key = (key * lax.rsqrt(square + eps_norm)).astype(jnp.bfloat16)
        right.append(jnp.concatenate([key, key_mask], axis=0))
        query = queries[:, of(i)]
        square = jnp.sum(query * query, axis=1, keepdims=True) / LANES
        query = (query * lax.rsqrt(square + eps_norm) * gain).astype(jnp.bfloat16)
        left.append(jnp.concatenate([query, own_mask], axis=1))
    scores = [mm(left[i], right[i]) for i in heads]
    weights = [jnp.exp2(score).astype(jnp.bfloat16) for score in scores]
    ones = jnp.ones((values.shape[0], LANES), jnp.bfloat16)
    mixed = [mm(weights[i], jnp.concatenate([values[:, of(i)], ones], axis=1)) for i in heads]
    for i in heads:
        place(i, (mixed[i][:, :LANES] / mixed[i][:, LANES:]).astype(jnp.bfloat16))


def each_head(refs):
    for ref in refs:
        if len(ref.shape) == 2:
            yield ref[...]
        else:
            for i in range(ref.shape[0]):
                yield ref[i]


def attend_kernel(count, *refs):
    folds, out_ref = refs[6 : 6 + count], refs[-1]
    first = 0
    if len(refs) > 7 + count:
        done_ref = refs[6 + count]
        first = done_ref.shape[1] // LANES
        out_ref[:, : first * LANES] = done_ref[...]

    def place(i, result):
        out_ref[:, (first + i) * LANES : (first + i + 1) * LANES] = result

    attend_heads(each_head(folds), place, *refs[:6])


def output_kernel(heads, neighbours, lists, own_ref, near_ref, out_ref, sems):
    mine, slot = lax.axis_index("enc"), lax.axis_index("seq") & (heads - 1)
    copies = []

    def put(ref, at, base, far, k):
        head = (base ^ far) * heads + (slot ^ k)
        column = pl.ds(pl.multiple_of(head * LANES, LANES), LANES)
        result = ref.at[:, at * LANES : (at + 1) * LANES]
        copies.append(pltpu.make_async_copy(result, out_ref.at[0, :, column], sems.at[len(copies)]))
        copies[-1].start()

    for ref, base in ((near_ref, mine ^ 1), (own_ref, mine)):
        first = 1 + len(neighbours)
        for at, partner in enumerate(((0, 0), *neighbours)):
            put(ref, at, base, *partner)
        for i, pair in enumerate(zip(*lists)):
            far, k = (jnp.where(base & 1 == 0, zero, one) for zero, one in zip(*pair))
            put(ref, first + 2 * i, base, far, k)
            put(ref, first + 2 * i + 1, base, far ^ 1, k)
    for copy in copies:
        copy.wait()


def vmem(count):
    return [pl.BlockSpec(memory_space=pltpu.VMEM)] * count


def hbm(count):
    return [pl.BlockSpec(memory_space=pltpu.HBM)] * count


def in_hbm(x):
    return pltpu.with_memory_space_constraint(x, pltpu.HBM)


def after(count):
    return [pl.BlockSpec(memory_space=pl.ANY)] * count


def call(kernel, ins, out_shape, scratch=(), cost=(1_000_000, 1_000_000)):
    return pl.pallas_call(
        kernel,
        in_specs=ins,
        out_specs=[pl.BlockSpec(memory_space=pltpu.VMEM)] * len(out_shape),
        out_shape=out_shape,
        scratch_shapes=list(scratch),
        compiler_params=pltpu.CompilerParams(vmem_limit_bytes=VMEM_LIMIT),
        cost_estimate=pl.CostEstimate(flops=cost[0], bytes_accessed=cost[1], transcendentals=0),
    )


def gate(x, *others):
    return pl.pallas_call(
        gate_kernel,
        in_specs=after(1 + len(others)),
        out_specs=after(1)[0],
        out_shape=jax.ShapeDtypeStruct(x.shape, x.dtype),
        input_output_aliases={0: 0},
        compiler_params=pltpu.CompilerParams(vmem_limit_bytes=VMEM_LIMIT),
    )(x, *others)


def exchange(x, axis, n, k):
    return lax.ppermute(x, axis, [(i, i ^ k) for i in range(n)])


def on_device(
    n_enc,
    n_seq,
    clip_features,
    clip_shape,
    packing,
    conv_weight,
    embed_weight,
    mod_shift,
    mod_scale,
    qkv_weight,
    q_gain,
    k_gain,
):
    caps = clip_features.shape[2:5]
    depth_all = clip_features.shape[5]
    cols = qkv_weight.shape[2]
    feats = embed_weight.shape[0]
    heads = cols // LANES
    rows = n_enc * BLOCK
    bf16, f32 = jnp.bfloat16, jnp.float32

    def folds(dtype, *lead):
        return jax.ShapeDtypeStruct((*lead, 3 * feats + TAIL, LANES), dtype)

    evens = [0]
    for bit in reversed(range(1, log2(n_enc))):
        evens += [at ^ (1 << bit) for at in evens]
    scale_rows, shift_rows = mod_scale.reshape(-1, LANES), mod_shift.reshape(-1, LANES)
    later = [
        clip_features.reshape(-1, depth_all),
        conv_weight.reshape(-1, depth_all),
        q_gain.reshape(1, -1),
        k_gain.reshape(1, -1),
    ]
    with jax.named_scope("fold"):
        embed, features, conv, q_gain, k_gain, keep, *sends = call(
            functools.partial(fold_kernel, len(later)),
            hbm(4 + len(later)),
            [jax.ShapeDtypeStruct(x.shape, x.dtype) for x in (embed_weight, *later)]
            + [folds(f32)]
            + [folds(bf16)] * max(heads - 1, 1),
            [
                pltpu.VMEM(scale_rows.shape, f32),
                pltpu.VMEM(shift_rows.shape, f32),
                pltpu.VMEM(qkv_weight.shape, bf16),
                pltpu.SemaphoreType.DMA((4 + len(later),)),
            ],
            cost=(200_000_000, 1_000_000),
        )(*map(in_hbm, (embed_weight, scale_rows, shift_rows, qkv_weight, *later)))

    with jax.named_scope("encode"):
        own_block = call(
            functools.partial(encode_kernel, caps),
            hbm(2) + vmem(2),
            [jax.ShapeDtypeStruct((NBS * TOKEN_ROWS, BLOCK), bf16)],
            [
                pltpu.SMEM(clip_shape.shape, jnp.int32),
                pltpu.SMEM(packing.shape, jnp.int32),
                pltpu.SemaphoreType.DMA((2,)),
            ],
            cost=(500_000_000, 2_000_000),
        )(in_hbm(clip_shape), in_hbm(packing), features, conv)[0]

    def add(keep, got, first):
        kernel = functools.partial(add_kernel, len(got))
        return call(kernel, vmem(1 + len(got)) + after(1), [folds(f32), folds(bf16)])(keep, *got, first)

    with jax.named_scope("fold_sum"):
        if heads > 1:
            got = [exchange(sends[k - 1], "seq", n_seq, k) for k in reversed(range(1, heads))]
            keep, send = add(keep, got, own_block)
        else:
            send = sends[0]

    with jax.named_scope("gram"):
        gram = call(gram_kernel, vmem(1) + after(1), [jax.ShapeDtypeStruct((2 * feats, feats), bf16)])(embed, keep)[0]

    with jax.named_scope("tokens"):
        own_block = gate(own_block, keep)
        blocks = [own_block] + [exchange(own_block, "enc", n_enc, k) for k in evens[1:]]

    with jax.named_scope("fold_sum"):
        for bit in range(log2(heads), log2(n_seq)):
            got = exchange(send, "seq", n_seq, 1 << bit)
            if bit + 1 < log2(n_seq):
                keep, send = add(keep, [got], own_block)
            else:
                fresh, swap = call(
                    functools.partial(last_add_kernel, len(blocks)),
                    vmem(2 + len(blocks)) + after(1),
                    [folds(bf16), folds(bf16, 1 + len(blocks))],
                )(keep, got, *blocks, gram)

    partners = [(far, k) for far in evens for k in range(heads) if far or k]
    partners.sort(key=lambda p: (p[0].bit_count() + p[1].bit_count(), p[0]))
    near_count = min(3, len(partners))
    half = (len(partners) - near_count) // 2
    assert len(partners) == near_count + 2 * half
    neighbours = tuple(partners[:near_count])
    lists = (tuple(partners[near_count : near_count + half]), tuple(partners[near_count + half :]))

    def spread(x, partner_of):
        pairs = []
        for e in range(n_enc):
            far, k = partner_of[e & 1]
            pairs += [(e * n_seq + i, (e ^ far) * n_seq + (i ^ k)) for i in range(n_seq)]
        return lax.ppermute(x, ("enc", "seq"), pairs)

    with jax.named_scope("gather"):
        singles = [spread(fresh, (partner, partner)) for partner in neighbours]
        swapped = exchange(swap, "enc", n_enc, 1)
        pair = call(pair_kernel, vmem(2), [folds(bf16, 2)])(fresh, swapped)[0]
        got = [spread(pair, partner_of) for partner_of in zip(*lists)]

    with jax.named_scope("pack"):
        *shared, own_rows, own_mask, far_rows, far_mask = call(
            functools.partial(pack_kernel, tuple(evens), feats),
            vmem(4 + len(evens)),
            [
                jax.ShapeDtypeStruct((APAD, rows), bf16),
                jax.ShapeDtypeStruct((rows, LANES), bf16),
                jax.ShapeDtypeStruct((LANES, rows), bf16),
                jax.ShapeDtypeStruct((1, LANES), f32),
            ]
            + [jax.ShapeDtypeStruct((BLOCK, LANES), bf16)] * 4,
            [pltpu.VMEM((LANES, rows), f32)],
        )(q_gain, k_gain, gram, *blocks, swapped)

    def attend(rows_here, groups, done=(), first=()):
        count = sum(group.size for group in groups) // ((3 * feats + TAIL) * LANES)
        total = count + sum(x.shape[1] for x in done) // LANES
        return call(
            functools.partial(attend_kernel, len(groups)),
            vmem(6 + len(groups) + len(done)) + after(len(first)),
            [jax.ShapeDtypeStruct((BLOCK, total * LANES), bf16)],
            cost=(count * 200_000_000, 1_000_000),
        )(*shared, *rows_here, *groups, *done, *first)[0]

    with jax.named_scope("attend"):
        own, other = (own_rows, own_mask), (far_rows, far_mask)
        early, rest = [fresh, *singles], got
        early_other, early_own = attend(other, early), attend(own, early)
        near = exchange(attend(other, rest, [early_other], [early_own]), "enc", n_enc, 1)
        own_done = attend(own, rest, [early_own])
        return pl.pallas_call(
            functools.partial(output_kernel, heads, neighbours, lists),
            in_specs=vmem(2),
            out_specs=hbm(1)[0],
            out_shape=jax.ShapeDtypeStruct((1, BLOCK, n_enc * cols), bf16),
            scratch_shapes=[pltpu.SemaphoreType.DMA((n_enc * heads,))],
            compiler_params=pltpu.CompilerParams(vmem_limit_bytes=VMEM_LIMIT),
        )(own_done, near)


def solution(mesh):
    return jax.shard_map(
        functools.partial(on_device, mesh.shape["enc"], mesh.shape["seq"]),
        mesh=mesh,
        in_specs=(
            P("enc", "seq", None, None, None, None),
            P("enc", "seq", None),
            P("enc", "seq", None, None),
            P(),
            P(),
            P(),
            P(),
            P(None, "seq", "enc"),
            P(),
            P(),
        ),
        out_specs=P("seq", "enc", None),
        check_vma=False,
    )
```

profile of v0, /device:TPU:0, one launch (start us, length us, event | category | flops | bytes accessed | tf_op | source)
XLA Modules:
  0.0 31.5 jit_solution(8461662200511496479)
XLA Ops:
  0.0 1.8 %fold.1 = (bf16[64,2048]{1,0:T(8,128)(2,1)S(1)}, bf16[1024,512]{1,0:T(8,128)(2,1)S(1)}, bf16[432,512]{1,0:T(8,128)(2,1)S(1)}, f32[1,128]{1,0:T(1,128)S(1)}, f32[...) custom-call(bf16[64,2048]{1,0:T(8,128)(2,1)} %embed_hbm.1, ...), custom_call_target="tpu_custom_call" | custom-call | flops 200000000 | bytes 1000000 | tf_op jit(solution)/shard_map/fold/pallas_call | solution.py:427
  1.8 4.0 %collective-permute-start = (bf16[200,128]{1,0:T(8,128)(2,1)S(1)}, bf16[200,128]{1,0:T(8,128)(2,1)S(1)}, u32[]{:S(2)}, u32[]{:S(2)}) collective-permute-start(bf16[200,128]{1,0:T(8,128)(2,1)S(1)} %get-tuple-element.30), channel_id=1, source_target_pairs={{0,3},{1,2},{2,1},{3,0},{4,7},{5,6},{6,5},{7,4},{8,11},{9,10},{10,... | collective-permute-start | bytes 153608 | tf_op jit(solution)/shard_map/fold_sum/ppermute | solution.py:388
  5.8 0.4 %collective-permute-start.1 = (bf16[200,128]{1,0:T(8,128)(2,1)S(1)}, bf16[200,128]{1,0:T(8,128)(2,1)S(1)}, u32[]{:S(2)}, u32[]{:S(2)}) collective-permute-start(bf16[200,128]{1,0:T(8,128)(2,1)S(1)} %get-tuple-element.31), channel_id=1, source_target_pairs={{0,2},{1,3},{2,0},{3,1},{4,6},{5,7},{6,4},{7,5},{8,10},{9,11},{10,... | collective-permute-start | bytes 153608 | tf_op jit(solution)/shard_map/fold_sum/ppermute | solution.py:388
  6.4 1.7 %encode.1.refs_3_.refs_0_ = bf16[160,128]{1,0:T(8,128)(2,1)S(1)} custom-call(s32[1,1,3]{2,1,0:T(1,128)} %shape_hbm.1, s32[1,1,2,2]{3,2,1,0:T(2,128)} %plan_hbm.1, bf16[1024,512]{1,0:T(8,128)(2,1)S(1)} %get-tuple-element.33.feat_ref, bf16[432,512]{1,0:T(8,128)(2,1)S(1)} %get-tuple-element.34.conv_ref), custom_call_target="tpu_custom_call" | custom-call | flops 500000000 | bytes 2000000 | tf_op jit(solution)/shard_map/encode/pallas_call | solution.py:443
  8.2 1.7 %collective-permute-done.1.refs_1_ = bf16[200,128]{1,0:T(8,128)(2,1)S(1)} collective-permute-done((bf16[200,128]{1,0:T(8,128)(2,1)S(1)}, bf16[200,128]{1,0:T(8,128)(2,1)S(1)}, u32[]{:S(2)}, u32[]{:S(2)}) %collective-permute-start.1) | collective-permute-done | bytes 51232 | tf_op jit(solution)/shard_map/fold_sum/ppermute | solution.py:388
  9.9 0.4 %collective-permute-done.2.refs_2_ = bf16[200,128]{1,0:T(8,128)(2,1)S(1)} collective-permute-done((bf16[200,128]{1,0:T(8,128)(2,1)S(1)}, bf16[200,128]{1,0:T(8,128)(2,1)S(1)}, u32[]{:S(2)}, u32[]{:S(2)}) %collective-permute-start.2) | collective-permute-done | bytes 51232 | tf_op jit(solution)/shard_map/fold_sum/ppermute | solution.py:388
  10.4 2.7 %collective-permute-start.4 = (bf16[200,128]{1,0:T(8,128)(2,1)S(1)}, bf16[200,128]{1,0:T(8,128)(2,1)S(1)}, u32[]{:S(2)}, u32[]{:S(2)}) collective-permute-start(bf16[200,128]{1,0:T(8,128)(2,1)S(1)} %get-tuple-element.36), channel_id=1, source_target_pairs={{0,4},{1,5},{2,6},{3,7},{4,0},{5,1},{6,2},{7,3},{8,12},{9,13},{10,... | collective-permute-start | bytes 153608 | tf_op jit(solution)/shard_map/fold_sum/ppermute | solution.py:388
  13.0 1.5 %collective-permute-start.3 = (bf16[160,128]{1,0:T(8,128)(2,1)S(1)}, bf16[160,128]{1,0:T(8,128)(2,1)S(1)}, u32[]{:S(2)}, u32[]{:S(2)}) collective-permute-start(bf16[160,128]{1,0:T(8,128)(2,1)S(1)} %tokens.1.refs_0_), channel_id=1, source_target_pairs={{0,16},{8,24},{16,0},{24,8},{1,17},{9,25},{17,1},{25,9},{2,18},{10... | collective-permute-start | bytes 122888 | tf_op jit(solution)/shard_map/tokens/ppermute | solution.py:388
  14.6 0.5 %gram.1.refs_2_.gram_ref = bf16[128,64]{1,0:T(8,128)(2,1)S(1)} custom-call(bf16[64,2048]{1,0:T(8,128)(2,1)S(1)} %get-tuple-element.28.embed_ref, f32[200,128]{1,0:T(8,128)S(1)} %get-tuple-element.35.first_ref.refs_1_.keep_in), custom_call_target="tpu_custom_call" | custom-call | flops 1000000 | bytes 1000000 | tf_op jit(solution)/shard_map/gram/pallas_call | solution.py:467
  15.0 2.0 %collective-permute-done.3.refs_1_ = bf16[160,128]{1,0:T(8,128)(2,1)S(1)} collective-permute-done((bf16[160,128]{1,0:T(8,128)(2,1)S(1)}, bf16[160,128]{1,0:T(8,128)(2,1)S(1)}, u32[]{:S(2)}, u32[]{:S(2)}) %collective-permute-start.3) | collective-permute-done | bytes 40992 | tf_op jit(solution)/shard_map/tokens/ppermute | solution.py:388
  17.1 1.6 %collective-permute-start.10 = (bf16[200,128]{1,0:T(8,128)(2,1)S(1)}, bf16[200,128]{1,0:T(8,128)(2,1)S(1)}, u32[]{:S(2)}, u32[]{:S(2)}) collective-permute-start(bf16[200,128]{1,0:T(8,128)(2,1)S(1)} %get-tuple-element.44.own_ref.refs_6_), channel_id=1, source_target_pairs={{0,16},{1,17},{2,18},{3,19},{4,20},{5,21},{6,22},{7,23},{8,24},{9,... | collective-permute-start | bytes 153608 | tf_op jit(solution)/shard_map/gather/ppermute | solution.py:498
  18.7 1.6 %collective-permute-start.9 = (bf16[200,128]{1,0:T(8,128)(2,1)S(1)}, bf16[200,128]{1,0:T(8,128)(2,1)S(1)}, u32[]{:S(2)}, u32[]{:S(2)}) collective-permute-start(bf16[200,128]{1,0:T(8,128)(2,1)S(1)} %get-tuple-element.44.own_ref.refs_6_), channel_id=1, source_target_pairs={{0,2},{1,3},{2,0},{3,1},{4,6},{5,7},{6,4},{7,5},{8,10},{9,11},{10,... | collective-permute-start | bytes 153608 | tf_op jit(solution)/shard_map/gather/ppermute | solution.py:498
  20.3 0.5 %collective-permute-start.8 = (bf16[200,128]{1,0:T(8,128)(2,1)S(1)}, bf16[200,128]{1,0:T(8,128)(2,1)S(1)}, u32[]{:S(2)}, u32[]{:S(2)}) collective-permute-start(bf16[200,128]{1,0:T(8,128)(2,1)S(1)} %get-tuple-element.44.own_ref.refs_6_), channel_id=1, source_target_pairs={{0,1},{1,0},{2,3},{3,2},{4,5},{5,4},{6,7},{7,6},{8,9},{9,8},{10,11... | collective-permute-start | bytes 153608 | tf_op jit(solution)/shard_map/gather/ppermute | solution.py:498
  20.9 1.5 %collective-permute-start.7 = (bf16[2,200,128]{2,1,0:T(8,128)(2,1)S(1)}, bf16[2,200,128]{2,1,0:T(8,128)(2,1)S(1)}, u32[]{:S(2)}, u32[]{:S(2)}) collective-permute-start(bf16[2,200,128]{2,1,0:T(8,128)(2,1)S(1)} %gather.1), channel_id=1, source_target_pairs={{0,17},{1,16},{2,19},{3,18},{4,21},{5,20},{6,23},{7,22},{8,27},{9,... | collective-permute-start | bytes 307208 | tf_op jit(solution)/shard_map/gather/ppermute | solution.py:498
  22.4 0.4 %collective-permute-start.6 = (bf16[2,200,128]{2,1,0:T(8,128)(2,1)S(1)}, bf16[2,200,128]{2,1,0:T(8,128)(2,1)S(1)}, u32[]{:S(2)}, u32[]{:S(2)}) collective-permute-start(bf16[2,200,128]{2,1,0:T(8,128)(2,1)S(1)} %gather.1), channel_id=1, source_target_pairs={{0,3},{1,2},{2,1},{3,0},{4,7},{5,6},{6,5},{7,4},{8,26},{9,27},{10,... | collective-permute-start | bytes 307208 | tf_op jit(solution)/shard_map/gather/ppermute | solution.py:498
  22.8 0.7 %pack.1 = (bf16[72,512]{1,0:T(8,128)(2,1)S(1)}, bf16[512,128]{1,0:T(8,128)(2,1)S(1)}, bf16[128,512]{1,0:T(8,128)(2,1)S(1)}, f32[1,128]{1,0:T(1,128)S(1)}, bf16[1...) custom-call(f32[1,128]{1,0:T(1,128)S(1)} %get-tuple-element.26.q_gai, ...), custom_call_target="tpu_custom_call" | custom-call | flops 1000000 | bytes 1000000 | tf_op jit(solution)/shard_map/pack/pallas_call | solution.py:507
  23.6 2.0 %collective-permute-done.8.refs_7_ = bf16[200,128]{1,0:T(8,128)(2,1)S(1)} collective-permute-done((bf16[200,128]{1,0:T(8,128)(2,1)S(1)}, bf16[200,128]{1,0:T(8,128)(2,1)S(1)}, u32[]{:S(2)}, u32[]{:S(2)}) %collective-permute-start.8) | collective-permute-done | bytes 51232 | tf_op jit(solution)/shard_map/gather/ppermute | solution.py:498
  25.5 0.9 %attend.5.refs_8_.refs_9_ = bf16[128,512]{1,0:T(8,128)(2,1)S(1)} custom-call(bf16[72,512]{1,0:T(8,128)(2,1)S(1)} %get-tuple-element.38.refs_0_, bf16[512,128]{1,0:T(8,128)(2,1)S(1)} %get-tuple-element.39.refs_1_, bf16[128,512]{1,0:T(8,128)(2,1)S(1)} %get-tuple-element.40.refs_2_, f32[1,128]{1,0:T(1,128)S(1)} %get-tuple-element.41.refs_3_, ...), custom_call_target="tpu_custom_call" | custom-call | flops 800000000 | bytes 1000000 | tf_op jit(solution)/shard_map/attend/pallas_call | solution.py:523
  26.4 0.9 %attend.7.refs_8_ = bf16[128,512]{1,0:T(8,128)(2,1)S(1)} custom-call(bf16[72,512]{1,0:T(8,128)(2,1)S(1)} %get-tuple-element.38.refs_0_, bf16[512,128]{1,0:T(8,128)(2,1)S(1)} %get-tuple-element.39.refs_1_, bf16[128,512]{1,0:T(8,128)(2,1)S(1)} %get-tuple-element.40.refs_2_, f32[1,128]{1,0:T(1,128)S(1)} %get-tuple-element.41.refs_3_, ...), custom_call_target="tpu_custom_call" | custom-call | flops 800000000 | bytes 1000000 | tf_op jit(solution)/shard_map/attend/pallas_call | solution.py:523
  27.3 0.8 %collective-permute-done.7.refs_7_ = bf16[2,200,128]{2,1,0:T(8,128)(2,1)S(1)} collective-permute-done((bf16[2,200,128]{2,1,0:T(8,128)(2,1)S(1)}, bf16[2,200,128]{2,1,0:T(8,128)(2,1)S(1)}, u32[]{:S(2)}, u32[]{:S(2)}) %collective-permute-start.7) | collective-permute-done | bytes 102432 | tf_op jit(solution)/shard_map/gather/ppermute | solution.py:498
  28.1 0.9 %attend.8 = bf16[128,1024]{1,0:T(8,128)(2,1)S(1)} custom-call(bf16[72,512]{1,0:T(8,128)(2,1)S(1)} %get-tuple-element.38.refs_0_, bf16[512,128]{1,0:T(8,128)(2,1)S(1)} %get-tuple-element.39.refs_1_, bf16[128,512]{1,0:T(8,128)(2,1)S(1)} %get-tuple-element.40.refs_2_, f32[1,128]{1,0:T(1,128)S(1)} %get-tuple-element.41.refs_3_, ...), custom_call_target="tpu_custom_call" | custom-call | flops 800000000 | bytes 1000000 | tf_op jit(solution)/shard_map/attend/pallas_call | solution.py:523
  29.1 0.9 %attend.6.own_ref = bf16[128,1024]{1,0:T(8,128)(2,1)S(1)} custom-call(bf16[72,512]{1,0:T(8,128)(2,1)S(1)} %get-tuple-element.38.refs_0_, bf16[512,128]{1,0:T(8,128)(2,1)S(1)} %get-tuple-element.39.refs_1_, bf16[128,512]{1,0:T(8,128)(2,1)S(1)} %get-tuple-element.40.refs_2_, f32[1,128]{1,0:T(1,128)S(1)} %get-tuple-element.41.refs_3_, ...), custom_call_target="tpu_custom_call" | custom-call | flops 800000000 | bytes 1000000 | tf_op jit(solution)/shard_map/attend/pallas_call | solution.py:523
  29.9 0.7 %collective-permute-done.11.near_ref = bf16[128,1024]{1,0:T(8,128)(2,1)S(1)} collective-permute-done((bf16[128,1024]{1,0:T(8,128)(2,1)S(1)}, bf16[128,1024]{1,0:T(8,128)(2,1)S(1)}, u32[]{:S(2)}, u32[]{:S(2)}) %collective-permute-start.11) | collective-permute-done | bytes 262176 | tf_op jit(solution)/shard_map/attend/ppermute | solution.py:388
  30.6 0.9 %attend.9 = bf16[1,128,2048]{2,1,0:T(8,128)(2,1)} custom-call(bf16[128,1024]{1,0:T(8,128)(2,1)S(1)} %attend.6.own_ref, bf16[128,1024]{1,0:T(8,128)(2,1)S(1)} %collective-permute-done.11.near_ref), custom_call_target="tpu_custom_call" | custom-call | tf_op jit(solution)/shard_map/attend/pallas_call | solution.py:536
  (13 shorter events, 0.4 us)
Async XLA Ops:
  1.8 6.4 %collective-permute-start = (bf16[200,128]{1,0:T(8,128)(2,1)S(1)}, bf16[200,128]{1,0:T(8,128)(2,1)S(1)}, u32[]{:S(2)}, u32[]{:S(2)}) collective-permute-start(bf16[200,128]{1,0:T(8,128)(2,1)S(1)} %get-tuple-element.30), channel_id=1, source_target_pairs={{0,3},{1,2},{2,1},{3,0},{4,7},{5,6},{6,5},{7,4},{8,11},{9,10},{10,... | collective-permute-start | bytes 153608 | tf_op jit(solution)/shard_map/fold_sum/ppermute | solution.py:388
  5.8 4.1 %collective-permute-start.1 = (bf16[200,128]{1,0:T(8,128)(2,1)S(1)}, bf16[200,128]{1,0:T(8,128)(2,1)S(1)}, u32[]{:S(2)}, u32[]{:S(2)}) collective-permute-start(bf16[200,128]{1,0:T(8,128)(2,1)S(1)} %get-tuple-element.31), channel_id=1, source_target_pairs={{0,2},{1,3},{2,0},{3,1},{4,6},{5,7},{6,4},{7,5},{8,10},{9,11},{10,... | collective-permute-start | bytes 153608 | tf_op jit(solution)/shard_map/fold_sum/ppermute | solution.py:388
  6.2 4.1 %collective-permute-start.2 = (bf16[200,128]{1,0:T(8,128)(2,1)S(1)}, bf16[200,128]{1,0:T(8,128)(2,1)S(1)}, u32[]{:S(2)}, u32[]{:S(2)}) collective-permute-start(bf16[200,128]{1,0:T(8,128)(2,1)S(1)} %get-tuple-element.32), channel_id=1, source_target_pairs={{0,1},{1,0},{2,3},{3,2},{4,5},{5,4},{6,7},{7,6},{8,9},{9,8},{10,11... | collective-permute-start | bytes 153608 | tf_op jit(solution)/shard_map/fold_sum/ppermute | solution.py:388
  10.4 6.7 %collective-permute-start.4 = (bf16[200,128]{1,0:T(8,128)(2,1)S(1)}, bf16[200,128]{1,0:T(8,128)(2,1)S(1)}, u32[]{:S(2)}, u32[]{:S(2)}) collective-permute-start(bf16[200,128]{1,0:T(8,128)(2,1)S(1)} %get-tuple-element.36), channel_id=1, source_target_pairs={{0,4},{1,5},{2,6},{3,7},{4,0},{5,1},{6,2},{7,3},{8,12},{9,13},{10,... | collective-permute-start | bytes 153608 | tf_op jit(solution)/shard_map/fold_sum/ppermute | solution.py:388
  13.0 4.0 %collective-permute-start.3 = (bf16[160,128]{1,0:T(8,128)(2,1)S(1)}, bf16[160,128]{1,0:T(8,128)(2,1)S(1)}, u32[]{:S(2)}, u32[]{:S(2)}) collective-permute-start(bf16[160,128]{1,0:T(8,128)(2,1)S(1)} %tokens.1.refs_0_), channel_id=1, source_target_pairs={{0,16},{8,24},{16,0},{24,8},{1,17},{9,25},{17,1},{25,9},{2,18},{10... | collective-permute-start | bytes 122888 | tf_op jit(solution)/shard_map/tokens/ppermute | solution.py:388
  17.1 3.8 %collective-permute-start.5 = (bf16[3,200,128]{2,1,0:T(8,128)(2,1)S(1)}, bf16[3,200,128]{2,1,0:T(8,128)(2,1)S(1)}, u32[]{:S(2)}, u32[]{:S(2)}) collective-permute-start(bf16[3,200,128]{2,1,0:T(8,128)(2,1)S(1)} %get-tuple-element.37), channel_id=1, source_target_pairs={{0,8},{8,0},{16,24},{24,16},{1,9},{9,1},{17,25},{25,17},{2,10},{10... | collective-permute-start | bytes 460808 | tf_op jit(solution)/shard_map/gather/ppermute | solution.py:388
  17.1 6.4 %collective-permute-start.10 = (bf16[200,128]{1,0:T(8,128)(2,1)S(1)}, bf16[200,128]{1,0:T(8,128)(2,1)S(1)}, u32[]{:S(2)}, u32[]{:S(2)}) collective-permute-start(bf16[200,128]{1,0:T(8,128)(2,1)S(1)} %get-tuple-element.44.own_ref.refs_6_), channel_id=1, source_target_pairs={{0,16},{1,17},{2,18},{3,19},{4,20},{5,21},{6,22},{7,23},{8,24},{9,... | collective-permute-start | bytes 153608 | tf_op jit(solution)/shard_map/gather/ppermute | solution.py:498
  18.7 4.8 %collective-permute-start.9 = (bf16[200,128]{1,0:T(8,128)(2,1)S(1)}, bf16[200,128]{1,0:T(8,128)(2,1)S(1)}, u32[]{:S(2)}, u32[]{:S(2)}) collective-permute-start(bf16[200,128]{1,0:T(8,128)(2,1)S(1)} %get-tuple-element.44.own_ref.refs_6_), channel_id=1, source_target_pairs={{0,2},{1,3},{2,0},{3,1},{4,6},{5,7},{6,4},{7,5},{8,10},{9,11},{10,... | collective-permute-start | bytes 153608 | tf_op jit(solution)/shard_map/gather/ppermute | solution.py:498
  20.3 5.2 %collective-permute-start.8 = (bf16[200,128]{1,0:T(8,128)(2,1)S(1)}, bf16[200,128]{1,0:T(8,128)(2,1)S(1)}, u32[]{:S(2)}, u32[]{:S(2)}) collective-permute-start(bf16[200,128]{1,0:T(8,128)(2,1)S(1)} %get-tuple-element.44.own_ref.refs_6_), channel_id=1, source_target_pairs={{0,1},{1,0},{2,3},{3,2},{4,5},{5,4},{6,7},{7,6},{8,9},{9,8},{10,11... | collective-permute-start | bytes 153608 | tf_op jit(solution)/shard_map/gather/ppermute | solution.py:498
  20.9 7.2 %collective-permute-start.7 = (bf16[2,200,128]{2,1,0:T(8,128)(2,1)S(1)}, bf16[2,200,128]{2,1,0:T(8,128)(2,1)S(1)}, u32[]{:S(2)}, u32[]{:S(2)}) collective-permute-start(bf16[2,200,128]{2,1,0:T(8,128)(2,1)S(1)} %gather.1), channel_id=1, source_target_pairs={{0,17},{1,16},{2,19},{3,18},{4,21},{5,20},{6,23},{7,22},{8,27},{9,... | collective-permute-start | bytes 307208 | tf_op jit(solution)/shard_map/gather/ppermute | solution.py:498
  22.4 5.8 %collective-permute-start.6 = (bf16[2,200,128]{2,1,0:T(8,128)(2,1)S(1)}, bf16[2,200,128]{2,1,0:T(8,128)(2,1)S(1)}, u32[]{:S(2)}, u32[]{:S(2)}) collective-permute-start(bf16[2,200,128]{2,1,0:T(8,128)(2,1)S(1)} %gather.1), channel_id=1, source_target_pairs={{0,3},{1,2},{2,1},{3,0},{4,7},{5,6},{6,5},{7,4},{8,26},{9,27},{10,... | collective-permute-start | bytes 307208 | tf_op jit(solution)/shard_map/gather/ppermute | solution.py:498
  29.0 1.6 %collective-permute-start.11 = (bf16[128,1024]{1,0:T(8,128)(2,1)S(1)}, bf16[128,1024]{1,0:T(8,128)(2,1)S(1)}, u32[]{:S(2)}, u32[]{:S(2)}) collective-permute-start(bf16[128,1024]{1,0:T(8,128)(2,1)S(1)} %attend.8), channel_id=1, source_target_pairs={{0,8},{8,0},{16,24},{24,16},{1,9},{9,1},{17,25},{25,17},{2,10},{10... | collective-permute-start | bytes 786440 | tf_op jit(solution)/shard_map/attend/ppermute | solution.py:388
where the time goes:
time: 31.7 us; the launch traced here: 31.5 us
  starting transfers between devices  14.6 us (46%)
  Pallas kernels  9.16 us (29%)
  waiting for transfers between devices  7.64 us (24%)
    ppermute x7, starting transfers between devices, exchange(): return lax.ppermute(x, axis, [(i, i ^ k) for i in range(n)])  8.97 us
    ppermute x5, starting transfers between devices, spread(): return lax.ppermute(x, ('enc', 'seq'), pairs)  5.62 us
    ppermute x7, waiting for transfers between devices, exchange(): return lax.ppermute(x, axis, [(i, i ^ k) for i in range(n)])  4.82 us
    pallas_call x4, Pallas kernels, attend(): call(functools.partial(attend_kernel, len(groups)), vmem(6 + len(groups)...  3.47 us
    ppermute x5, waiting for transfers between devices, spread(): return lax.ppermute(x, ('enc', 'seq'), pairs)  2.82 us
    pallas_call x1, Pallas kernels, on_device(): call(functools.partial(fold_kernel, len(later)), hbm(4 + len(later)), [ja...  1.75 us
    pallas_call x1, Pallas kernels, on_device(): call(functools.partial(encode_kernel, caps), hbm(2) + vmem(2), [jax.Shape...  1.72 us
    pallas_call x1, Pallas kernels, on_device(): pl.pallas_call(functools.partial(output_kernel, heads, neighbours, lists)...  0.91 us
  transfers between devices with their start and end apart: 12, of which 6 were waited for; matrix products, arithmetic and copies ran while one was open for 0% of the time, Pallas kernels for 18%

commit v1 on v0

--- a/solution.py
+++ b/solution.py
@@ -310,19 +310,14 @@
 
 def attend_kernel(count, *refs):
     folds, out_ref = refs[6 : 6 + count], refs[-1]
-    first = 0
-    if len(refs) > 7 + count:
-        done_ref = refs[6 + count]
-        first = done_ref.shape[1] // LANES
-        out_ref[:, : first * LANES] = done_ref[...]
 
     def place(i, result):
-        out_ref[:, (first + i) * LANES : (first + i + 1) * LANES] = result
+        out_ref[:, i * LANES : (i + 1) * LANES] = result
 
     attend_heads(each_head(folds), place, *refs[:6])
 
 
-def output_kernel(heads, neighbours, lists, own_ref, near_ref, out_ref, sems):
+def output_kernel(heads, neighbours, lists, near_early_ref, near_rest_ref, own_early_ref, own_rest_ref, out_ref, sems):
     mine, slot = lax.axis_index("enc"), lax.axis_index("seq") & (heads - 1)
     copies = []
 
@@ -333,14 +328,16 @@
         copies.append(pltpu.make_async_copy(result, out_ref.at[0, :, column], sems.at[len(copies)]))
         copies[-1].start()
 
-    for ref, base in ((near_ref, mine ^ 1), (own_ref, mine)):
-        first = 1 + len(neighbours)
+    for early, rest, base in (
+        (near_early_ref, near_rest_ref, mine ^ 1),
+        (own_early_ref, own_rest_ref, mine),
+    ):
         for at, partner in enumerate(((0, 0), *neighbours)):
-            put(ref, at, base, *partner)
+            put(early, at, base, *partner)
         for i, pair in enumerate(zip(*lists)):
             far, k = (jnp.where(base & 1 == 0, zero, one) for zero, one in zip(*pair))
-            put(ref, first + 2 * i, base, far, k)
-            put(ref, first + 2 * i + 1, base, far ^ 1, k)
+            put(rest, 2 * i, base, far, k)
+            put(rest, 2 * i + 1, base, far ^ 1, k)
     for copy in copies:
         copy.wait()
 
@@ -517,30 +514,31 @@
             [pltpu.VMEM((LANES, rows), f32)],
         )(q_gain, k_gain, gram, *blocks, swapped)
 
-    def attend(rows_here, groups, done=(), first=()):
+    def attend(rows_here, groups, first=()):
         count = sum(group.size for group in groups) // ((3 * feats + TAIL) * LANES)
-        total = count + sum(x.shape[1] for x in done) // LANES
         return call(
             functools.partial(attend_kernel, len(groups)),
-            vmem(6 + len(groups) + len(done)) + after(len(first)),
-            [jax.ShapeDtypeStruct((BLOCK, total * LANES), bf16)],
+            vmem(6 + len(groups)) + after(len(first)),
+            [jax.ShapeDtypeStruct((BLOCK, count * LANES), bf16)],
             cost=(count * 200_000_000, 1_000_000),
-        )(*shared, *rows_here, *groups, *done, *first)[0]
+        )(*shared, *rows_here, *groups, *first)[0]
 
     with jax.named_scope("attend"):
         own, other = (own_rows, own_mask), (far_rows, far_mask)
         early, rest = [fresh, *singles], got
-        early_other, early_own = attend(other, early), attend(own, early)
-        near = exchange(attend(other, rest, [early_other], [early_own]), "enc", n_enc, 1)
-        own_done = attend(own, rest, [early_own])
+        early_other = attend(other, early)
+        early_own = attend(own, early, [early_other])
+        near_early = exchange(gate(early_other, early_own), "enc", n_enc, 1)
+        near_rest = exchange(attend(other, rest, [early_own]), "enc", n_enc, 1)
+        rest_own = attend(own, rest)
         return pl.pallas_call(
             functools.partial(output_kernel, heads, neighbours, lists),
-            in_specs=vmem(2),
+            in_specs=vmem(4),
             out_specs=hbm(1)[0],
             out_shape=jax.ShapeDtypeStruct((1, BLOCK, n_enc * cols), bf16),
             scratch_shapes=[pltpu.SemaphoreType.DMA((n_enc * heads,))],
             compiler_params=pltpu.CompilerParams(vmem_limit_bytes=VMEM_LIMIT),
-        )(own_done, near)
+        )(near_early, near_rest, early_own, rest_own)
 
 
 def solution(mesh):

time: 31.7 us -> 31.5 us (level)
    ppermute x7 -> x8, waiting for transfers between devices: 4.82 us -> 4.62 us  [exchange(): return lax.ppermute(x, axis, [(i, i ^ k) for i in range(n)])]
    ppermute x7 -> x8, starting transfers between devices: 8.97 us -> 9.05 us  [exchange(): return lax.ppermute(x, axis, [(i, i ^ k) for i in range(n)])]
  transfers between devices with their start and end apart: 12 -> 13, of which waited for: 6 -> 6; matrix products, arithmetic and copies ran while one was open for 0% -> 0% of each run, Pallas kernels for 18% -> 21%
where the time goes in v1:
time: 31.5 us; the launch traced here: 31.3 us
  starting transfers between devices  14.7 us (47%)
  Pallas kernels  9.16 us (29%)
  waiting for transfers between devices  7.35 us (23%)
    ppermute x8, starting transfers between devices, exchange(): return lax.ppermute(x, axis, [(i, i ^ k) for i in range(n)])  9.05 us
    ppermute x5, starting transfers between devices, spread(): return lax.ppermute(x, ('enc', 'seq'), pairs)  5.62 us
    ppermute x8, waiting for transfers between devices, exchange(): return lax.ppermute(x, axis, [(i, i ^ k) for i in range(n)])  4.62 us
    pallas_call x4, Pallas kernels, attend(): call(functools.partial(attend_kernel, len(groups)), vmem(6 + len(groups))...  3.47 us
    ppermute x5, waiting for transfers between devices, spread(): return lax.ppermute(x, ('enc', 'seq'), pairs)  2.72 us
    pallas_call x1, Pallas kernels, on_device(): call(functools.partial(fold_kernel, len(later)), hbm(4 + len(later)), [ja...  1.75 us
    pallas_call x1, Pallas kernels, on_device(): call(functools.partial(encode_kernel, caps), hbm(2) + vmem(2), [jax.Shape...  1.72 us
    pallas_call x1, Pallas kernels, on_device(): pl.pallas_call(functools.partial(output_kernel, heads, neighbours, lists)...  0.91 us
  transfers between devices with their start and end apart: 13, of which 6 were waited for; matrix products, arithmetic and copies ran while one was open for 0% of the time, Pallas kernels for 21%

profile of v1, /device:TPU:0, one launch (start us, length us, event | category | flops | bytes accessed | tf_op | source)
XLA Modules:
  0.0 31.3 jit_solution(18433063721905024575)
XLA Ops:
  0.0 1.8 %fold.1 = (bf16[64,2048]{1,0:T(8,128)(2,1)S(1)}, bf16[1024,512]{1,0:T(8,128)(2,1)S(1)}, bf16[432,512]{1,0:T(8,128)(2,1)S(1)}, f32[1,128]{1,0:T(1,128)S(1)}, f32[...) custom-call(bf16[64,2048]{1,0:T(8,128)(2,1)} %embed_hbm.1, ...), custom_call_target="tpu_custom_call" | custom-call | flops 200000000 | bytes 1000000 | tf_op jit(solution)/shard_map/fold/pallas_call | solution.py:424
  1.8 4.0 %collective-permute-start = (bf16[200,128]{1,0:T(8,128)(2,1)S(1)}, bf16[200,128]{1,0:T(8,128)(2,1)S(1)}, u32[]{:S(2)}, u32[]{:S(2)}) collective-permute-start(bf16[200,128]{1,0:T(8,128)(2,1)S(1)} %get-tuple-element.30), channel_id=1, source_target_pairs={{0,3},{1,2},{2,1},{3,0},{4,7},{5,6},{6,5},{7,4},{8,11},{9,10},{10,... | collective-permute-start | bytes 153608 | tf_op jit(solution)/shard_map/fold_sum/ppermute | solution.py:385
  5.8 0.4 %collective-permute-start.1 = (bf16[200,128]{1,0:T(8,128)(2,1)S(1)}, bf16[200,128]{1,0:T(8,128)(2,1)S(1)}, u32[]{:S(2)}, u32[]{:S(2)}) collective-permute-start(bf16[200,128]{1,0:T(8,128)(2,1)S(1)} %get-tuple-element.31), channel_id=1, source_target_pairs={{0,2},{1,3},{2,0},{3,1},{4,6},{5,7},{6,4},{7,5},{8,10},{9,11},{10,... | collective-permute-start | bytes 153608 | tf_op jit(solution)/shard_map/fold_sum/ppermute | solution.py:385
  6.4 1.7 %encode.1.refs_3_.refs_0_ = bf16[160,128]{1,0:T(8,128)(2,1)S(1)} custom-call(s32[1,1,3]{2,1,0:T(1,128)} %shape_hbm.1, s32[1,1,2,2]{3,2,1,0:T(2,128)} %plan_hbm.1, bf16[1024,512]{1,0:T(8,128)(2,1)S(1)} %get-tuple-element.33.feat_ref, bf16[432,512]{1,0:T(8,128)(2,1)S(1)} %get-tuple-element.34.conv_ref), custom_call_target="tpu_custom_call" | custom-call | flops 500000000 | bytes 2000000 | tf_op jit(solution)/shard_map/encode/pallas_call | solution.py:440
  8.2 1.7 %collective-permute-done.1.refs_1_ = bf16[200,128]{1,0:T(8,128)(2,1)S(1)} collective-permute-done((bf16[200,128]{1,0:T(8,128)(2,1)S(1)}, bf16[200,128]{1,0:T(8,128)(2,1)S(1)}, u32[]{:S(2)}, u32[]{:S(2)}) %collective-permute-start.1) | collective-permute-done | bytes 51232 | tf_op jit(solution)/shard_map/fold_sum/ppermute | solution.py:385
  9.9 0.4 %collective-permute-done.2.refs_2_ = bf16[200,128]{1,0:T(8,128)(2,1)S(1)} collective-permute-done((bf16[200,128]{1,0:T(8,128)(2,1)S(1)}, bf16[200,128]{1,0:T(8,128)(2,1)S(1)}, u32[]{:S(2)}, u32[]{:S(2)}) %collective-permute-start.2) | collective-permute-done | bytes 51232 | tf_op jit(solution)/shard_map/fold_sum/ppermute | solution.py:385
  10.4 2.7 %collective-permute-start.4 = (bf16[200,128]{1,0:T(8,128)(2,1)S(1)}, bf16[200,128]{1,0:T(8,128)(2,1)S(1)}, u32[]{:S(2)}, u32[]{:S(2)}) collective-permute-start(bf16[200,128]{1,0:T(8,128)(2,1)S(1)} %get-tuple-element.36), channel_id=1, source_target_pairs={{0,4},{1,5},{2,6},{3,7},{4,0},{5,1},{6,2},{7,3},{8,12},{9,13},{10,... | collective-permute-start | bytes 153608 | tf_op jit(solution)/shard_map/fold_sum/ppermute | solution.py:385
  13.0 1.5 %collective-permute-start.3 = (bf16[160,128]{1,0:T(8,128)(2,1)S(1)}, bf16[160,128]{1,0:T(8,128)(2,1)S(1)}, u32[]{:S(2)}, u32[]{:S(2)}) collective-permute-start(bf16[160,128]{1,0:T(8,128)(2,1)S(1)} %tokens.1.refs_0_), channel_id=1, source_target_pairs={{0,16},{8,24},{16,0},{24,8},{1,17},{9,25},{17,1},{25,9},{2,18},{10... | collective-permute-start | bytes 122888 | tf_op jit(solution)/shard_map/tokens/ppermute | solution.py:385
  14.6 0.5 %gram.1.refs_2_.gram_ref = bf16[128,64]{1,0:T(8,128)(2,1)S(1)} custom-call(bf16[64,2048]{1,0:T(8,128)(2,1)S(1)} %get-tuple-element.28.embed_ref, f32[200,128]{1,0:T(8,128)S(1)} %get-tuple-element.35.first_ref.refs_1_.keep_in), custom_call_target="tpu_custom_call" | custom-call | flops 1000000 | bytes 1000000 | tf_op jit(solution)/shard_map/gram/pallas_call | solution.py:464
  15.0 2.0 %collective-permute-done.3.refs_1_ = bf16[160,128]{1,0:T(8,128)(2,1)S(1)} collective-permute-done((bf16[160,128]{1,0:T(8,128)(2,1)S(1)}, bf16[160,128]{1,0:T(8,128)(2,1)S(1)}, u32[]{:S(2)}, u32[]{:S(2)}) %collective-permute-start.3) | collective-permute-done | bytes 40992 | tf_op jit(solution)/shard_map/tokens/ppermute | solution.py:385
  17.1 1.6 %collective-permute-start.8 = (bf16[200,128]{1,0:T(8,128)(2,1)S(1)}, bf16[200,128]{1,0:T(8,128)(2,1)S(1)}, u32[]{:S(2)}, u32[]{:S(2)}) collective-permute-start(bf16[200,128]{1,0:T(8,128)(2,1)S(1)} %get-tuple-element.44.refs_6_.own_ref), channel_id=1, source_target_pairs={{0,16},{1,17},{2,18},{3,19},{4,20},{5,21},{6,22},{7,23},{8,24},{9,... | collective-permute-start | bytes 153608 | tf_op jit(solution)/shard_map/gather/ppermute | solution.py:495
  18.7 1.6 %collective-permute-start.7 = (bf16[200,128]{1,0:T(8,128)(2,1)S(1)}, bf16[200,128]{1,0:T(8,128)(2,1)S(1)}, u32[]{:S(2)}, u32[]{:S(2)}) collective-permute-start(bf16[200,128]{1,0:T(8,128)(2,1)S(1)} %get-tuple-element.44.refs_6_.own_ref), channel_id=1, source_target_pairs={{0,2},{1,3},{2,0},{3,1},{4,6},{5,7},{6,4},{7,5},{8,10},{9,11},{10,... | collective-permute-start | bytes 153608 | tf_op jit(solution)/shard_map/gather/ppermute | solution.py:495
  20.3 0.5 %collective-permute-start.6 = (bf16[200,128]{1,0:T(8,128)(2,1)S(1)}, bf16[200,128]{1,0:T(8,128)(2,1)S(1)}, u32[]{:S(2)}, u32[]{:S(2)}) collective-permute-start(bf16[200,128]{1,0:T(8,128)(2,1)S(1)} %get-tuple-element.44.refs_6_.own_ref), channel_id=1, source_target_pairs={{0,1},{1,0},{2,3},{3,2},{4,5},{5,4},{6,7},{7,6},{8,9},{9,8},{10,11... | collective-permute-start | bytes 153608 | tf_op jit(solution)/shard_map/gather/ppermute | solution.py:495
  20.9 1.5 %collective-permute-start.11 = (bf16[2,200,128]{2,1,0:T(8,128)(2,1)S(1)}, bf16[2,200,128]{2,1,0:T(8,128)(2,1)S(1)}, u32[]{:S(2)}, u32[]{:S(2)}) collective-permute-start(bf16[2,200,128]{2,1,0:T(8,128)(2,1)S(1)} %gather.1), channel_id=1, source_target_pairs={{0,17},{1,16},{2,19},{3,18},{4,21},{5,20},{6,23},{7,22},{8,27},{9,... | collective-permute-start | bytes 307208 | tf_op jit(solution)/shard_map/gather/ppermute | solution.py:495
  22.4 0.4 %collective-permute-start.10 = (bf16[2,200,128]{2,1,0:T(8,128)(2,1)S(1)}, bf16[2,200,128]{2,1,0:T(8,128)(2,1)S(1)}, u32[]{:S(2)}, u32[]{:S(2)}) collective-permute-start(bf16[2,200,128]{2,1,0:T(8,128)(2,1)S(1)} %gather.1), channel_id=1, source_target_pairs={{0,3},{1,2},{2,1},{3,0},{4,7},{5,6},{6,5},{7,4},{8,26},{9,27},{10,... | collective-permute-start | bytes 307208 | tf_op jit(solution)/shard_map/gather/ppermute | solution.py:495
  22.8 0.7 %pack.1 = (bf16[72,512]{1,0:T(8,128)(2,1)S(1)}, bf16[512,128]{1,0:T(8,128)(2,1)S(1)}, bf16[128,512]{1,0:T(8,128)(2,1)S(1)}, f32[1,128]{1,0:T(1,128)S(1)}, bf16[1...) custom-call(f32[1,128]{1,0:T(1,128)S(1)} %get-tuple-element.26.q_gai, ...), custom_call_target="tpu_custom_call" | custom-call | flops 1000000 | bytes 1000000 | tf_op jit(solution)/shard_map/pack/pallas_call | solution.py:504
  23.6 2.0 %collective-permute-done.6.refs_7_ = bf16[200,128]{1,0:T(8,128)(2,1)S(1)} collective-permute-done((bf16[200,128]{1,0:T(8,128)(2,1)S(1)}, bf16[200,128]{1,0:T(8,128)(2,1)S(1)}, u32[]{:S(2)}, u32[]{:S(2)}) %collective-permute-start.6) | collective-permute-done | bytes 51232 | tf_op jit(solution)/shard_map/gather/ppermute | solution.py:495
  25.5 0.9 %attend.6.refs_10_.refs_0_ = bf16[128,512]{1,0:T(8,128)(2,1)S(1)} custom-call(bf16[72,512]{1,0:T(8,128)(2,1)S(1)} %get-tuple-element.38.refs_0_, bf16[512,128]{1,0:T(8,128)(2,1)S(1)} %get-tuple-element.39.refs_1_, bf16[128,512]{1,0:T(8,128)(2,1)S(1)} %get-tuple-element.40.refs_2_, f32[1,128]{1,0:T(1,128)S(1)} %get-tuple-element.41.refs_3_, ...), custom_call_target="tpu_custom_call" | custom-call | flops 800000000 | bytes 1000000 | tf_op jit(solution)/shard_map/attend/pallas_call | solution.py:519
  26.4 0.9 %attend.7.refs_1_.refs_8_.own_early_ref = bf16[128,512]{1,0:T(8,128)(2,1)S(1)} custom-call(bf16[72,512]{1,0:T(8,128)(2,1)S(1)} %get-tuple-element.38.refs_0_, bf16[512,128]{1,0:T(8,128)(2,1)S(1)} %get-tuple-element.39.refs_1_, bf16[128,512]{1,0:T(8,128)(2,1)S(1)} %get-tuple-element.40.refs_2_, f32[1,128]{1,0:T(1,128)S(1)} %get-tuple-element.41.refs_3_, ...), custom_call_target="tpu_custom_call" | custom-call | flops 800000000 | bytes 1000000 | tf_op jit(solution)/shard_map/attend/pallas_call | solution.py:519
  27.4 0.8 %collective-permute-done.11.refs_7_ = bf16[2,200,128]{2,1,0:T(8,128)(2,1)S(1)} collective-permute-done((bf16[2,200,128]{2,1,0:T(8,128)(2,1)S(1)}, bf16[2,200,128]{2,1,0:T(8,128)(2,1)S(1)}, u32[]{:S(2)}, u32[]{:S(2)}) %collective-permute-start.11) | collective-permute-done | bytes 102432 | tf_op jit(solution)/shard_map/gather/ppermute | solution.py:495
  28.1 0.9 %attend.9 = bf16[128,512]{1,0:T(8,128)(2,1)S(1)} custom-call(bf16[72,512]{1,0:T(8,128)(2,1)S(1)} %get-tuple-element.38.refs_0_, bf16[512,128]{1,0:T(8,128)(2,1)S(1)} %get-tuple-element.39.refs_1_, bf16[128,512]{1,0:T(8,128)(2,1)S(1)} %get-tuple-element.40.refs_2_, f32[1,128]{1,0:T(1,128)S(1)} %get-tuple-element.41.refs_3_, ...), custom_call_target="tpu_custom_call" | custom-call | flops 800000000 | bytes 1000000 | tf_op jit(solution)/shard_map/attend/pallas_call | solution.py:519
  29.1 0.9 %attend.10.own_rest_ref = bf16[128,512]{1,0:T(8,128)(2,1)S(1)} custom-call(bf16[72,512]{1,0:T(8,128)(2,1)S(1)} %get-tuple-element.38.refs_0_, bf16[512,128]{1,0:T(8,128)(2,1)S(1)} %get-tuple-element.39.refs_1_, bf16[128,512]{1,0:T(8,128)(2,1)S(1)} %get-tuple-element.40.refs_2_, f32[1,128]{1,0:T(1,128)S(1)} %get-tuple-element.41.refs_3_, ...), custom_call_target="tpu_custom_call" | custom-call | flops 800000000 | bytes 1000000 | tf_op jit(solution)/shard_map/attend/pallas_call | solution.py:519
  29.9 0.4 %collective-permute-done.12.near_rest_ref = bf16[128,512]{1,0:T(8,128)(2,1)S(1)} collective-permute-done((bf16[128,512]{1,0:T(8,128)(2,1)S(1)}, bf16[128,512]{1,0:T(8,128)(2,1)S(1)}, u32[]{:S(2)}, u32[]{:S(2)}) %collective-permute-start.12) | collective-permute-done | bytes 131104 | tf_op jit(solution)/shard_map/attend/ppermute | solution.py:385
  30.4 0.9 %attend.11 = bf16[1,128,2048]{2,1,0:T(8,128)(2,1)} custom-call(bf16[128,512]{1,0:T(8,128)(2,1)S(1)} %collective-permute-done.9.near_early_ref, bf16[128,512]{1,0:T(8,128)(2,1)S(1)} %collective-permute-done.12.near_rest_ref, bf16[128,512]{1,0:T(8,128)(2,1)S(1)} %attend.7.refs_1_.refs_8_.own_early_ref, bf16[128,512]{1,0:T(8,128)(2,1)S(1)} %attend.10.own_rest_ref), custom_call_target="tpu_custom_call" | custom-call | tf_op jit(solution)/shard_map/attend/pallas_call | solution.py:534
  (16 shorter events, 0.5 us)
Async XLA Ops:
  1.8 6.4 %collective-permute-start = (bf16[200,128]{1,0:T(8,128)(2,1)S(1)}, bf16[200,128]{1,0:T(8,128)(2,1)S(1)}, u32[]{:S(2)}, u32[]{:S(2)}) collective-permute-start(bf16[200,128]{1,0:T(8,128)(2,1)S(1)} %get-tuple-element.30), channel_id=1, source_target_pairs={{0,3},{1,2},{2,1},{3,0},{4,7},{5,6},{6,5},{7,4},{8,11},{9,10},{10,... | collective-permute-start | bytes 153608 | tf_op jit(solution)/shard_map/fold_sum/ppermute | solution.py:385
  5.8 4.1 %collective-permute-start.1 = (bf16[200,128]{1,0:T(8,128)(2,1)S(1)}, bf16[200,128]{1,0:T(8,128)(2,1)S(1)}, u32[]{:S(2)}, u32[]{:S(2)}) collective-permute-start(bf16[200,128]{1,0:T(8,128)(2,1)S(1)} %get-tuple-element.31), channel_id=1, source_target_pairs={{0,2},{1,3},{2,0},{3,1},{4,6},{5,7},{6,4},{7,5},{8,10},{9,11},{10,... | collective-permute-start | bytes 153608 | tf_op jit(solution)/shard_map/fold_sum/ppermute | solution.py:385
  6.2 4.1 %collective-permute-start.2 = (bf16[200,128]{1,0:T(8,128)(2,1)S(1)}, bf16[200,128]{1,0:T(8,128)(2,1)S(1)}, u32[]{:S(2)}, u32[]{:S(2)}) collective-permute-start(bf16[200,128]{1,0:T(8,128)(2,1)S(1)} %get-tuple-element.32), channel_id=1, source_target_pairs={{0,1},{1,0},{2,3},{3,2},{4,5},{5,4},{6,7},{7,6},{8,9},{9,8},{10,11... | collective-permute-start | bytes 153608 | tf_op jit(solution)/shard_map/fold_sum/ppermute | solution.py:385
  10.4 6.7 %collective-permute-start.4 = (bf16[200,128]{1,0:T(8,128)(2,1)S(1)}, bf16[200,128]{1,0:T(8,128)(2,1)S(1)}, u32[]{:S(2)}, u32[]{:S(2)}) collective-permute-start(bf16[200,128]{1,0:T(8,128)(2,1)S(1)} %get-tuple-element.36), channel_id=1, source_target_pairs={{0,4},{1,5},{2,6},{3,7},{4,0},{5,1},{6,2},{7,3},{8,12},{9,13},{10,... | collective-permute-start | bytes 153608 | tf_op jit(solution)/shard_map/fold_sum/ppermute | solution.py:385
  13.0 4.0 %collective-permute-start.3 = (bf16[160,128]{1,0:T(8,128)(2,1)S(1)}, bf16[160,128]{1,0:T(8,128)(2,1)S(1)}, u32[]{:S(2)}, u32[]{:S(2)}) collective-permute-start(bf16[160,128]{1,0:T(8,128)(2,1)S(1)} %tokens.1.refs_0_), channel_id=1, source_target_pairs={{0,16},{8,24},{16,0},{24,8},{1,17},{9,25},{17,1},{25,9},{2,18},{10... | collective-permute-start | bytes 122888 | tf_op jit(solution)/shard_map/tokens/ppermute | solution.py:385
  17.1 3.8 %collective-permute-start.5 = (bf16[3,200,128]{2,1,0:T(8,128)(2,1)S(1)}, bf16[3,200,128]{2,1,0:T(8,128)(2,1)S(1)}, u32[]{:S(2)}, u32[]{:S(2)}) collective-permute-start(bf16[3,200,128]{2,1,0:T(8,128)(2,1)S(1)} %get-tuple-element.37), channel_id=1, source_target_pairs={{0,8},{8,0},{16,24},{24,16},{1,9},{9,1},{17,25},{25,17},{2,10},{10... | collective-permute-start | bytes 460808 | tf_op jit(solution)/shard_map/gather/ppermute | solution.py:385
  17.1 6.4 %collective-permute-start.8 = (bf16[200,128]{1,0:T(8,128)(2,1)S(1)}, bf16[200,128]{1,0:T(8,128)(2,1)S(1)}, u32[]{:S(2)}, u32[]{:S(2)}) collective-permute-start(bf16[200,128]{1,0:T(8,128)(2,1)S(1)} %get-tuple-element.44.refs_6_.own_ref), channel_id=1, source_target_pairs={{0,16},{1,17},{2,18},{3,19},{4,20},{5,21},{6,22},{7,23},{8,24},{9,... | collective-permute-start | bytes 153608 | tf_op jit(solution)/shard_map/gather/ppermute | solution.py:495
  18.7 4.8 %collective-permute-start.7 = (bf16[200,128]{1,0:T(8,128)(2,1)S(1)}, bf16[200,128]{1,0:T(8,128)(2,1)S(1)}, u32[]{:S(2)}, u32[]{:S(2)}) collective-permute-start(bf16[200,128]{1,0:T(8,128)(2,1)S(1)} %get-tuple-element.44.refs_6_.own_ref), channel_id=1, source_target_pairs={{0,2},{1,3},{2,0},{3,1},{4,6},{5,7},{6,4},{7,5},{8,10},{9,11},{10,... | collective-permute-start | bytes 153608 | tf_op jit(solution)/shard_map/gather/ppermute | solution.py:495
  20.3 5.2 %collective-permute-start.6 = (bf16[200,128]{1,0:T(8,128)(2,1)S(1)}, bf16[200,128]{1,0:T(8,128)(2,1)S(1)}, u32[]{:S(2)}, u32[]{:S(2)}) collective-permute-start(bf16[200,128]{1,0:T(8,128)(2,1)S(1)} %get-tuple-element.44.refs_6_.own_ref), channel_id=1, source_target_pairs={{0,1},{1,0},{2,3},{3,2},{4,5},{5,4},{6,7},{7,6},{8,9},{9,8},{10,11... | collective-permute-start | bytes 153608 | tf_op jit(solution)/shard_map/gather/ppermute | solution.py:495
  20.9 7.2 %collective-permute-start.11 = (bf16[2,200,128]{2,1,0:T(8,128)(2,1)S(1)}, bf16[2,200,128]{2,1,0:T(8,128)(2,1)S(1)}, u32[]{:S(2)}, u32[]{:S(2)}) collective-permute-start(bf16[2,200,128]{2,1,0:T(8,128)(2,1)S(1)} %gather.1), channel_id=1, source_target_pairs={{0,17},{1,16},{2,19},{3,18},{4,21},{5,20},{6,23},{7,22},{8,27},{9,... | collective-permute-start | bytes 307208 | tf_op jit(solution)/shard_map/gather/ppermute | solution.py:495
  22.4 5.8 %collective-permute-start.10 = (bf16[2,200,128]{2,1,0:T(8,128)(2,1)S(1)}, bf16[2,200,128]{2,1,0:T(8,128)(2,1)S(1)}, u32[]{:S(2)}, u32[]{:S(2)}) collective-permute-start(bf16[2,200,128]{2,1,0:T(8,128)(2,1)S(1)} %gather.1), channel_id=1, source_target_pairs={{0,3},{1,2},{2,1},{3,0},{4,7},{5,6},{6,5},{7,4},{8,26},{9,27},{10,... | collective-permute-start | bytes 307208 | tf_op jit(solution)/shard_map/gather/ppermute | solution.py:495
  27.3 2.7 %collective-permute-start.9 = (bf16[128,512]{1,0:T(8,128)(2,1)S(1)}, bf16[128,512]{1,0:T(8,128)(2,1)S(1)}, u32[]{:S(2)}, u32[]{:S(2)}) collective-permute-start(bf16[128,512]{1,0:T(8,128)(2,1)S(1)} %attend.8), channel_id=1, source_target_pairs={{0,8},{8,0},{16,24},{24,16},{1,9},{9,1},{17,25},{25,17},{2,10},{10... | collective-permute-start | bytes 393224 | tf_op jit(solution)/shard_map/attend/ppermute | solution.py:385
  29.0 1.4 %collective-permute-start.12 = (bf16[128,512]{1,0:T(8,128)(2,1)S(1)}, bf16[128,512]{1,0:T(8,128)(2,1)S(1)}, u32[]{:S(2)}, u32[]{:S(2)}) collective-permute-start(bf16[128,512]{1,0:T(8,128)(2,1)S(1)} %attend.9), channel_id=1, source_target_pairs={{0,8},{8,0},{16,24},{24,16},{1,9},{9,1},{17,25},{25,17},{2,10},{10... | collective-permute-start | bytes 393224 | tf_op jit(solution)/shard_map/attend/ppermute | solution.py:385

commit v2 on v1

--- a/solution.py
+++ b/solution.py
@@ -485,7 +485,7 @@
     half = (len(partners) - near_count) // 2
     assert len(partners) == near_count + 2 * half
     neighbours = tuple(partners[:near_count])
-    lists = (tuple(partners[near_count : near_count + half]), tuple(partners[near_count + half :]))
+    lists = (tuple(reversed(partners[near_count : near_count + half])), tuple(partners[near_count + half :]))
 
     def spread(x, partner_of):
         pairs = []

time: 31.5 us -> 32.3 us (1.025)
  waiting for transfers between devices: 7.35 us -> 8.21 us
    ppermute x5, waiting for transfers between devices: 2.72 us -> 3.58 us  [spread(): return lax.ppermute(x, ('enc', 'seq'), pairs)]
  transfers between devices with their start and end apart: 13 -> 13, of which waited for: 6 -> 6; matrix products, arithmetic and copies ran while one was open for 0% -> 0% of each run, Pallas kernels for 21% -> 20%
where the time goes in v2:
time: 32.3 us; the launch traced here: 32.2 us
  starting transfers between devices  14.7 us (46%)
  Pallas kernels  9.16 us (28%)
  waiting for transfers between devices  8.21 us (25%)
    ppermute x8, starting transfers between devices, exchange(): return lax.ppermute(x, axis, [(i, i ^ k) for i in range(n)])  9.05 us
    ppermute x5, starting transfers between devices, spread(): return lax.ppermute(x, ('enc', 'seq'), pairs)  5.62 us
    ppermute x8, waiting for transfers between devices, exchange(): return lax.ppermute(x, axis, [(i, i ^ k) for i in range(n)])  4.63 us
    ppermute x5, waiting for transfers between devices, spread(): return lax.ppermute(x, ('enc', 'seq'), pairs)  3.58 us
    pallas_call x4, Pallas kernels, attend(): call(functools.partial(attend_kernel, len(groups)), vmem(6 + len(groups))...  3.46 us
    pallas_call x1, Pallas kernels, on_device(): call(functools.partial(fold_kernel, len(later)), hbm(4 + len(later)), [ja...  1.75 us
    pallas_call x1, Pallas kernels, on_device(): call(functools.partial(encode_kernel, caps), hbm(2) + vmem(2), [jax.Shape...  1.72 us
    pallas_call x1, Pallas kernels, on_device(): pl.pallas_call(functools.partial(output_kernel, heads, neighbours, lists)...  0.91 us
  transfers between devices with their start and end apart: 13, of which 6 were waited for; matrix products, arithmetic and copies ran while one was open for 0% of the time, Pallas kernels for 20%

profile of v2, /device:TPU:0, one launch (start us, length us, event | category | flops | bytes accessed | tf_op | source)
XLA Modules:
  0.0 32.2 jit_solution(9605347361976125855)
XLA Ops:
  0.0 1.8 %fold.1 = (bf16[64,2048]{1,0:T(8,128)(2,1)S(1)}, bf16[1024,512]{1,0:T(8,128)(2,1)S(1)}, bf16[432,512]{1,0:T(8,128)(2,1)S(1)}, f32[1,128]{1,0:T(1,128)S(1)}, f32[...) custom-call(bf16[64,2048]{1,0:T(8,128)(2,1)} %embed_hbm.1, ...), custom_call_target="tpu_custom_call" | custom-call | flops 200000000 | bytes 1000000 | tf_op jit(solution)/shard_map/fold/pallas_call | solution.py:424
  1.8 4.0 %collective-permute-start = (bf16[200,128]{1,0:T(8,128)(2,1)S(1)}, bf16[200,128]{1,0:T(8,128)(2,1)S(1)}, u32[]{:S(2)}, u32[]{:S(2)}) collective-permute-start(bf16[200,128]{1,0:T(8,128)(2,1)S(1)} %get-tuple-element.30), channel_id=1, source_target_pairs={{0,3},{1,2},{2,1},{3,0},{4,7},{5,6},{6,5},{7,4},{8,11},{9,10},{10,... | collective-permute-start | bytes 153608 | tf_op jit(solution)/shard_map/fold_sum/ppermute | solution.py:385
  5.8 0.4 %collective-permute-start.1 = (bf16[200,128]{1,0:T(8,128)(2,1)S(1)}, bf16[200,128]{1,0:T(8,128)(2,1)S(1)}, u32[]{:S(2)}, u32[]{:S(2)}) collective-permute-start(bf16[200,128]{1,0:T(8,128)(2,1)S(1)} %get-tuple-element.31), channel_id=1, source_target_pairs={{0,2},{1,3},{2,0},{3,1},{4,6},{5,7},{6,4},{7,5},{8,10},{9,11},{10,... | collective-permute-start | bytes 153608 | tf_op jit(solution)/shard_map/fold_sum/ppermute | solution.py:385
  6.4 1.7 %encode.1.refs_3_.refs_0_ = bf16[160,128]{1,0:T(8,128)(2,1)S(1)} custom-call(s32[1,1,3]{2,1,0:T(1,128)} %shape_hbm.1, s32[1,1,2,2]{3,2,1,0:T(2,128)} %plan_hbm.1, bf16[1024,512]{1,0:T(8,128)(2,1)S(1)} %get-tuple-element.33.feat_ref, bf16[432,512]{1,0:T(8,128)(2,1)S(1)} %get-tuple-element.34.conv_ref), custom_call_target="tpu_custom_call" | custom-call | flops 500000000 | bytes 2000000 | tf_op jit(solution)/shard_map/encode/pallas_call | solution.py:440
  8.2 1.7 %collective-permute-done.1.refs_1_ = bf16[200,128]{1,0:T(8,128)(2,1)S(1)} collective-permute-done((bf16[200,128]{1,0:T(8,128)(2,1)S(1)}, bf16[200,128]{1,0:T(8,128)(2,1)S(1)}, u32[]{:S(2)}, u32[]{:S(2)}) %collective-permute-start.1) | collective-permute-done | bytes 51232 | tf_op jit(solution)/shard_map/fold_sum/ppermute | solution.py:385
  9.9 0.4 %collective-permute-done.2.refs_2_ = bf16[200,128]{1,0:T(8,128)(2,1)S(1)} collective-permute-done((bf16[200,128]{1,0:T(8,128)(2,1)S(1)}, bf16[200,128]{1,0:T(8,128)(2,1)S(1)}, u32[]{:S(2)}, u32[]{:S(2)}) %collective-permute-start.2) | collective-permute-done | bytes 51232 | tf_op jit(solution)/shard_map/fold_sum/ppermute | solution.py:385
  10.4 2.7 %collective-permute-start.4 = (bf16[200,128]{1,0:T(8,128)(2,1)S(1)}, bf16[200,128]{1,0:T(8,128)(2,1)S(1)}, u32[]{:S(2)}, u32[]{:S(2)}) collective-permute-start(bf16[200,128]{1,0:T(8,128)(2,1)S(1)} %get-tuple-element.36), channel_id=1, source_target_pairs={{0,4},{1,5},{2,6},{3,7},{4,0},{5,1},{6,2},{7,3},{8,12},{9,13},{10,... | collective-permute-start | bytes 153608 | tf_op jit(solution)/shard_map/fold_sum/ppermute | solution.py:385
  13.0 1.5 %collective-permute-start.3 = (bf16[160,128]{1,0:T(8,128)(2,1)S(1)}, bf16[160,128]{1,0:T(8,128)(2,1)S(1)}, u32[]{:S(2)}, u32[]{:S(2)}) collective-permute-start(bf16[160,128]{1,0:T(8,128)(2,1)S(1)} %tokens.1.refs_0_), channel_id=1, source_target_pairs={{0,16},{8,24},{16,0},{24,8},{1,17},{9,25},{17,1},{25,9},{2,18},{10... | collective-permute-start | bytes 122888 | tf_op jit(solution)/shard_map/tokens/ppermute | solution.py:385
  14.6 0.5 %gram.1.refs_2_.gram_ref = bf16[128,64]{1,0:T(8,128)(2,1)S(1)} custom-call(bf16[64,2048]{1,0:T(8,128)(2,1)S(1)} %get-tuple-element.28.embed_ref, f32[200,128]{1,0:T(8,128)S(1)} %get-tuple-element.35.first_ref.refs_1_.keep_in), custom_call_target="tpu_custom_call" | custom-call | flops 1000000 | bytes 1000000 | tf_op jit(solution)/shard_map/gram/pallas_call | solution.py:464
  15.0 2.0 %collective-permute-done.3.refs_1_ = bf16[160,128]{1,0:T(8,128)(2,1)S(1)} collective-permute-done((bf16[160,128]{1,0:T(8,128)(2,1)S(1)}, bf16[160,128]{1,0:T(8,128)(2,1)S(1)}, u32[]{:S(2)}, u32[]{:S(2)}) %collective-permute-start.3) | collective-permute-done | bytes 40992 | tf_op jit(solution)/shard_map/tokens/ppermute | solution.py:385
  17.1 1.6 %collective-permute-start.8 = (bf16[200,128]{1,0:T(8,128)(2,1)S(1)}, bf16[200,128]{1,0:T(8,128)(2,1)S(1)}, u32[]{:S(2)}, u32[]{:S(2)}) collective-permute-start(bf16[200,128]{1,0:T(8,128)(2,1)S(1)} %get-tuple-element.44.refs_6_.own_ref), channel_id=1, source_target_pairs={{0,16},{1,17},{2,18},{3,19},{4,20},{5,21},{6,22},{7,23},{8,24},{9,... | collective-permute-start | bytes 153608 | tf_op jit(solution)/shard_map/gather/ppermute | solution.py:495
  18.7 1.6 %collective-permute-start.7 = (bf16[200,128]{1,0:T(8,128)(2,1)S(1)}, bf16[200,128]{1,0:T(8,128)(2,1)S(1)}, u32[]{:S(2)}, u32[]{:S(2)}) collective-permute-start(bf16[200,128]{1,0:T(8,128)(2,1)S(1)} %get-tuple-element.44.refs_6_.own_ref), channel_id=1, source_target_pairs={{0,2},{1,3},{2,0},{3,1},{4,6},{5,7},{6,4},{7,5},{8,10},{9,11},{10,... | collective-permute-start | bytes 153608 | tf_op jit(solution)/shard_map/gather/ppermute | solution.py:495
  20.3 0.5 %collective-permute-start.6 = (bf16[200,128]{1,0:T(8,128)(2,1)S(1)}, bf16[200,128]{1,0:T(8,128)(2,1)S(1)}, u32[]{:S(2)}, u32[]{:S(2)}) collective-permute-start(bf16[200,128]{1,0:T(8,128)(2,1)S(1)} %get-tuple-element.44.refs_6_.own_ref), channel_id=1, source_target_pairs={{0,1},{1,0},{2,3},{3,2},{4,5},{5,4},{6,7},{7,6},{8,9},{9,8},{10,11... | collective-permute-start | bytes 153608 | tf_op jit(solution)/shard_map/gather/ppermute | solution.py:495
  20.9 1.4 %collective-permute-start.11 = (bf16[2,200,128]{2,1,0:T(8,128)(2,1)S(1)}, bf16[2,200,128]{2,1,0:T(8,128)(2,1)S(1)}, u32[]{:S(2)}, u32[]{:S(2)}) collective-permute-start(bf16[2,200,128]{2,1,0:T(8,128)(2,1)S(1)} %gather.1), channel_id=1, source_target_pairs={{0,3},{1,2},{2,1},{3,0},{4,7},{5,6},{6,5},{7,4},{8,27},{9,26},{10,... | collective-permute-start | bytes 307208 | tf_op jit(solution)/shard_map/gather/ppermute | solution.py:495
  22.3 0.5 %collective-permute-start.10 = (bf16[2,200,128]{2,1,0:T(8,128)(2,1)S(1)}, bf16[2,200,128]{2,1,0:T(8,128)(2,1)S(1)}, u32[]{:S(2)}, u32[]{:S(2)}) collective-permute-start(bf16[2,200,128]{2,1,0:T(8,128)(2,1)S(1)} %gather.1), channel_id=1, source_target_pairs={{0,17},{1,16},{2,19},{3,18},{4,21},{5,20},{6,23},{7,22},{8,26},{9,... | collective-permute-start | bytes 307208 | tf_op jit(solution)/shard_map/gather/ppermute | solution.py:495
  22.8 0.7 %pack.1 = (bf16[72,512]{1,0:T(8,128)(2,1)S(1)}, bf16[512,128]{1,0:T(8,128)(2,1)S(1)}, bf16[128,512]{1,0:T(8,128)(2,1)S(1)}, f32[1,128]{1,0:T(1,128)S(1)}, bf16[1...) custom-call(f32[1,128]{1,0:T(1,128)S(1)} %get-tuple-element.26.q_gai, ...), custom_call_target="tpu_custom_call" | custom-call | flops 1000000 | bytes 1000000 | tf_op jit(solution)/shard_map/pack/pallas_call | solution.py:504
  23.6 2.0 %collective-permute-done.6.refs_7_ = bf16[200,128]{1,0:T(8,128)(2,1)S(1)} collective-permute-done((bf16[200,128]{1,0:T(8,128)(2,1)S(1)}, bf16[200,128]{1,0:T(8,128)(2,1)S(1)}, u32[]{:S(2)}, u32[]{:S(2)}) %collective-permute-start.6) | collective-permute-done | bytes 51232 | tf_op jit(solution)/shard_map/gather/ppermute | solution.py:495
  25.6 0.9 %attend.6.refs_10_.refs_0_ = bf16[128,512]{1,0:T(8,128)(2,1)S(1)} custom-call(bf16[72,512]{1,0:T(8,128)(2,1)S(1)} %get-tuple-element.38.refs_0_, bf16[512,128]{1,0:T(8,128)(2,1)S(1)} %get-tuple-element.39.refs_1_, bf16[128,512]{1,0:T(8,128)(2,1)S(1)} %get-tuple-element.40.refs_2_, f32[1,128]{1,0:T(1,128)S(1)} %get-tuple-element.41.refs_3_, ...), custom_call_target="tpu_custom_call" | custom-call | flops 800000000 | bytes 1000000 | tf_op jit(solution)/shard_map/attend/pallas_call | solution.py:519
  26.5 0.9 %attend.7.refs_1_.refs_8_.own_early_ref = bf16[128,512]{1,0:T(8,128)(2,1)S(1)} custom-call(bf16[72,512]{1,0:T(8,128)(2,1)S(1)} %get-tuple-element.38.refs_0_, bf16[512,128]{1,0:T(8,128)(2,1)S(1)} %get-tuple-element.39.refs_1_, bf16[128,512]{1,0:T(8,128)(2,1)S(1)} %get-tuple-element.40.refs_2_, f32[1,128]{1,0:T(1,128)S(1)} %get-tuple-element.41.refs_3_, ...), custom_call_target="tpu_custom_call" | custom-call | flops 800000000 | bytes 1000000 | tf_op jit(solution)/shard_map/attend/pallas_call | solution.py:519
  27.4 1.5 %collective-permute-done.10.refs_6_ = bf16[2,200,128]{2,1,0:T(8,128)(2,1)S(1)} collective-permute-done((bf16[2,200,128]{2,1,0:T(8,128)(2,1)S(1)}, bf16[2,200,128]{2,1,0:T(8,128)(2,1)S(1)}, u32[]{:S(2)}, u32[]{:S(2)}) %collective-permute-start.10) | collective-permute-done | bytes 102432 | tf_op jit(solution)/shard_map/gather/ppermute | solution.py:495
  29.0 0.9 %attend.9 = bf16[128,512]{1,0:T(8,128)(2,1)S(1)} custom-call(bf16[72,512]{1,0:T(8,128)(2,1)S(1)} %get-tuple-element.38.refs_0_, bf16[512,128]{1,0:T(8,128)(2,1)S(1)} %get-tuple-element.39.refs_1_, bf16[128,512]{1,0:T(8,128)(2,1)S(1)} %get-tuple-element.40.refs_2_, f32[1,128]{1,0:T(1,128)S(1)} %get-tuple-element.41.refs_3_, ...), custom_call_target="tpu_custom_call" | custom-call | flops 800000000 | bytes 1000000 | tf_op jit(solution)/shard_map/attend/pallas_call | solution.py:519
  29.9 0.9 %attend.10.own_rest_ref = bf16[128,512]{1,0:T(8,128)(2,1)S(1)} custom-call(bf16[72,512]{1,0:T(8,128)(2,1)S(1)} %get-tuple-element.38.refs_0_, bf16[512,128]{1,0:T(8,128)(2,1)S(1)} %get-tuple-element.39.refs_1_, bf16[128,512]{1,0:T(8,128)(2,1)S(1)} %get-tuple-element.40.refs_2_, f32[1,128]{1,0:T(1,128)S(1)} %get-tuple-element.41.refs_3_, ...), custom_call_target="tpu_custom_call" | custom-call | flops 800000000 | bytes 1000000 | tf_op jit(solution)/shard_map/attend/pallas_call | solution.py:519
  30.8 0.5 %collective-permute-done.12.near_rest_ref = bf16[128,512]{1,0:T(8,128)(2,1)S(1)} collective-permute-done((bf16[128,512]{1,0:T(8,128)(2,1)S(1)}, bf16[128,512]{1,0:T(8,128)(2,1)S(1)}, u32[]{:S(2)}, u32[]{:S(2)}) %collective-permute-start.12) | collective-permute-done | bytes 131104 | tf_op jit(solution)/shard_map/attend/ppermute | solution.py:385
  31.3 0.9 %attend.11 = bf16[1,128,2048]{2,1,0:T(8,128)(2,1)} custom-call(bf16[128,512]{1,0:T(8,128)(2,1)S(1)} %collective-permute-done.9.near_early_ref, bf16[128,512]{1,0:T(8,128)(2,1)S(1)} %collective-permute-done.12.near_rest_ref, bf16[128,512]{1,0:T(8,128)(2,1)S(1)} %attend.7.refs_1_.refs_8_.own_early_ref, bf16[128,512]{1,0:T(8,128)(2,1)S(1)} %attend.10.own_rest_ref), custom_call_target="tpu_custom_call" | custom-call | tf_op jit(solution)/shard_map/attend/pallas_call | solution.py:534
  (16 shorter events, 0.5 us)
Async XLA Ops:
  1.8 6.4 %collective-permute-start = (bf16[200,128]{1,0:T(8,128)(2,1)S(1)}, bf16[200,128]{1,0:T(8,128)(2,1)S(1)}, u32[]{:S(2)}, u32[]{:S(2)}) collective-permute-start(bf16[200,128]{1,0:T(8,128)(2,1)S(1)} %get-tuple-element.30), channel_id=1, source_target_pairs={{0,3},{1,2},{2,1},{3,0},{4,7},{5,6},{6,5},{7,4},{8,11},{9,10},{10,... | collective-permute-start | bytes 153608 | tf_op jit(solution)/shard_map/fold_sum/ppermute | solution.py:385
  5.8 4.1 %collective-permute-start.1 = (bf16[200,128]{1,0:T(8,128)(2,1)S(1)}, bf16[200,128]{1,0:T(8,128)(2,1)S(1)}, u32[]{:S(2)}, u32[]{:S(2)}) collective-permute-start(bf16[200,128]{1,0:T(8,128)(2,1)S(1)} %get-tuple-element.31), channel_id=1, source_target_pairs={{0,2},{1,3},{2,0},{3,1},{4,6},{5,7},{6,4},{7,5},{8,10},{9,11},{10,... | collective-permute-start | bytes 153608 | tf_op jit(solution)/shard_map/fold_sum/ppermute | solution.py:385
  6.2 4.1 %collective-permute-start.2 = (bf16[200,128]{1,0:T(8,128)(2,1)S(1)}, bf16[200,128]{1,0:T(8,128)(2,1)S(1)}, u32[]{:S(2)}, u32[]{:S(2)}) collective-permute-start(bf16[200,128]{1,0:T(8,128)(2,1)S(1)} %get-tuple-element.32), channel_id=1, source_target_pairs={{0,1},{1,0},{2,3},{3,2},{4,5},{5,4},{6,7},{7,6},{8,9},{9,8},{10,11... | collective-permute-start | bytes 153608 | tf_op jit(solution)/shard_map/fold_sum/ppermute | solution.py:385
  10.4 6.7 %collective-permute-start.4 = (bf16[200,128]{1,0:T(8,128)(2,1)S(1)}, bf16[200,128]{1,0:T(8,128)(2,1)S(1)}, u32[]{:S(2)}, u32[]{:S(2)}) collective-permute-start(bf16[200,128]{1,0:T(8,128)(2,1)S(1)} %get-tuple-element.36), channel_id=1, source_target_pairs={{0,4},{1,5},{2,6},{3,7},{4,0},{5,1},{6,2},{7,3},{8,12},{9,13},{10,... | collective-permute-start | bytes 153608 | tf_op jit(solution)/shard_map/fold_sum/ppermute | solution.py:385
  13.0 4.0 %collective-permute-start.3 = (bf16[160,128]{1,0:T(8,128)(2,1)S(1)}, bf16[160,128]{1,0:T(8,128)(2,1)S(1)}, u32[]{:S(2)}, u32[]{:S(2)}) collective-permute-start(bf16[160,128]{1,0:T(8,128)(2,1)S(1)} %tokens.1.refs_0_), channel_id=1, source_target_pairs={{0,16},{8,24},{16,0},{24,8},{1,17},{9,25},{17,1},{25,9},{2,18},{10... | collective-permute-start | bytes 122888 | tf_op jit(solution)/shard_map/tokens/ppermute | solution.py:385
  17.1 3.8 %collective-permute-start.5 = (bf16[3,200,128]{2,1,0:T(8,128)(2,1)S(1)}, bf16[3,200,128]{2,1,0:T(8,128)(2,1)S(1)}, u32[]{:S(2)}, u32[]{:S(2)}) collective-permute-start(bf16[3,200,128]{2,1,0:T(8,128)(2,1)S(1)} %get-tuple-element.37), channel_id=1, source_target_pairs={{0,8},{8,0},{16,24},{24,16},{1,9},{9,1},{17,25},{25,17},{2,10},{10... | collective-permute-start | bytes 460808 | tf_op jit(solution)/shard_map/gather/ppermute | solution.py:385
  17.1 6.4 %collective-permute-start.8 = (bf16[200,128]{1,0:T(8,128)(2,1)S(1)}, bf16[200,128]{1,0:T(8,128)(2,1)S(1)}, u32[]{:S(2)}, u32[]{:S(2)}) collective-permute-start(bf16[200,128]{1,0:T(8,128)(2,1)S(1)} %get-tuple-element.44.refs_6_.own_ref), channel_id=1, source_target_pairs={{0,16},{1,17},{2,18},{3,19},{4,20},{5,21},{6,22},{7,23},{8,24},{9,... | collective-permute-start | bytes 153608 | tf_op jit(solution)/shard_map/gather/ppermute | solution.py:495
  18.7 4.8 %collective-permute-start.7 = (bf16[200,128]{1,0:T(8,128)(2,1)S(1)}, bf16[200,128]{1,0:T(8,128)(2,1)S(1)}, u32[]{:S(2)}, u32[]{:S(2)}) collective-permute-start(bf16[200,128]{1,0:T(8,128)(2,1)S(1)} %get-tuple-element.44.refs_6_.own_ref), channel_id=1, source_target_pairs={{0,2},{1,3},{2,0},{3,1},{4,6},{5,7},{6,4},{7,5},{8,10},{9,11},{10,... | collective-permute-start | bytes 153608 | tf_op jit(solution)/shard_map/gather/ppermute | solution.py:495
  20.3 5.3 %collective-permute-start.6 = (bf16[200,128]{1,0:T(8,128)(2,1)S(1)}, bf16[200,128]{1,0:T(8,128)(2,1)S(1)}, u32[]{:S(2)}, u32[]{:S(2)}) collective-permute-start(bf16[200,128]{1,0:T(8,128)(2,1)S(1)} %get-tuple-element.44.refs_6_.own_ref), channel_id=1, source_target_pairs={{0,1},{1,0},{2,3},{3,2},{4,5},{5,4},{6,7},{7,6},{8,9},{9,8},{10,11... | collective-permute-start | bytes 153608 | tf_op jit(solution)/shard_map/gather/ppermute | solution.py:495
  20.9 6.6 %collective-permute-start.11 = (bf16[2,200,128]{2,1,0:T(8,128)(2,1)S(1)}, bf16[2,200,128]{2,1,0:T(8,128)(2,1)S(1)}, u32[]{:S(2)}, u32[]{:S(2)}) collective-permute-start(bf16[2,200,128]{2,1,0:T(8,128)(2,1)S(1)} %gather.1), channel_id=1, source_target_pairs={{0,3},{1,2},{2,1},{3,0},{4,7},{5,6},{6,5},{7,4},{8,27},{9,26},{10,... | collective-permute-start | bytes 307208 | tf_op jit(solution)/shard_map/gather/ppermute | solution.py:495
  22.3 6.7 %collective-permute-start.10 = (bf16[2,200,128]{2,1,0:T(8,128)(2,1)S(1)}, bf16[2,200,128]{2,1,0:T(8,128)(2,1)S(1)}, u32[]{:S(2)}, u32[]{:S(2)}) collective-permute-start(bf16[2,200,128]{2,1,0:T(8,128)(2,1)S(1)} %gather.1), channel_id=1, source_target_pairs={{0,17},{1,16},{2,19},{3,18},{4,21},{5,20},{6,23},{7,22},{8,26},{9,... | collective-permute-start | bytes 307208 | tf_op jit(solution)/shard_map/gather/ppermute | solution.py:495
  27.4 3.4 %collective-permute-start.9 = (bf16[128,512]{1,0:T(8,128)(2,1)S(1)}, bf16[128,512]{1,0:T(8,128)(2,1)S(1)}, u32[]{:S(2)}, u32[]{:S(2)}) collective-permute-start(bf16[128,512]{1,0:T(8,128)(2,1)S(1)} %attend.8), channel_id=1, source_target_pairs={{0,8},{8,0},{16,24},{24,16},{1,9},{9,1},{17,25},{25,17},{2,10},{10... | collective-permute-start | bytes 393224 | tf_op jit(solution)/shard_map/attend/ppermute | solution.py:385
  29.8 1.4 %collective-permute-start.12 = (bf16[128,512]{1,0:T(8,128)(2,1)S(1)}, bf16[128,512]{1,0:T(8,128)(2,1)S(1)}, u32[]{:S(2)}, u32[]{:S(2)}) collective-permute-start(bf16[128,512]{1,0:T(8,128)(2,1)S(1)} %attend.9), channel_id=1, source_target_pairs={{0,8},{8,0},{16,24},{24,16},{1,9},{9,1},{17,25},{25,17},{2,10},{10... | collective-permute-start | bytes 393224 | tf_op jit(solution)/shard_map/attend/ppermute | solution.py:385

commit v3 on v2

--- a/solution.py
+++ b/solution.py
@@ -485,7 +485,7 @@
     half = (len(partners) - near_count) // 2
     assert len(partners) == near_count + 2 * half
     neighbours = tuple(partners[:near_count])
-    lists = (tuple(reversed(partners[near_count : near_count + half])), tuple(partners[near_count + half :]))
+    lists = (tuple(partners[near_count : near_count + half]), tuple(reversed(partners[near_count + half :])))
 
     def spread(x, partner_of):
         pairs = []

time: 32.3 us -> 31.3 us (0.969)
  waiting for transfers between devices: 8.21 us -> 6.99 us
    ppermute x5, waiting for transfers between devices: 3.58 us -> 2.36 us  [spread(): return lax.ppermute(x, ('enc', 'seq'), pairs)]
  transfers between devices with their start and end apart: 13 -> 13, of which waited for: 6 -> 7; matrix products, arithmetic and copies ran while one was open for 0% -> 0% of each run, Pallas kernels for 20% -> 21%
where the time goes in v3:
time: 31.3 us; the launch traced here: 31.1 us
  starting transfers between devices  14.8 us (47%)
  Pallas kernels  9.16 us (29%)
  waiting for transfers between devices  6.99 us (22%)
    ppermute x8, starting transfers between devices, exchange(): return lax.ppermute(x, axis, [(i, i ^ k) for i in range(n)])  9.23 us
    ppermute x5, starting transfers between devices, spread(): return lax.ppermute(x, ('enc', 'seq'), pairs)  5.62 us
    ppermute x8, waiting for transfers between devices, exchange(): return lax.ppermute(x, axis, [(i, i ^ k) for i in range(n)])  4.63 us
    pallas_call x4, Pallas kernels, attend(): call(functools.partial(attend_kernel, len(groups)), vmem(6 + len(groups))...  3.46 us
    ppermute x5, waiting for transfers between devices, spread(): return lax.ppermute(x, ('enc', 'seq'), pairs)  2.36 us
    pallas_call x1, Pallas kernels, on_device(): call(functools.partial(fold_kernel, len(later)), hbm(4 + len(later)), [ja...  1.75 us
    pallas_call x1, Pallas kernels, on_device(): call(functools.partial(encode_kernel, caps), hbm(2) + vmem(2), [jax.Shape...  1.72 us
    pallas_call x1, Pallas kernels, on_device(): pl.pallas_call(functools.partial(output_kernel, heads, neighbours, lists)...  0.91 us
  transfers between devices with their start and end apart: 13, of which 7 were waited for; matrix products, arithmetic and copies ran while one was open for 0% of the time, Pallas kernels for 21%

profile of v3, /device:TPU:0, one launch (start us, length us, event | category | flops | bytes accessed | tf_op | source)
XLA Modules:
  0.0 31.1 jit_solution(15477526793938429796)
XLA Ops:
  0.0 1.8 %fold.1 = (bf16[64,2048]{1,0:T(8,128)(2,1)S(1)}, bf16[1024,512]{1,0:T(8,128)(2,1)S(1)}, bf16[432,512]{1,0:T(8,128)(2,1)S(1)}, f32[1,128]{1,0:T(1,128)S(1)}, f32[...) custom-call(bf16[64,2048]{1,0:T(8,128)(2,1)} %embed_hbm.1, ...), custom_call_target="tpu_custom_call" | custom-call | flops 200000000 | bytes 1000000 | tf_op jit(solution)/shard_map/fold/pallas_call | solution.py:424
  1.8 4.0 %collective-permute-start = (bf16[200,128]{1,0:T(8,128)(2,1)S(1)}, bf16[200,128]{1,0:T(8,128)(2,1)S(1)}, u32[]{:S(2)}, u32[]{:S(2)}) collective-permute-start(bf16[200,128]{1,0:T(8,128)(2,1)S(1)} %get-tuple-element.30), channel_id=1, source_target_pairs={{0,3},{1,2},{2,1},{3,0},{4,7},{5,6},{6,5},{7,4},{8,11},{9,10},{10,... | collective-permute-start | bytes 153608 | tf_op jit(solution)/shard_map/fold_sum/ppermute | solution.py:385
  5.8 0.4 %collective-permute-start.1 = (bf16[200,128]{1,0:T(8,128)(2,1)S(1)}, bf16[200,128]{1,0:T(8,128)(2,1)S(1)}, u32[]{:S(2)}, u32[]{:S(2)}) collective-permute-start(bf16[200,128]{1,0:T(8,128)(2,1)S(1)} %get-tuple-element.31), channel_id=1, source_target_pairs={{0,2},{1,3},{2,0},{3,1},{4,6},{5,7},{6,4},{7,5},{8,10},{9,11},{10,... | collective-permute-start | bytes 153608 | tf_op jit(solution)/shard_map/fold_sum/ppermute | solution.py:385
  6.4 1.7 %encode.1.refs_3_.refs_0_ = bf16[160,128]{1,0:T(8,128)(2,1)S(1)} custom-call(s32[1,1,3]{2,1,0:T(1,128)} %shape_hbm.1, s32[1,1,2,2]{3,2,1,0:T(2,128)} %plan_hbm.1, bf16[1024,512]{1,0:T(8,128)(2,1)S(1)} %get-tuple-element.33.feat_ref, bf16[432,512]{1,0:T(8,128)(2,1)S(1)} %get-tuple-element.34.conv_ref), custom_call_target="tpu_custom_call" | custom-call | flops 500000000 | bytes 2000000 | tf_op jit(solution)/shard_map/encode/pallas_call | solution.py:440
  8.2 1.7 %collective-permute-done.1.refs_1_ = bf16[200,128]{1,0:T(8,128)(2,1)S(1)} collective-permute-done((bf16[200,128]{1,0:T(8,128)(2,1)S(1)}, bf16[200,128]{1,0:T(8,128)(2,1)S(1)}, u32[]{:S(2)}, u32[]{:S(2)}) %collective-permute-start.1) | collective-permute-done | bytes 51232 | tf_op jit(solution)/shard_map/fold_sum/ppermute | solution.py:385
  9.9 0.4 %collective-permute-done.2.refs_2_ = bf16[200,128]{1,0:T(8,128)(2,1)S(1)} collective-permute-done((bf16[200,128]{1,0:T(8,128)(2,1)S(1)}, bf16[200,128]{1,0:T(8,128)(2,1)S(1)}, u32[]{:S(2)}, u32[]{:S(2)}) %collective-permute-start.2) | collective-permute-done | bytes 51232 | tf_op jit(solution)/shard_map/fold_sum/ppermute | solution.py:385
  10.4 2.7 %collective-permute-start.4 = (bf16[200,128]{1,0:T(8,128)(2,1)S(1)}, bf16[200,128]{1,0:T(8,128)(2,1)S(1)}, u32[]{:S(2)}, u32[]{:S(2)}) collective-permute-start(bf16[200,128]{1,0:T(8,128)(2,1)S(1)} %get-tuple-element.36), channel_id=1, source_target_pairs={{0,4},{1,5},{2,6},{3,7},{4,0},{5,1},{6,2},{7,3},{8,12},{9,13},{10,... | collective-permute-start | bytes 153608 | tf_op jit(solution)/shard_map/fold_sum/ppermute | solution.py:385
  13.0 1.5 %collective-permute-start.3 = (bf16[160,128]{1,0:T(8,128)(2,1)S(1)}, bf16[160,128]{1,0:T(8,128)(2,1)S(1)}, u32[]{:S(2)}, u32[]{:S(2)}) collective-permute-start(bf16[160,128]{1,0:T(8,128)(2,1)S(1)} %tokens.1.refs_0_), channel_id=1, source_target_pairs={{0,16},{8,24},{16,0},{24,8},{1,17},{9,25},{17,1},{25,9},{2,18},{10... | collective-permute-start | bytes 122888 | tf_op jit(solution)/shard_map/tokens/ppermute | solution.py:385
  14.6 0.5 %gram.1.refs_2_.gram_ref = bf16[128,64]{1,0:T(8,128)(2,1)S(1)} custom-call(bf16[64,2048]{1,0:T(8,128)(2,1)S(1)} %get-tuple-element.28.embed_ref, f32[200,128]{1,0:T(8,128)S(1)} %get-tuple-element.35.first_ref.refs_1_.keep_in), custom_call_target="tpu_custom_call" | custom-call | flops 1000000 | bytes 1000000 | tf_op jit(solution)/shard_map/gram/pallas_call | solution.py:464
  15.0 2.0 %collective-permute-done.3.refs_1_ = bf16[160,128]{1,0:T(8,128)(2,1)S(1)} collective-permute-done((bf16[160,128]{1,0:T(8,128)(2,1)S(1)}, bf16[160,128]{1,0:T(8,128)(2,1)S(1)}, u32[]{:S(2)}, u32[]{:S(2)}) %collective-permute-start.3) | collective-permute-done | bytes 40992 | tf_op jit(solution)/shard_map/tokens/ppermute | solution.py:385
  17.1 1.6 %collective-permute-start.8 = (bf16[200,128]{1,0:T(8,128)(2,1)S(1)}, bf16[200,128]{1,0:T(8,128)(2,1)S(1)}, u32[]{:S(2)}, u32[]{:S(2)}) collective-permute-start(bf16[200,128]{1,0:T(8,128)(2,1)S(1)} %get-tuple-element.44.refs_6_.own_ref), channel_id=1, source_target_pairs={{0,16},{1,17},{2,18},{3,19},{4,20},{5,21},{6,22},{7,23},{8,24},{9,... | collective-permute-start | bytes 153608 | tf_op jit(solution)/shard_map/gather/ppermute | solution.py:495
  18.7 1.6 %collective-permute-start.7 = (bf16[200,128]{1,0:T(8,128)(2,1)S(1)}, bf16[200,128]{1,0:T(8,128)(2,1)S(1)}, u32[]{:S(2)}, u32[]{:S(2)}) collective-permute-start(bf16[200,128]{1,0:T(8,128)(2,1)S(1)} %get-tuple-element.44.refs_6_.own_ref), channel_id=1, source_target_pairs={{0,2},{1,3},{2,0},{3,1},{4,6},{5,7},{6,4},{7,5},{8,10},{9,11},{10,... | collective-permute-start | bytes 153608 | tf_op jit(solution)/shard_map/gather/ppermute | solution.py:495
  20.3 0.5 %collective-permute-start.6 = (bf16[200,128]{1,0:T(8,128)(2,1)S(1)}, bf16[200,128]{1,0:T(8,128)(2,1)S(1)}, u32[]{:S(2)}, u32[]{:S(2)}) collective-permute-start(bf16[200,128]{1,0:T(8,128)(2,1)S(1)} %get-tuple-element.44.refs_6_.own_ref), channel_id=1, source_target_pairs={{0,1},{1,0},{2,3},{3,2},{4,5},{5,4},{6,7},{7,6},{8,9},{9,8},{10,11... | collective-permute-start | bytes 153608 | tf_op jit(solution)/shard_map/gather/ppermute | solution.py:495
  20.9 1.5 %collective-permute-start.11 = (bf16[2,200,128]{2,1,0:T(8,128)(2,1)S(1)}, bf16[2,200,128]{2,1,0:T(8,128)(2,1)S(1)}, u32[]{:S(2)}, u32[]{:S(2)}) collective-permute-start(bf16[2,200,128]{2,1,0:T(8,128)(2,1)S(1)} %gather.1), channel_id=1, source_target_pairs={{0,17},{1,16},{2,19},{3,18},{4,21},{5,20},{6,23},{7,22},{8,26},{9,... | collective-permute-start | bytes 307208 | tf_op jit(solution)/shard_map/gather/ppermute | solution.py:495
  22.4 0.4 %collective-permute-start.10 = (bf16[2,200,128]{2,1,0:T(8,128)(2,1)S(1)}, bf16[2,200,128]{2,1,0:T(8,128)(2,1)S(1)}, u32[]{:S(2)}, u32[]{:S(2)}) collective-permute-start(bf16[2,200,128]{2,1,0:T(8,128)(2,1)S(1)} %gather.1), channel_id=1, source_target_pairs={{0,3},{1,2},{2,1},{3,0},{4,7},{5,6},{6,5},{7,4},{8,27},{9,26},{10,... | collective-permute-start | bytes 307208 | tf_op jit(solution)/shard_map/gather/ppermute | solution.py:495
  22.8 0.7 %pack.1 = (bf16[72,512]{1,0:T(8,128)(2,1)S(1)}, bf16[512,128]{1,0:T(8,128)(2,1)S(1)}, bf16[128,512]{1,0:T(8,128)(2,1)S(1)}, f32[1,128]{1,0:T(1,128)S(1)}, bf16[1...) custom-call(f32[1,128]{1,0:T(1,128)S(1)} %get-tuple-element.26.q_gai, ...), custom_call_target="tpu_custom_call" | custom-call | flops 1000000 | bytes 1000000 | tf_op jit(solution)/shard_map/pack/pallas_call | solution.py:504
  23.6 0.9 %collective-permute-done.6.refs_7_ = bf16[200,128]{1,0:T(8,128)(2,1)S(1)} collective-permute-done((bf16[200,128]{1,0:T(8,128)(2,1)S(1)}, bf16[200,128]{1,0:T(8,128)(2,1)S(1)}, u32[]{:S(2)}, u32[]{:S(2)}) %collective-permute-start.6) | collective-permute-done | bytes 51232 | tf_op jit(solution)/shard_map/gather/ppermute | solution.py:495
  24.4 0.9 %attend.6.refs_10_.refs_0_ = bf16[128,512]{1,0:T(8,128)(2,1)S(1)} custom-call(bf16[72,512]{1,0:T(8,128)(2,1)S(1)} %get-tuple-element.38.refs_0_, bf16[512,128]{1,0:T(8,128)(2,1)S(1)} %get-tuple-element.39.refs_1_, bf16[128,512]{1,0:T(8,128)(2,1)S(1)} %get-tuple-element.40.refs_2_, f32[1,128]{1,0:T(1,128)S(1)} %get-tuple-element.41.refs_3_, ...), custom_call_target="tpu_custom_call" | custom-call | flops 800000000 | bytes 1000000 | tf_op jit(solution)/shard_map/attend/pallas_call | solution.py:519
  25.3 0.9 %attend.7.refs_1_.refs_8_.own_early_ref = bf16[128,512]{1,0:T(8,128)(2,1)S(1)} custom-call(bf16[72,512]{1,0:T(8,128)(2,1)S(1)} %get-tuple-element.38.refs_0_, bf16[512,128]{1,0:T(8,128)(2,1)S(1)} %get-tuple-element.39.refs_1_, bf16[128,512]{1,0:T(8,128)(2,1)S(1)} %get-tuple-element.40.refs_2_, f32[1,128]{1,0:T(1,128)S(1)} %get-tuple-element.41.refs_3_, ...), custom_call_target="tpu_custom_call" | custom-call | flops 800000000 | bytes 1000000 | tf_op jit(solution)/shard_map/attend/pallas_call | solution.py:519
  26.4 1.1 %collective-permute-done.11.refs_7_ = bf16[2,200,128]{2,1,0:T(8,128)(2,1)S(1)} collective-permute-done((bf16[2,200,128]{2,1,0:T(8,128)(2,1)S(1)}, bf16[2,200,128]{2,1,0:T(8,128)(2,1)S(1)}, u32[]{:S(2)}, u32[]{:S(2)}) %collective-permute-start.11) | collective-permute-done | bytes 102432 | tf_op jit(solution)/shard_map/gather/ppermute | solution.py:495
  27.9 0.9 %attend.9 = bf16[128,512]{1,0:T(8,128)(2,1)S(1)} custom-call(bf16[72,512]{1,0:T(8,128)(2,1)S(1)} %get-tuple-element.38.refs_0_, bf16[512,128]{1,0:T(8,128)(2,1)S(1)} %get-tuple-element.39.refs_1_, bf16[128,512]{1,0:T(8,128)(2,1)S(1)} %get-tuple-element.40.refs_2_, f32[1,128]{1,0:T(1,128)S(1)} %get-tuple-element.41.refs_3_, ...), custom_call_target="tpu_custom_call" | custom-call | flops 800000000 | bytes 1000000 | tf_op jit(solution)/shard_map/attend/pallas_call | solution.py:519
  28.9 0.9 %attend.10.own_rest_ref = bf16[128,512]{1,0:T(8,128)(2,1)S(1)} custom-call(bf16[72,512]{1,0:T(8,128)(2,1)S(1)} %get-tuple-element.38.refs_0_, bf16[512,128]{1,0:T(8,128)(2,1)S(1)} %get-tuple-element.39.refs_1_, bf16[128,512]{1,0:T(8,128)(2,1)S(1)} %get-tuple-element.40.refs_2_, f32[1,128]{1,0:T(1,128)S(1)} %get-tuple-element.41.refs_3_, ...), custom_call_target="tpu_custom_call" | custom-call | flops 800000000 | bytes 1000000 | tf_op jit(solution)/shard_map/attend/pallas_call | solution.py:519
  29.8 0.5 %collective-permute-done.12.near_rest_ref = bf16[128,512]{1,0:T(8,128)(2,1)S(1)} collective-permute-done((bf16[128,512]{1,0:T(8,128)(2,1)S(1)}, bf16[128,512]{1,0:T(8,128)(2,1)S(1)}, u32[]{:S(2)}, u32[]{:S(2)}) %collective-permute-start.12) | collective-permute-done | bytes 131104 | tf_op jit(solution)/shard_map/attend/ppermute | solution.py:385
  30.2 0.9 %attend.11 = bf16[1,128,2048]{2,1,0:T(8,128)(2,1)} custom-call(bf16[128,512]{1,0:T(8,128)(2,1)S(1)} %collective-permute-done.9.near_early_ref, bf16[128,512]{1,0:T(8,128)(2,1)S(1)} %collective-permute-done.12.near_rest_ref, bf16[128,512]{1,0:T(8,128)(2,1)S(1)} %attend.7.refs_1_.refs_8_.own_early_ref, bf16[128,512]{1,0:T(8,128)(2,1)S(1)} %attend.10.own_rest_ref), custom_call_target="tpu_custom_call" | custom-call | tf_op jit(solution)/shard_map/attend/pallas_call | solution.py:534
  (16 shorter events, 1.0 us)
Async XLA Ops:
  1.8 6.4 %collective-permute-start = (bf16[200,128]{1,0:T(8,128)(2,1)S(1)}, bf16[200,128]{1,0:T(8,128)(2,1)S(1)}, u32[]{:S(2)}, u32[]{:S(2)}) collective-permute-start(bf16[200,128]{1,0:T(8,128)(2,1)S(1)} %get-tuple-element.30), channel_id=1, source_target_pairs={{0,3},{1,2},{2,1},{3,0},{4,7},{5,6},{6,5},{7,4},{8,11},{9,10},{10,... | collective-permute-start | bytes 153608 | tf_op jit(solution)/shard_map/fold_sum/ppermute | solution.py:385
  5.8 4.1 %collective-permute-start.1 = (bf16[200,128]{1,0:T(8,128)(2,1)S(1)}, bf16[200,128]{1,0:T(8,128)(2,1)S(1)}, u32[]{:S(2)}, u32[]{:S(2)}) collective-permute-start(bf16[200,128]{1,0:T(8,128)(2,1)S(1)} %get-tuple-element.31), channel_id=1, source_target_pairs={{0,2},{1,3},{2,0},{3,1},{4,6},{5,7},{6,4},{7,5},{8,10},{9,11},{10,... | collective-permute-start | bytes 153608 | tf_op jit(solution)/shard_map/fold_sum/ppermute | solution.py:385
  6.2 4.1 %collective-permute-start.2 = (bf16[200,128]{1,0:T(8,128)(2,1)S(1)}, bf16[200,128]{1,0:T(8,128)(2,1)S(1)}, u32[]{:S(2)}, u32[]{:S(2)}) collective-permute-start(bf16[200,128]{1,0:T(8,128)(2,1)S(1)} %get-tuple-element.32), channel_id=1, source_target_pairs={{0,1},{1,0},{2,3},{3,2},{4,5},{5,4},{6,7},{7,6},{8,9},{9,8},{10,11... | collective-permute-start | bytes 153608 | tf_op jit(solution)/shard_map/fold_sum/ppermute | solution.py:385
  10.4 6.7 %collective-permute-start.4 = (bf16[200,128]{1,0:T(8,128)(2,1)S(1)}, bf16[200,128]{1,0:T(8,128)(2,1)S(1)}, u32[]{:S(2)}, u32[]{:S(2)}) collective-permute-start(bf16[200,128]{1,0:T(8,128)(2,1)S(1)} %get-tuple-element.36), channel_id=1, source_target_pairs={{0,4},{1,5},{2,6},{3,7},{4,0},{5,1},{6,2},{7,3},{8,12},{9,13},{10,... | collective-permute-start | bytes 153608 | tf_op jit(solution)/shard_map/fold_sum/ppermute | solution.py:385
  13.0 4.0 %collective-permute-start.3 = (bf16[160,128]{1,0:T(8,128)(2,1)S(1)}, bf16[160,128]{1,0:T(8,128)(2,1)S(1)}, u32[]{:S(2)}, u32[]{:S(2)}) collective-permute-start(bf16[160,128]{1,0:T(8,128)(2,1)S(1)} %tokens.1.refs_0_), channel_id=1, source_target_pairs={{0,16},{8,24},{16,0},{24,8},{1,17},{9,25},{17,1},{25,9},{2,18},{10... | collective-permute-start | bytes 122888 | tf_op jit(solution)/shard_map/tokens/ppermute | solution.py:385
  17.1 3.8 %collective-permute-start.5 = (bf16[3,200,128]{2,1,0:T(8,128)(2,1)S(1)}, bf16[3,200,128]{2,1,0:T(8,128)(2,1)S(1)}, u32[]{:S(2)}, u32[]{:S(2)}) collective-permute-start(bf16[3,200,128]{2,1,0:T(8,128)(2,1)S(1)} %get-tuple-element.37), channel_id=1, source_target_pairs={{0,8},{8,0},{16,24},{24,16},{1,9},{9,1},{17,25},{25,17},{2,10},{10... | collective-permute-start | bytes 460808 | tf_op jit(solution)/shard_map/gather/ppermute | solution.py:385
  17.1 6.4 %collective-permute-start.8 = (bf16[200,128]{1,0:T(8,128)(2,1)S(1)}, bf16[200,128]{1,0:T(8,128)(2,1)S(1)}, u32[]{:S(2)}, u32[]{:S(2)}) collective-permute-start(bf16[200,128]{1,0:T(8,128)(2,1)S(1)} %get-tuple-element.44.refs_6_.own_ref), channel_id=1, source_target_pairs={{0,16},{1,17},{2,18},{3,19},{4,20},{5,21},{6,22},{7,23},{8,24},{9,... | collective-permute-start | bytes 153608 | tf_op jit(solution)/shard_map/gather/ppermute | solution.py:495
  18.7 4.8 %collective-permute-start.7 = (bf16[200,128]{1,0:T(8,128)(2,1)S(1)}, bf16[200,128]{1,0:T(8,128)(2,1)S(1)}, u32[]{:S(2)}, u32[]{:S(2)}) collective-permute-start(bf16[200,128]{1,0:T(8,128)(2,1)S(1)} %get-tuple-element.44.refs_6_.own_ref), channel_id=1, source_target_pairs={{0,2},{1,3},{2,0},{3,1},{4,6},{5,7},{6,4},{7,5},{8,10},{9,11},{10,... | collective-permute-start | bytes 153608 | tf_op jit(solution)/shard_map/gather/ppermute | solution.py:495
  20.3 4.1 %collective-permute-start.6 = (bf16[200,128]{1,0:T(8,128)(2,1)S(1)}, bf16[200,128]{1,0:T(8,128)(2,1)S(1)}, u32[]{:S(2)}, u32[]{:S(2)}) collective-permute-start(bf16[200,128]{1,0:T(8,128)(2,1)S(1)} %get-tuple-element.44.refs_6_.own_ref), channel_id=1, source_target_pairs={{0,1},{1,0},{2,3},{3,2},{4,5},{5,4},{6,7},{7,6},{8,9},{9,8},{10,11... | collective-permute-start | bytes 153608 | tf_op jit(solution)/shard_map/gather/ppermute | solution.py:495
  20.9 6.7 %collective-permute-start.11 = (bf16[2,200,128]{2,1,0:T(8,128)(2,1)S(1)}, bf16[2,200,128]{2,1,0:T(8,128)(2,1)S(1)}, u32[]{:S(2)}, u32[]{:S(2)}) collective-permute-start(bf16[2,200,128]{2,1,0:T(8,128)(2,1)S(1)} %gather.1), channel_id=1, source_target_pairs={{0,17},{1,16},{2,19},{3,18},{4,21},{5,20},{6,23},{7,22},{8,26},{9,... | collective-permute-start | bytes 307208 | tf_op jit(solution)/shard_map/gather/ppermute | solution.py:495
  22.4 5.6 %collective-permute-start.10 = (bf16[2,200,128]{2,1,0:T(8,128)(2,1)S(1)}, bf16[2,200,128]{2,1,0:T(8,128)(2,1)S(1)}, u32[]{:S(2)}, u32[]{:S(2)}) collective-permute-start(bf16[2,200,128]{2,1,0:T(8,128)(2,1)S(1)} %gather.1), channel_id=1, source_target_pairs={{0,3},{1,2},{2,1},{3,0},{4,7},{5,6},{6,5},{7,4},{8,27},{9,26},{10,... | collective-permute-start | bytes 307208 | tf_op jit(solution)/shard_map/gather/ppermute | solution.py:495
  26.2 3.6 %collective-permute-start.9 = (bf16[128,512]{1,0:T(8,128)(2,1)S(1)}, bf16[128,512]{1,0:T(8,128)(2,1)S(1)}, u32[]{:S(2)}, u32[]{:S(2)}) collective-permute-start(bf16[128,512]{1,0:T(8,128)(2,1)S(1)} %attend.8), channel_id=1, source_target_pairs={{0,8},{8,0},{16,24},{24,16},{1,9},{9,1},{17,25},{25,17},{2,10},{10... | collective-permute-start | bytes 393224 | tf_op jit(solution)/shard_map/attend/ppermute | solution.py:385
  28.8 1.4 %collective-permute-start.12 = (bf16[128,512]{1,0:T(8,128)(2,1)S(1)}, bf16[128,512]{1,0:T(8,128)(2,1)S(1)}, u32[]{:S(2)}, u32[]{:S(2)}) collective-permute-start(bf16[128,512]{1,0:T(8,128)(2,1)S(1)} %attend.9), channel_id=1, source_target_pairs={{0,8},{8,0},{16,24},{24,16},{1,9},{9,1},{17,25},{25,17},{2,10},{10... | collective-permute-start | bytes 393224 | tf_op jit(solution)/shard_map/attend/ppermute | solution.py:385

commit v4 on v1

--- a/solution.py
+++ b/solution.py
@@ -14,6 +14,7 @@
 APAD = 72
 TAIL = 8
 TOKEN_ROWS = 80
+TOKEN_MESSAGE = 208
 eps_norm = 1e-06
 FAR = 2.0**20
 VMEM_LIMIT = 48 * 1024 * 1024
@@ -111,7 +112,7 @@
     out_ref[...] = total
     swap_ref[0] = total
     for i in range(count):
-        block = refs[i][...]
+        block = refs[i][...][: NBS * TOKEN_ROWS]
         rest = jnp.zeros((total.shape[0] - block.shape[0], LANES), jnp.bfloat16)
         swap_ref[1 + i] = jnp.concatenate([block, rest], axis=0)
 
@@ -197,6 +198,9 @@
             jnp.where(kind == 1, plan_ref[0, 0, b, 1], jnp.where(kind == 2, count, 0)),
         )
         pieces += [picked[:, b * BLOCK : (b + 1) * BLOCK], info.astype(jnp.float32)]
+    rest = out_ref.shape[0] - NBS * TOKEN_ROWS
+    if rest > 0:
+        pieces.append(jnp.zeros((rest, BLOCK), jnp.float32))
     out_ref[...] = jnp.concatenate(pieces, axis=0).astype(jnp.bfloat16)
 
 
@@ -440,7 +444,7 @@
         own_block = call(
             functools.partial(encode_kernel, caps),
             hbm(2) + vmem(2),
-            [jax.ShapeDtypeStruct((NBS * TOKEN_ROWS, BLOCK), bf16)],
+            [jax.ShapeDtypeStruct((TOKEN_MESSAGE, BLOCK), bf16)],
             [
                 pltpu.SMEM(clip_shape.shape, jnp.int32),
                 pltpu.SMEM(packing.shape, jnp.int32),
@@ -460,11 +464,7 @@
         else:
             send = sends[0]
 
-    with jax.named_scope("gram"):
-        gram = call(gram_kernel, vmem(1) + after(1), [jax.ShapeDtypeStruct((2 * feats, feats), bf16)])(embed, keep)[0]
-
     with jax.named_scope("tokens"):
-        own_block = gate(own_block, keep)
         blocks = [own_block] + [exchange(own_block, "enc", n_enc, k) for k in evens[1:]]
 
     with jax.named_scope("fold_sum"):
@@ -477,7 +477,7 @@
                     functools.partial(last_add_kernel, len(blocks)),
                     vmem(2 + len(blocks)) + after(1),
                     [folds(bf16), folds(bf16, 1 + len(blocks))],
-                )(keep, got, *blocks, gram)
+                )(keep, got, *blocks, keep)
 
     partners = [(far, k) for far in evens for k in range(heads) if far or k]
     partners.sort(key=lambda p: (p[0].bit_count() + p[1].bit_count(), p[0]))
@@ -499,6 +499,9 @@
         swapped = exchange(swap, "enc", n_enc, 1)
         pair = call(pair_kernel, vmem(2), [folds(bf16, 2)])(fresh, swapped)[0]
         got = [spread(pair, partner_of) for partner_of in zip(*lists)]
+
+    with jax.named_scope("gram"):
+        gram = call(gram_kernel, vmem(1) + after(1), [jax.ShapeDtypeStruct((2 * feats, feats), bf16)])(embed, pair)[0]
 
     with jax.named_scope("pack"):
         *shared, own_rows, own_mask, far_rows, far_mask = call(

time: 31.5 us -> 29.9 us (0.949)
  waiting for transfers between devices: 7.35 us -> 4.36 us
  starting transfers between devices: 14.7 us -> 16.1 us
    ppermute x5, waiting for transfers between devices: 2.72 us -> 1.22 us  [spread(): return lax.ppermute(x, ('enc', 'seq'), pairs)]
    ppermute x8, waiting for transfers between devices: 4.62 us -> 3.14 us  [exchange(): return lax.ppermute(x, axis, [(i, i ^ k) for i in range(n)])]
    ppermute x8, starting transfers between devices: 9.05 us -> 9.78 us  [exchange(): return lax.ppermute(x, axis, [(i, i ^ k) for i in range(n)])]
    ppermute x5, starting transfers between devices: 5.62 us -> 6.33 us  [spread(): return lax.ppermute(x, ('enc', 'seq'), pairs)]
  transfers between devices with their start and end apart: 13 -> 13, of which waited for: 6 -> 4; matrix products, arithmetic and copies ran while one was open for 0% -> 0% of each run, Pallas kernels for 21% -> 22%
where the time goes in v4:
time: 29.9 us; the launch traced here: 29.8 us
  starting transfers between devices  16.1 us (54%)
  Pallas kernels  9.16 us (31%)
  waiting for transfers between devices  4.36 us (15%)
    ppermute x8, starting transfers between devices, exchange(): return lax.ppermute(x, axis, [(i, i ^ k) for i in range(n)])  9.78 us
    ppermute x5, starting transfers between devices, spread(): return lax.ppermute(x, ('enc', 'seq'), pairs)  6.33 us
    pallas_call x4, Pallas kernels, attend(): call(functools.partial(attend_kernel, len(groups)), vmem(6 + len(groups))...  3.47 us
    ppermute x8, waiting for transfers between devices, exchange(): return lax.ppermute(x, axis, [(i, i ^ k) for i in range(n)])  3.14 us
    pallas_call x1, Pallas kernels, on_device(): call(functools.partial(fold_kernel, len(later)), hbm(4 + len(later)), [ja...  1.75 us
    pallas_call x1, Pallas kernels, on_device(): call(functools.partial(encode_kernel, caps), hbm(2) + vmem(2), [jax.Shape...  1.72 us
    ppermute x5, waiting for transfers between devices, spread(): return lax.ppermute(x, ('enc', 'seq'), pairs)  1.22 us
    pallas_call x1, Pallas kernels, on_device(): pl.pallas_call(functools.partial(output_kernel, heads, neighbours, lists)...  0.91 us
  transfers between devices with their start and end apart: 13, of which 4 were waited for; matrix products, arithmetic and copies ran while one was open for 0% of the time, Pallas kernels for 22%

profile of v4, /device:TPU:0, one launch (start us, length us, event | category | flops | bytes accessed | tf_op | source)
XLA Modules:
  0.0 29.8 jit_solution(3774481109328521407)
XLA Ops:
  0.0 1.8 %fold.1 = (bf16[64,2048]{1,0:T(8,128)(2,1)S(1)}, bf16[1024,512]{1,0:T(8,128)(2,1)S(1)}, bf16[432,512]{1,0:T(8,128)(2,1)S(1)}, f32[1,128]{1,0:T(1,128)S(1)}, f32[...) custom-call(bf16[64,2048]{1,0:T(8,128)(2,1)} %embed_hbm.1, ...), custom_call_target="tpu_custom_call" | custom-call | flops 200000000 | bytes 1000000 | tf_op jit(solution)/shard_map/fold/pallas_call | solution.py:428
  1.8 4.0 %collective-permute-start = (bf16[200,128]{1,0:T(8,128)(2,1)S(1)}, bf16[200,128]{1,0:T(8,128)(2,1)S(1)}, u32[]{:S(2)}, u32[]{:S(2)}) collective-permute-start(bf16[200,128]{1,0:T(8,128)(2,1)S(1)} %get-tuple-element.30), channel_id=1, source_target_pairs={{0,3},{1,2},{2,1},{3,0},{4,7},{5,6},{6,5},{7,4},{8,11},{9,10},{10,... | collective-permute-start | bytes 153608 | tf_op jit(solution)/shard_map/fold_sum/ppermute | solution.py:389
  5.8 0.4 %collective-permute-start.1 = (bf16[200,128]{1,0:T(8,128)(2,1)S(1)}, bf16[200,128]{1,0:T(8,128)(2,1)S(1)}, u32[]{:S(2)}, u32[]{:S(2)}) collective-permute-start(bf16[200,128]{1,0:T(8,128)(2,1)S(1)} %get-tuple-element.31), channel_id=1, source_target_pairs={{0,2},{1,3},{2,0},{3,1},{4,6},{5,7},{6,4},{7,5},{8,10},{9,11},{10,... | collective-permute-start | bytes 153608 | tf_op jit(solution)/shard_map/fold_sum/ppermute | solution.py:389
  6.2 0.2 collective-permute-start.2
  6.4 1.7 %encode.1.refs_3_.refs_0_ = bf16[208,128]{1,0:T(8,128)(2,1)S(1)} custom-call(s32[1,1,3]{2,1,0:T(1,128)} %shape_hbm.1, s32[1,1,2,2]{3,2,1,0:T(2,128)} %plan_hbm.1, bf16[1024,512]{1,0:T(8,128)(2,1)S(1)} %get-tuple-element.33.feat_ref, bf16[432,512]{1,0:T(8,128)(2,1)S(1)} %get-tuple-element.34.conv_ref), custom_call_target="tpu_custom_call" | custom-call | flops 500000000 | bytes 2000000 | tf_op jit(solution)/shard_map/encode/pallas_call | solution.py:444
  8.2 1.9 %collective-permute-start.4 = (bf16[208,128]{1,0:T(8,128)(2,1)S(1)}, bf16[208,128]{1,0:T(8,128)(2,1)S(1)}, u32[]{:S(2)}, u32[]{:S(2)}) collective-permute-start(bf16[208,128]{1,0:T(8,128)(2,1)S(1)} %encode.1.refs_3_.refs_0_), channel_id=1, source_target_pairs={{0,16},{8,24},{16,0},{24,8},{1,17},{9,25},{17,1},{25,9},{2,18},{10... | collective-permute-start | bytes 159752 | tf_op jit(solution)/shard_map/tokens/ppermute | solution.py:389
  10.1 0.3 collective-permute-done.2.refs_2_
  10.4 2.7 %collective-permute-start.3 = (bf16[200,128]{1,0:T(8,128)(2,1)S(1)}, bf16[200,128]{1,0:T(8,128)(2,1)S(1)}, u32[]{:S(2)}, u32[]{:S(2)}) collective-permute-start(bf16[200,128]{1,0:T(8,128)(2,1)S(1)} %get-tuple-element.36), channel_id=1, source_target_pairs={{0,4},{1,5},{2,6},{3,7},{4,0},{5,1},{6,2},{7,3},{8,12},{9,13},{10,... | collective-permute-start | bytes 153608 | tf_op jit(solution)/shard_map/fold_sum/ppermute | solution.py:389
  13.0 2.4 %collective-permute-done.3.got_ref = bf16[200,128]{1,0:T(8,128)(2,1)S(1)} collective-permute-done((bf16[200,128]{1,0:T(8,128)(2,1)S(1)}, bf16[200,128]{1,0:T(8,128)(2,1)S(1)}, u32[]{:S(2)}, u32[]{:S(2)}) %collective-permute-start.3) | collective-permute-done | bytes 51232 | tf_op jit(solution)/shard_map/fold_sum/ppermute | solution.py:389
  15.6 1.6 %collective-permute-start.8 = (bf16[200,128]{1,0:T(8,128)(2,1)S(1)}, bf16[200,128]{1,0:T(8,128)(2,1)S(1)}, u32[]{:S(2)}, u32[]{:S(2)}) collective-permute-start(bf16[200,128]{1,0:T(8,128)(2,1)S(1)} %get-tuple-element.37.own_ref.refs_6_), channel_id=1, source_target_pairs={{0,16},{1,17},{2,18},{3,19},{4,20},{5,21},{6,22},{7,23},{8,24},{9,... | collective-permute-start | bytes 153608 | tf_op jit(solution)/shard_map/gather/ppermute | solution.py:495
  17.1 1.6 %collective-permute-start.7 = (bf16[200,128]{1,0:T(8,128)(2,1)S(1)}, bf16[200,128]{1,0:T(8,128)(2,1)S(1)}, u32[]{:S(2)}, u32[]{:S(2)}) collective-permute-start(bf16[200,128]{1,0:T(8,128)(2,1)S(1)} %get-tuple-element.37.own_ref.refs_6_), channel_id=1, source_target_pairs={{0,2},{1,3},{2,0},{3,1},{4,6},{5,7},{6,4},{7,5},{8,10},{9,11},{10,... | collective-permute-start | bytes 153608 | tf_op jit(solution)/shard_map/gather/ppermute | solution.py:495
  18.7 0.5 %collective-permute-start.6 = (bf16[200,128]{1,0:T(8,128)(2,1)S(1)}, bf16[200,128]{1,0:T(8,128)(2,1)S(1)}, u32[]{:S(2)}, u32[]{:S(2)}) collective-permute-start(bf16[200,128]{1,0:T(8,128)(2,1)S(1)} %get-tuple-element.37.own_ref.refs_6_), channel_id=1, source_target_pairs={{0,1},{1,0},{2,3},{3,2},{4,5},{5,4},{6,7},{7,6},{8,9},{9,8},{10,11... | collective-permute-start | bytes 153608 | tf_op jit(solution)/shard_map/gather/ppermute | solution.py:495
  19.3 1.5 %collective-permute-start.11 = (bf16[2,200,128]{2,1,0:T(8,128)(2,1)S(1)}, bf16[2,200,128]{2,1,0:T(8,128)(2,1)S(1)}, u32[]{:S(2)}, u32[]{:S(2)}) collective-permute-start(bf16[2,200,128]{2,1,0:T(8,128)(2,1)S(1)} %gather.1.first_ref), channel_id=1, source_target_pairs={{0,17},{1,16},{2,19},{3,18},{4,21},{5,20},{6,23},{7,22},{8,27},{9,... | collective-permute-start | bytes 307208 | tf_op jit(solution)/shard_map/gather/ppermute | solution.py:495
  20.8 1.1 %collective-permute-start.10 = (bf16[2,200,128]{2,1,0:T(8,128)(2,1)S(1)}, bf16[2,200,128]{2,1,0:T(8,128)(2,1)S(1)}, u32[]{:S(2)}, u32[]{:S(2)}) collective-permute-start(bf16[2,200,128]{2,1,0:T(8,128)(2,1)S(1)} %gather.1.first_ref), channel_id=1, source_target_pairs={{0,3},{1,2},{2,1},{3,0},{4,7},{5,6},{6,5},{7,4},{8,26},{9,27},{10,... | collective-permute-start | bytes 307208 | tf_op jit(solution)/shard_map/gather/ppermute | solution.py:495
  21.9 0.5 %gram.1.gram_ref = bf16[128,64]{1,0:T(8,128)(2,1)S(1)} custom-call(bf16[64,2048]{1,0:T(8,128)(2,1)S(1)} %get-tuple-element.28.embed_ref, bf16[2,200,128]{2,1,0:T(8,128)(2,1)S(1)} %gather.1.first_ref), custom_call_target="tpu_custom_call" | custom-call | flops 1000000 | bytes 1000000 | tf_op jit(solution)/shard_map/gram/pallas_call | solution.py:504
  22.4 0.7 %pack.1 = (bf16[72,512]{1,0:T(8,128)(2,1)S(1)}, bf16[512,128]{1,0:T(8,128)(2,1)S(1)}, bf16[128,512]{1,0:T(8,128)(2,1)S(1)}, f32[1,128]{1,0:T(1,128)S(1)}, bf16[1...) custom-call(f32[1,128]{1,0:T(1,128)S(1)} %get-tuple-element.26.q_gai, ...), custom_call_target="tpu_custom_call" | custom-call | flops 1000000 | bytes 1000000 | tf_op jit(solution)/shard_map/pack/pallas_call | solution.py:507
  23.2 0.9 %attend.6.refs_10_.refs_0_ = bf16[128,512]{1,0:T(8,128)(2,1)S(1)} custom-call(bf16[72,512]{1,0:T(8,128)(2,1)S(1)} %get-tuple-element.39.refs_0_, bf16[512,128]{1,0:T(8,128)(2,1)S(1)} %get-tuple-element.40.refs_1_, bf16[128,512]{1,0:T(8,128)(2,1)S(1)} %get-tuple-element.41.refs_2_, f32[1,128]{1,0:T(1,128)S(1)} %get-tuple-element.42.refs_3_, ...), custom_call_target="tpu_custom_call" | custom-call | flops 800000000 | bytes 1000000 | tf_op jit(solution)/shard_map/attend/pallas_call | solution.py:522
  24.1 0.9 %attend.7.refs_1_.refs_8_.own_early_ref = bf16[128,512]{1,0:T(8,128)(2,1)S(1)} custom-call(bf16[72,512]{1,0:T(8,128)(2,1)S(1)} %get-tuple-element.39.refs_0_, bf16[512,128]{1,0:T(8,128)(2,1)S(1)} %get-tuple-element.40.refs_1_, bf16[128,512]{1,0:T(8,128)(2,1)S(1)} %get-tuple-element.41.refs_2_, f32[1,128]{1,0:T(1,128)S(1)} %get-tuple-element.42.refs_3_, ...), custom_call_target="tpu_custom_call" | custom-call | flops 800000000 | bytes 1000000 | tf_op jit(solution)/shard_map/attend/pallas_call | solution.py:522
  24.9 0.4 %collective-permute-start.9 = (bf16[128,512]{1,0:T(8,128)(2,1)S(1)}, bf16[128,512]{1,0:T(8,128)(2,1)S(1)}, u32[]{:S(2)}, u32[]{:S(2)}) collective-permute-start(bf16[128,512]{1,0:T(8,128)(2,1)S(1)} %attend.8), channel_id=1, source_target_pairs={{0,8},{8,0},{16,24},{24,16},{1,9},{9,1},{17,25},{25,17},{2,10},{10... | collective-permute-start | bytes 393224 | tf_op jit(solution)/shard_map/attend/ppermute | solution.py:389
  25.3 1.2 %collective-permute-done.11.refs_7_ = bf16[2,200,128]{2,1,0:T(8,128)(2,1)S(1)} collective-permute-done((bf16[2,200,128]{2,1,0:T(8,128)(2,1)S(1)}, bf16[2,200,128]{2,1,0:T(8,128)(2,1)S(1)}, u32[]{:S(2)}, u32[]{:S(2)}) %collective-permute-start.11) | collective-permute-done | bytes 102432 | tf_op jit(solution)/shard_map/gather/ppermute | solution.py:495
  26.6 0.9 %attend.9 = bf16[128,512]{1,0:T(8,128)(2,1)S(1)} custom-call(bf16[72,512]{1,0:T(8,128)(2,1)S(1)} %get-tuple-element.39.refs_0_, bf16[512,128]{1,0:T(8,128)(2,1)S(1)} %get-tuple-element.40.refs_1_, bf16[128,512]{1,0:T(8,128)(2,1)S(1)} %get-tuple-element.41.refs_2_, f32[1,128]{1,0:T(1,128)S(1)} %get-tuple-element.42.refs_3_, ...), custom_call_target="tpu_custom_call" | custom-call | flops 800000000 | bytes 1000000 | tf_op jit(solution)/shard_map/attend/pallas_call | solution.py:522
  27.5 0.9 %attend.10.own_rest_ref = bf16[128,512]{1,0:T(8,128)(2,1)S(1)} custom-call(bf16[72,512]{1,0:T(8,128)(2,1)S(1)} %get-tuple-element.39.refs_0_, bf16[512,128]{1,0:T(8,128)(2,1)S(1)} %get-tuple-element.40.refs_1_, bf16[128,512]{1,0:T(8,128)(2,1)S(1)} %get-tuple-element.41.refs_2_, f32[1,128]{1,0:T(1,128)S(1)} %get-tuple-element.42.refs_3_, ...), custom_call_target="tpu_custom_call" | custom-call | flops 800000000 | bytes 1000000 | tf_op jit(solution)/shard_map/attend/pallas_call | solution.py:522
  28.4 0.5 %collective-permute-done.12.near_rest_ref = bf16[128,512]{1,0:T(8,128)(2,1)S(1)} collective-permute-done((bf16[128,512]{1,0:T(8,128)(2,1)S(1)}, bf16[128,512]{1,0:T(8,128)(2,1)S(1)}, u32[]{:S(2)}, u32[]{:S(2)}) %collective-permute-start.12) | collective-permute-done | bytes 131104 | tf_op jit(solution)/shard_map/attend/ppermute | solution.py:389
  28.8 0.9 %attend.11 = bf16[1,128,2048]{2,1,0:T(8,128)(2,1)} custom-call(bf16[128,512]{1,0:T(8,128)(2,1)S(1)} %collective-permute-done.9.near_early_ref, bf16[128,512]{1,0:T(8,128)(2,1)S(1)} %collective-permute-done.12.near_rest_ref, bf16[128,512]{1,0:T(8,128)(2,1)S(1)} %attend.7.refs_1_.refs_8_.own_early_ref, bf16[128,512]{1,0:T(8,128)(2,1)S(1)} %attend.10.own_rest_ref), custom_call_target="tpu_custom_call" | custom-call | tf_op jit(solution)/shard_map/attend/pallas_call | solution.py:537
  (15 shorter events, 0.3 us)
Async XLA Ops:
  1.8 8.3 %collective-permute-start = (bf16[200,128]{1,0:T(8,128)(2,1)S(1)}, bf16[200,128]{1,0:T(8,128)(2,1)S(1)}, u32[]{:S(2)}, u32[]{:S(2)}) collective-permute-start(bf16[200,128]{1,0:T(8,128)(2,1)S(1)} %get-tuple-element.30), channel_id=1, source_target_pairs={{0,3},{1,2},{2,1},{3,0},{4,7},{5,6},{6,5},{7,4},{8,11},{9,10},{10,... | collective-permute-start | bytes 153608 | tf_op jit(solution)/shard_map/fold_sum/ppermute | solution.py:389
  5.8 4.3 %collective-permute-start.1 = (bf16[200,128]{1,0:T(8,128)(2,1)S(1)}, bf16[200,128]{1,0:T(8,128)(2,1)S(1)}, u32[]{:S(2)}, u32[]{:S(2)}) collective-permute-start(bf16[200,128]{1,0:T(8,128)(2,1)S(1)} %get-tuple-element.31), channel_id=1, source_target_pairs={{0,2},{1,3},{2,0},{3,1},{4,6},{5,7},{6,4},{7,5},{8,10},{9,11},{10,... | collective-permute-start | bytes 153608 | tf_op jit(solution)/shard_map/fold_sum/ppermute | solution.py:389
  6.2 4.1 %collective-permute-start.2 = (bf16[200,128]{1,0:T(8,128)(2,1)S(1)}, bf16[200,128]{1,0:T(8,128)(2,1)S(1)}, u32[]{:S(2)}, u32[]{:S(2)}) collective-permute-start(bf16[200,128]{1,0:T(8,128)(2,1)S(1)} %get-tuple-element.32), channel_id=1, source_target_pairs={{0,1},{1,0},{2,3},{3,2},{4,5},{5,4},{6,7},{7,6},{8,9},{9,8},{10,11... | collective-permute-start | bytes 153608 | tf_op jit(solution)/shard_map/fold_sum/ppermute | solution.py:389
  8.2 4.9 %collective-permute-start.4 = (bf16[208,128]{1,0:T(8,128)(2,1)S(1)}, bf16[208,128]{1,0:T(8,128)(2,1)S(1)}, u32[]{:S(2)}, u32[]{:S(2)}) collective-permute-start(bf16[208,128]{1,0:T(8,128)(2,1)S(1)} %encode.1.refs_3_.refs_0_), channel_id=1, source_target_pairs={{0,16},{8,24},{16,0},{24,8},{1,17},{9,25},{17,1},{25,9},{2,18},{10... | collective-permute-start | bytes 159752 | tf_op jit(solution)/shard_map/tokens/ppermute | solution.py:389
  10.4 5.1 %collective-permute-start.3 = (bf16[200,128]{1,0:T(8,128)(2,1)S(1)}, bf16[200,128]{1,0:T(8,128)(2,1)S(1)}, u32[]{:S(2)}, u32[]{:S(2)}) collective-permute-start(bf16[200,128]{1,0:T(8,128)(2,1)S(1)} %get-tuple-element.36), channel_id=1, source_target_pairs={{0,4},{1,5},{2,6},{3,7},{4,0},{5,1},{6,2},{7,3},{8,12},{9,13},{10,... | collective-permute-start | bytes 153608 | tf_op jit(solution)/shard_map/fold_sum/ppermute | solution.py:389
  15.5 3.8 %collective-permute-start.5 = (bf16[3,200,128]{2,1,0:T(8,128)(2,1)S(1)}, bf16[3,200,128]{2,1,0:T(8,128)(2,1)S(1)}, u32[]{:S(2)}, u32[]{:S(2)}) collective-permute-start(bf16[3,200,128]{2,1,0:T(8,128)(2,1)S(1)} %get-tuple-element.38), channel_id=1, source_target_pairs={{0,8},{8,0},{16,24},{24,16},{1,9},{9,1},{17,25},{25,17},{2,10},{10... | collective-permute-start | bytes 460808 | tf_op jit(solution)/shard_map/gather/ppermute | solution.py:389
  15.6 7.6 %collective-permute-start.8 = (bf16[200,128]{1,0:T(8,128)(2,1)S(1)}, bf16[200,128]{1,0:T(8,128)(2,1)S(1)}, u32[]{:S(2)}, u32[]{:S(2)}) collective-permute-start(bf16[200,128]{1,0:T(8,128)(2,1)S(1)} %get-tuple-element.37.own_ref.refs_6_), channel_id=1, source_target_pairs={{0,16},{1,17},{2,18},{3,19},{4,20},{5,21},{6,22},{7,23},{8,24},{9,... | collective-permute-start | bytes 153608 | tf_op jit(solution)/shard_map/gather/ppermute | solution.py:495
  17.1 6.0 %collective-permute-start.7 = (bf16[200,128]{1,0:T(8,128)(2,1)S(1)}, bf16[200,128]{1,0:T(8,128)(2,1)S(1)}, u32[]{:S(2)}, u32[]{:S(2)}) collective-permute-start(bf16[200,128]{1,0:T(8,128)(2,1)S(1)} %get-tuple-element.37.own_ref.refs_6_), channel_id=1, source_target_pairs={{0,2},{1,3},{2,0},{3,1},{4,6},{5,7},{6,4},{7,5},{8,10},{9,11},{10,... | collective-permute-start | bytes 153608 | tf_op jit(solution)/shard_map/gather/ppermute | solution.py:495
  18.7 4.5 %collective-permute-start.6 = (bf16[200,128]{1,0:T(8,128)(2,1)S(1)}, bf16[200,128]{1,0:T(8,128)(2,1)S(1)}, u32[]{:S(2)}, u32[]{:S(2)}) collective-permute-start(bf16[200,128]{1,0:T(8,128)(2,1)S(1)} %get-tuple-element.37.own_ref.refs_6_), channel_id=1, source_target_pairs={{0,1},{1,0},{2,3},{3,2},{4,5},{5,4},{6,7},{7,6},{8,9},{9,8},{10,11... | collective-permute-start | bytes 153608 | tf_op jit(solution)/shard_map/gather/ppermute | solution.py:495
  19.3 7.2 %collective-permute-start.11 = (bf16[2,200,128]{2,1,0:T(8,128)(2,1)S(1)}, bf16[2,200,128]{2,1,0:T(8,128)(2,1)S(1)}, u32[]{:S(2)}, u32[]{:S(2)}) collective-permute-start(bf16[2,200,128]{2,1,0:T(8,128)(2,1)S(1)} %gather.1.first_ref), channel_id=1, source_target_pairs={{0,17},{1,16},{2,19},{3,18},{4,21},{5,20},{6,23},{7,22},{8,27},{9,... | collective-permute-start | bytes 307208 | tf_op jit(solution)/shard_map/gather/ppermute | solution.py:495
  20.8 5.8 %collective-permute-start.10 = (bf16[2,200,128]{2,1,0:T(8,128)(2,1)S(1)}, bf16[2,200,128]{2,1,0:T(8,128)(2,1)S(1)}, u32[]{:S(2)}, u32[]{:S(2)}) collective-permute-start(bf16[2,200,128]{2,1,0:T(8,128)(2,1)S(1)} %gather.1.first_ref), channel_id=1, source_target_pairs={{0,3},{1,2},{2,1},{3,0},{4,7},{5,6},{6,5},{7,4},{8,26},{9,27},{10,... | collective-permute-start | bytes 307208 | tf_op jit(solution)/shard_map/gather/ppermute | solution.py:495
  24.9 3.4 %collective-permute-start.9 = (bf16[128,512]{1,0:T(8,128)(2,1)S(1)}, bf16[128,512]{1,0:T(8,128)(2,1)S(1)}, u32[]{:S(2)}, u32[]{:S(2)}) collective-permute-start(bf16[128,512]{1,0:T(8,128)(2,1)S(1)} %attend.8), channel_id=1, source_target_pairs={{0,8},{8,0},{16,24},{24,16},{1,9},{9,1},{17,25},{25,17},{2,10},{10... | collective-permute-start | bytes 393224 | tf_op jit(solution)/shard_map/attend/ppermute | solution.py:389
  27.4 1.4 %collective-permute-start.12 = (bf16[128,512]{1,0:T(8,128)(2,1)S(1)}, bf16[128,512]{1,0:T(8,128)(2,1)S(1)}, u32[]{:S(2)}, u32[]{:S(2)}) collective-permute-start(bf16[128,512]{1,0:T(8,128)(2,1)S(1)} %attend.9), channel_id=1, source_target_pairs={{0,8},{8,0},{16,24},{24,16},{1,9},{9,1},{17,25},{25,17},{2,10},{10... | collective-permute-start | bytes 393224 | tf_op jit(solution)/shard_map/attend/ppermute | solution.py:389

commit v5 on v4

--- a/solution.py
+++ b/solution.py
@@ -467,6 +467,9 @@
     with jax.named_scope("tokens"):
         blocks = [own_block] + [exchange(own_block, "enc", n_enc, k) for k in evens[1:]]
 
+    with jax.named_scope("gram"):
+        gram = call(gram_kernel, vmem(1) + after(1), [jax.ShapeDtypeStruct((2 * feats, feats), bf16)])(embed, keep)[0]
+
     with jax.named_scope("fold_sum"):
         for bit in range(log2(heads), log2(n_seq)):
             got = exchange(send, "seq", n_seq, 1 << bit)
@@ -477,7 +480,7 @@
                     functools.partial(last_add_kernel, len(blocks)),
                     vmem(2 + len(blocks)) + after(1),
                     [folds(bf16), folds(bf16, 1 + len(blocks))],
-                )(keep, got, *blocks, keep)
+                )(keep, got, *blocks, gram)
 
     partners = [(far, k) for far in evens for k in range(heads) if far or k]
     partners.sort(key=lambda p: (p[0].bit_count() + p[1].bit_count(), p[0]))
@@ -499,9 +502,6 @@
         swapped = exchange(swap, "enc", n_enc, 1)
         pair = call(pair_kernel, vmem(2), [folds(bf16, 2)])(fresh, swapped)[0]
         got = [spread(pair, partner_of) for partner_of in zip(*lists)]
-
-    with jax.named_scope("gram"):
-        gram = call(gram_kernel, vmem(1) + after(1), [jax.ShapeDtypeStruct((2 * feats, feats), bf16)])(embed, pair)[0]
 
     with jax.named_scope("pack"):
         *shared, own_rows, own_mask, far_rows, far_mask = call(

time: 29.9 us -> 29.9 us (level)
    ppermute x5, waiting for transfers between devices: 1.22 us -> 1.86 us  [spread(): return lax.ppermute(x, ('enc', 'seq'), pairs)]
    ppermute x8, waiting for transfers between devices: 3.14 us -> 2.64 us  [exchange(): return lax.ppermute(x, axis, [(i, i ^ k) for i in range(n)])]
  transfers between devices with their start and end apart: 13 -> 13, of which waited for: 4 -> 5; matrix products, arithmetic and copies ran while one was open for 0% -> 0% of each run, Pallas kernels for 22% -> 22%
where the time goes in v5:
time: 29.9 us; the launch traced here: 29.8 us
  starting transfers between devices  16 us (54%)
  Pallas kernels  9.14 us (31%)
  waiting for transfers between devices  4.51 us (15%)
    ppermute x8, starting transfers between devices, exchange(): return lax.ppermute(x, axis, [(i, i ^ k) for i in range(n)])  9.65 us
    ppermute x5, starting transfers between devices, spread(): return lax.ppermute(x, ('enc', 'seq'), pairs)  6.33 us
    pallas_call x4, Pallas kernels, attend(): call(functools.partial(attend_kernel, len(groups)), vmem(6 + len(groups))...  3.45 us
    ppermute x8, waiting for transfers between devices, exchange(): return lax.ppermute(x, axis, [(i, i ^ k) for i in range(n)])  2.64 us
    ppermute x5, waiting for transfers between devices, spread(): return lax.ppermute(x, ('enc', 'seq'), pairs)  1.86 us
    pallas_call x1, Pallas kernels, on_device(): call(functools.partial(fold_kernel, len(later)), hbm(4 + len(later)), [ja...  1.75 us
    pallas_call x1, Pallas kernels, on_device(): call(functools.partial(encode_kernel, caps), hbm(2) + vmem(2), [jax.Shape...  1.72 us
    pallas_call x1, Pallas kernels, on_device(): pl.pallas_call(functools.partial(output_kernel, heads, neighbours, lists)...  0.91 us
  transfers between devices with their start and end apart: 13, of which 5 were waited for; matrix products, arithmetic and copies ran while one was open for 0% of the time, Pallas kernels for 22%

profile of v5, /device:TPU:0, one launch (start us, length us, event | category | flops | bytes accessed | tf_op | source)
XLA Modules:
  0.0 29.8 jit_solution(3075367264327521926)
XLA Ops:
  0.0 1.8 %fold.1 = (bf16[64,2048]{1,0:T(8,128)(2,1)S(1)}, bf16[1024,512]{1,0:T(8,128)(2,1)S(1)}, bf16[432,512]{1,0:T(8,128)(2,1)S(1)}, f32[1,128]{1,0:T(1,128)S(1)}, f32[...) custom-call(bf16[64,2048]{1,0:T(8,128)(2,1)} %embed_hbm.1, ...), custom_call_target="tpu_custom_call" | custom-call | flops 200000000 | bytes 1000000 | tf_op jit(solution)/shard_map/fold/pallas_call | solution.py:428
  1.8 4.0 %collective-permute-start = (bf16[200,128]{1,0:T(8,128)(2,1)S(1)}, bf16[200,128]{1,0:T(8,128)(2,1)S(1)}, u32[]{:S(2)}, u32[]{:S(2)}) collective-permute-start(bf16[200,128]{1,0:T(8,128)(2,1)S(1)} %get-tuple-element.30), channel_id=1, source_target_pairs={{0,3},{1,2},{2,1},{3,0},{4,7},{5,6},{6,5},{7,4},{8,11},{9,10},{10,... | collective-permute-start | bytes 153608 | tf_op jit(solution)/shard_map/fold_sum/ppermute | solution.py:389
  5.8 0.4 %collective-permute-start.1 = (bf16[200,128]{1,0:T(8,128)(2,1)S(1)}, bf16[200,128]{1,0:T(8,128)(2,1)S(1)}, u32[]{:S(2)}, u32[]{:S(2)}) collective-permute-start(bf16[200,128]{1,0:T(8,128)(2,1)S(1)} %get-tuple-element.31), channel_id=1, source_target_pairs={{0,2},{1,3},{2,0},{3,1},{4,6},{5,7},{6,4},{7,5},{8,10},{9,11},{10,... | collective-permute-start | bytes 153608 | tf_op jit(solution)/shard_map/fold_sum/ppermute | solution.py:389
  6.2 0.2 collective-permute-start.2
  6.4 1.7 %encode.1.refs_3_.refs_0_ = bf16[208,128]{1,0:T(8,128)(2,1)S(1)} custom-call(s32[1,1,3]{2,1,0:T(1,128)} %shape_hbm.1, s32[1,1,2,2]{3,2,1,0:T(2,128)} %plan_hbm.1, bf16[1024,512]{1,0:T(8,128)(2,1)S(1)} %get-tuple-element.33.feat_ref, bf16[432,512]{1,0:T(8,128)(2,1)S(1)} %get-tuple-element.34.conv_ref), custom_call_target="tpu_custom_call" | custom-call | flops 500000000 | bytes 2000000 | tf_op jit(solution)/shard_map/encode/pallas_call | solution.py:444
  8.2 1.9 %collective-permute-start.3 = (bf16[208,128]{1,0:T(8,128)(2,1)S(1)}, bf16[208,128]{1,0:T(8,128)(2,1)S(1)}, u32[]{:S(2)}, u32[]{:S(2)}) collective-permute-start(bf16[208,128]{1,0:T(8,128)(2,1)S(1)} %encode.1.refs_3_.refs_0_), channel_id=1, source_target_pairs={{0,16},{8,24},{16,0},{24,8},{1,17},{9,25},{17,1},{25,9},{2,18},{10... | collective-permute-start | bytes 159752 | tf_op jit(solution)/shard_map/tokens/ppermute | solution.py:389
  10.1 0.3 collective-permute-done.2.refs_2_
  10.4 2.7 %collective-permute-start.4 = (bf16[200,128]{1,0:T(8,128)(2,1)S(1)}, bf16[200,128]{1,0:T(8,128)(2,1)S(1)}, u32[]{:S(2)}, u32[]{:S(2)}) collective-permute-start(bf16[200,128]{1,0:T(8,128)(2,1)S(1)} %get-tuple-element.36), channel_id=1, source_target_pairs={{0,4},{1,5},{2,6},{3,7},{4,0},{5,1},{6,2},{7,3},{8,12},{9,13},{10,... | collective-permute-start | bytes 153608 | tf_op jit(solution)/shard_map/fold_sum/ppermute | solution.py:389
  13.0 0.5 %gram.1.refs_2_.gram_ref = bf16[128,64]{1,0:T(8,128)(2,1)S(1)} custom-call(bf16[64,2048]{1,0:T(8,128)(2,1)S(1)} %get-tuple-element.28.embed_ref, f32[200,128]{1,0:T(8,128)S(1)} %get-tuple-element.35.first_ref.keep_in), custom_call_target="tpu_custom_call" | custom-call | flops 1000000 | bytes 1000000 | tf_op jit(solution)/shard_map/gram/pallas_call | solution.py:471
  13.5 1.9 %collective-permute-done.4.got_ref = bf16[200,128]{1,0:T(8,128)(2,1)S(1)} collective-permute-done((bf16[200,128]{1,0:T(8,128)(2,1)S(1)}, bf16[200,128]{1,0:T(8,128)(2,1)S(1)}, u32[]{:S(2)}, u32[]{:S(2)}) %collective-permute-start.4) | collective-permute-done | bytes 51232 | tf_op jit(solution)/shard_map/fold_sum/ppermute | solution.py:389
  15.6 1.6 %collective-permute-start.8 = (bf16[200,128]{1,0:T(8,128)(2,1)S(1)}, bf16[200,128]{1,0:T(8,128)(2,1)S(1)}, u32[]{:S(2)}, u32[]{:S(2)}) collective-permute-start(bf16[200,128]{1,0:T(8,128)(2,1)S(1)} %get-tuple-element.44.refs_6_.own_ref), channel_id=1, source_target_pairs={{0,16},{1,17},{2,18},{3,19},{4,20},{5,21},{6,22},{7,23},{8,24},{9,... | collective-permute-start | bytes 153608 | tf_op jit(solution)/shard_map/gather/ppermute | solution.py:498
  17.1 1.6 %collective-permute-start.7 = (bf16[200,128]{1,0:T(8,128)(2,1)S(1)}, bf16[200,128]{1,0:T(8,128)(2,1)S(1)}, u32[]{:S(2)}, u32[]{:S(2)}) collective-permute-start(bf16[200,128]{1,0:T(8,128)(2,1)S(1)} %get-tuple-element.44.refs_6_.own_ref), channel_id=1, source_target_pairs={{0,2},{1,3},{2,0},{3,1},{4,6},{5,7},{6,4},{7,5},{8,10},{9,11},{10,... | collective-permute-start | bytes 153608 | tf_op jit(solution)/shard_map/gather/ppermute | solution.py:498
  18.7 0.5 %collective-permute-start.6 = (bf16[200,128]{1,0:T(8,128)(2,1)S(1)}, bf16[200,128]{1,0:T(8,128)(2,1)S(1)}, u32[]{:S(2)}, u32[]{:S(2)}) collective-permute-start(bf16[200,128]{1,0:T(8,128)(2,1)S(1)} %get-tuple-element.44.refs_6_.own_ref), channel_id=1, source_target_pairs={{0,1},{1,0},{2,3},{3,2},{4,5},{5,4},{6,7},{7,6},{8,9},{9,8},{10,11... | collective-permute-start | bytes 153608 | tf_op jit(solution)/shard_map/gather/ppermute | solution.py:498
  19.3 1.5 %collective-permute-start.11 = (bf16[2,200,128]{2,1,0:T(8,128)(2,1)S(1)}, bf16[2,200,128]{2,1,0:T(8,128)(2,1)S(1)}, u32[]{:S(2)}, u32[]{:S(2)}) collective-permute-start(bf16[2,200,128]{2,1,0:T(8,128)(2,1)S(1)} %gather.1), channel_id=1, source_target_pairs={{0,17},{1,16},{2,19},{3,18},{4,21},{5,20},{6,23},{7,22},{8,27},{9,... | collective-permute-start | bytes 307208 | tf_op jit(solution)/shard_map/gather/ppermute | solution.py:498
  20.8 1.1 %collective-permute-start.10 = (bf16[2,200,128]{2,1,0:T(8,128)(2,1)S(1)}, bf16[2,200,128]{2,1,0:T(8,128)(2,1)S(1)}, u32[]{:S(2)}, u32[]{:S(2)}) collective-permute-start(bf16[2,200,128]{2,1,0:T(8,128)(2,1)S(1)} %gather.1), channel_id=1, source_target_pairs={{0,3},{1,2},{2,1},{3,0},{4,7},{5,6},{6,5},{7,4},{8,26},{9,27},{10,... | collective-permute-start | bytes 307208 | tf_op jit(solution)/shard_map/gather/ppermute | solution.py:498
  21.9 0.7 %pack.1 = (bf16[72,512]{1,0:T(8,128)(2,1)S(1)}, bf16[512,128]{1,0:T(8,128)(2,1)S(1)}, bf16[128,512]{1,0:T(8,128)(2,1)S(1)}, f32[1,128]{1,0:T(1,128)S(1)}, bf16[1...) custom-call(f32[1,128]{1,0:T(1,128)S(1)} %get-tuple-element.26.q_gai, ...), custom_call_target="tpu_custom_call" | custom-call | flops 1000000 | bytes 1000000 | tf_op jit(solution)/shard_map/pack/pallas_call | solution.py:507
  22.8 0.9 %attend.6.refs_10_.refs_0_ = bf16[128,512]{1,0:T(8,128)(2,1)S(1)} custom-call(bf16[72,512]{1,0:T(8,128)(2,1)S(1)} %get-tuple-element.38.refs_0_, bf16[512,128]{1,0:T(8,128)(2,1)S(1)} %get-tuple-element.39.refs_1_, bf16[128,512]{1,0:T(8,128)(2,1)S(1)} %get-tuple-element.40.refs_2_, f32[1,128]{1,0:T(1,128)S(1)} %get-tuple-element.41.refs_3_, ...), custom_call_target="tpu_custom_call" | custom-call | flops 800000000 | bytes 1000000 | tf_op jit(solution)/shard_map/attend/pallas_call | solution.py:522
  23.7 0.9 %attend.7.refs_1_.refs_8_.own_early_ref = bf16[128,512]{1,0:T(8,128)(2,1)S(1)} custom-call(bf16[72,512]{1,0:T(8,128)(2,1)S(1)} %get-tuple-element.38.refs_0_, bf16[512,128]{1,0:T(8,128)(2,1)S(1)} %get-tuple-element.39.refs_1_, bf16[128,512]{1,0:T(8,128)(2,1)S(1)} %get-tuple-element.40.refs_2_, f32[1,128]{1,0:T(1,128)S(1)} %get-tuple-element.41.refs_3_, ...), custom_call_target="tpu_custom_call" | custom-call | flops 800000000 | bytes 1000000 | tf_op jit(solution)/shard_map/attend/pallas_call | solution.py:522
  24.6 0.3 collective-permute-start.9
  24.9 1.7 %collective-permute-done.11.refs_7_ = bf16[2,200,128]{2,1,0:T(8,128)(2,1)S(1)} collective-permute-done((bf16[2,200,128]{2,1,0:T(8,128)(2,1)S(1)}, bf16[2,200,128]{2,1,0:T(8,128)(2,1)S(1)}, u32[]{:S(2)}, u32[]{:S(2)}) %collective-permute-start.11) | collective-permute-done | bytes 102432 | tf_op jit(solution)/shard_map/gather/ppermute | solution.py:498
  26.6 0.9 %attend.9 = bf16[128,512]{1,0:T(8,128)(2,1)S(1)} custom-call(bf16[72,512]{1,0:T(8,128)(2,1)S(1)} %get-tuple-element.38.refs_0_, bf16[512,128]{1,0:T(8,128)(2,1)S(1)} %get-tuple-element.39.refs_1_, bf16[128,512]{1,0:T(8,128)(2,1)S(1)} %get-tuple-element.40.refs_2_, f32[1,128]{1,0:T(1,128)S(1)} %get-tuple-element.41.refs_3_, ...), custom_call_target="tpu_custom_call" | custom-call | flops 800000000 | bytes 1000000 | tf_op jit(solution)/shard_map/attend/pallas_call | solution.py:522
  27.5 0.9 %attend.10.own_rest_ref = bf16[128,512]{1,0:T(8,128)(2,1)S(1)} custom-call(bf16[72,512]{1,0:T(8,128)(2,1)S(1)} %get-tuple-element.38.refs_0_, bf16[512,128]{1,0:T(8,128)(2,1)S(1)} %get-tuple-element.39.refs_1_, bf16[128,512]{1,0:T(8,128)(2,1)S(1)} %get-tuple-element.40.refs_2_, f32[1,128]{1,0:T(1,128)S(1)} %get-tuple-element.41.refs_3_, ...), custom_call_target="tpu_custom_call" | custom-call | flops 800000000 | bytes 1000000 | tf_op jit(solution)/shard_map/attend/pallas_call | solution.py:522
  28.4 0.5 %collective-permute-done.12.near_rest_ref = bf16[128,512]{1,0:T(8,128)(2,1)S(1)} collective-permute-done((bf16[128,512]{1,0:T(8,128)(2,1)S(1)}, bf16[128,512]{1,0:T(8,128)(2,1)S(1)}, u32[]{:S(2)}, u32[]{:S(2)}) %collective-permute-start.12) | collective-permute-done | bytes 131104 | tf_op jit(solution)/shard_map/attend/ppermute | solution.py:389
  28.8 0.9 %attend.11 = bf16[1,128,2048]{2,1,0:T(8,128)(2,1)} custom-call(bf16[128,512]{1,0:T(8,128)(2,1)S(1)} %collective-permute-done.9.near_early_ref, bf16[128,512]{1,0:T(8,128)(2,1)S(1)} %collective-permute-done.12.near_rest_ref, bf16[128,512]{1,0:T(8,128)(2,1)S(1)} %attend.7.refs_1_.refs_8_.own_early_ref, bf16[128,512]{1,0:T(8,128)(2,1)S(1)} %attend.10.own_rest_ref), custom_call_target="tpu_custom_call" | custom-call | tf_op jit(solution)/shard_map/attend/pallas_call | solution.py:537
  (15 shorter events, 0.4 us)
Async XLA Ops:
  1.8 8.3 %collective-permute-start = (bf16[200,128]{1,0:T(8,128)(2,1)S(1)}, bf16[200,128]{1,0:T(8,128)(2,1)S(1)}, u32[]{:S(2)}, u32[]{:S(2)}) collective-permute-start(bf16[200,128]{1,0:T(8,128)(2,1)S(1)} %get-tuple-element.30), channel_id=1, source_target_pairs={{0,3},{1,2},{2,1},{3,0},{4,7},{5,6},{6,5},{7,4},{8,11},{9,10},{10,... | collective-permute-start | bytes 153608 | tf_op jit(solution)/shard_map/fold_sum/ppermute | solution.py:389
  5.8 4.3 %collective-permute-start.1 = (bf16[200,128]{1,0:T(8,128)(2,1)S(1)}, bf16[200,128]{1,0:T(8,128)(2,1)S(1)}, u32[]{:S(2)}, u32[]{:S(2)}) collective-permute-start(bf16[200,128]{1,0:T(8,128)(2,1)S(1)} %get-tuple-element.31), channel_id=1, source_target_pairs={{0,2},{1,3},{2,0},{3,1},{4,6},{5,7},{6,4},{7,5},{8,10},{9,11},{10,... | collective-permute-start | bytes 153608 | tf_op jit(solution)/shard_map/fold_sum/ppermute | solution.py:389
  6.2 4.1 %collective-permute-start.2 = (bf16[200,128]{1,0:T(8,128)(2,1)S(1)}, bf16[200,128]{1,0:T(8,128)(2,1)S(1)}, u32[]{:S(2)}, u32[]{:S(2)}) collective-permute-start(bf16[200,128]{1,0:T(8,128)(2,1)S(1)} %get-tuple-element.32), channel_id=1, source_target_pairs={{0,1},{1,0},{2,3},{3,2},{4,5},{5,4},{6,7},{7,6},{8,9},{9,8},{10,11... | collective-permute-start | bytes 153608 | tf_op jit(solution)/shard_map/fold_sum/ppermute | solution.py:389
  8.2 5.4 %collective-permute-start.3 = (bf16[208,128]{1,0:T(8,128)(2,1)S(1)}, bf16[208,128]{1,0:T(8,128)(2,1)S(1)}, u32[]{:S(2)}, u32[]{:S(2)}) collective-permute-start(bf16[208,128]{1,0:T(8,128)(2,1)S(1)} %encode.1.refs_3_.refs_0_), channel_id=1, source_target_pairs={{0,16},{8,24},{16,0},{24,8},{1,17},{9,25},{17,1},{25,9},{2,18},{10... | collective-permute-start | bytes 159752 | tf_op jit(solution)/shard_map/tokens/ppermute | solution.py:389
  10.4 5.1 %collective-permute-start.4 = (bf16[200,128]{1,0:T(8,128)(2,1)S(1)}, bf16[200,128]{1,0:T(8,128)(2,1)S(1)}, u32[]{:S(2)}, u32[]{:S(2)}) collective-permute-start(bf16[200,128]{1,0:T(8,128)(2,1)S(1)} %get-tuple-element.36), channel_id=1, source_target_pairs={{0,4},{1,5},{2,6},{3,7},{4,0},{5,1},{6,2},{7,3},{8,12},{9,13},{10,... | collective-permute-start | bytes 153608 | tf_op jit(solution)/shard_map/fold_sum/ppermute | solution.py:389
  15.5 3.8 %collective-permute-start.5 = (bf16[3,200,128]{2,1,0:T(8,128)(2,1)S(1)}, bf16[3,200,128]{2,1,0:T(8,128)(2,1)S(1)}, u32[]{:S(2)}, u32[]{:S(2)}) collective-permute-start(bf16[3,200,128]{2,1,0:T(8,128)(2,1)S(1)} %get-tuple-element.37), channel_id=1, source_target_pairs={{0,8},{8,0},{16,24},{24,16},{1,9},{9,1},{17,25},{25,17},{2,10},{10... | collective-permute-start | bytes 460808 | tf_op jit(solution)/shard_map/gather/ppermute | solution.py:389
  15.6 7.1 %collective-permute-start.8 = (bf16[200,128]{1,0:T(8,128)(2,1)S(1)}, bf16[200,128]{1,0:T(8,128)(2,1)S(1)}, u32[]{:S(2)}, u32[]{:S(2)}) collective-permute-start(bf16[200,128]{1,0:T(8,128)(2,1)S(1)} %get-tuple-element.44.refs_6_.own_ref), channel_id=1, source_target_pairs={{0,16},{1,17},{2,18},{3,19},{4,20},{5,21},{6,22},{7,23},{8,24},{9,... | collective-permute-start | bytes 153608 | tf_op jit(solution)/shard_map/gather/ppermute | solution.py:498
  17.1 5.5 %collective-permute-start.7 = (bf16[200,128]{1,0:T(8,128)(2,1)S(1)}, bf16[200,128]{1,0:T(8,128)(2,1)S(1)}, u32[]{:S(2)}, u32[]{:S(2)}) collective-permute-start(bf16[200,128]{1,0:T(8,128)(2,1)S(1)} %get-tuple-element.44.refs_6_.own_ref), channel_id=1, source_target_pairs={{0,2},{1,3},{2,0},{3,1},{4,6},{5,7},{6,4},{7,5},{8,10},{9,11},{10,... | collective-permute-start | bytes 153608 | tf_op jit(solution)/shard_map/gather/ppermute | solution.py:498
  18.7 4.1 %collective-permute-start.6 = (bf16[200,128]{1,0:T(8,128)(2,1)S(1)}, bf16[200,128]{1,0:T(8,128)(2,1)S(1)}, u32[]{:S(2)}, u32[]{:S(2)}) collective-permute-start(bf16[200,128]{1,0:T(8,128)(2,1)S(1)} %get-tuple-element.44.refs_6_.own_ref), channel_id=1, source_target_pairs={{0,1},{1,0},{2,3},{3,2},{4,5},{5,4},{6,7},{7,6},{8,9},{9,8},{10,11... | collective-permute-start | bytes 153608 | tf_op jit(solution)/shard_map/gather/ppermute | solution.py:498
  19.3 7.2 %collective-permute-start.11 = (bf16[2,200,128]{2,1,0:T(8,128)(2,1)S(1)}, bf16[2,200,128]{2,1,0:T(8,128)(2,1)S(1)}, u32[]{:S(2)}, u32[]{:S(2)}) collective-permute-start(bf16[2,200,128]{2,1,0:T(8,128)(2,1)S(1)} %gather.1), channel_id=1, source_target_pairs={{0,17},{1,16},{2,19},{3,18},{4,21},{5,20},{6,23},{7,22},{8,27},{9,... | collective-permute-start | bytes 307208 | tf_op jit(solution)/shard_map/gather/ppermute | solution.py:498
  20.8 5.8 %collective-permute-start.10 = (bf16[2,200,128]{2,1,0:T(8,128)(2,1)S(1)}, bf16[2,200,128]{2,1,0:T(8,128)(2,1)S(1)}, u32[]{:S(2)}, u32[]{:S(2)}) collective-permute-start(bf16[2,200,128]{2,1,0:T(8,128)(2,1)S(1)} %gather.1), channel_id=1, source_target_pairs={{0,3},{1,2},{2,1},{3,0},{4,7},{5,6},{6,5},{7,4},{8,26},{9,27},{10,... | collective-permute-start | bytes 307208 | tf_op jit(solution)/shard_map/gather/ppermute | solution.py:498
  24.6 3.8 %collective-permute-start.9 = (bf16[128,512]{1,0:T(8,128)(2,1)S(1)}, bf16[128,512]{1,0:T(8,128)(2,1)S(1)}, u32[]{:S(2)}, u32[]{:S(2)}) collective-permute-start(bf16[128,512]{1,0:T(8,128)(2,1)S(1)} %attend.8), channel_id=1, source_target_pairs={{0,8},{8,0},{16,24},{24,16},{1,9},{9,1},{17,25},{25,17},{2,10},{10... | collective-permute-start | bytes 393224 | tf_op jit(solution)/shard_map/attend/ppermute | solution.py:389
  27.4 1.4 %collective-permute-start.12 = (bf16[128,512]{1,0:T(8,128)(2,1)S(1)}, bf16[128,512]{1,0:T(8,128)(2,1)S(1)}, u32[]{:S(2)}, u32[]{:S(2)}) collective-permute-start(bf16[128,512]{1,0:T(8,128)(2,1)S(1)} %attend.9), channel_id=1, source_target_pairs={{0,8},{8,0},{16,24},{24,16},{1,9},{9,1},{17,25},{25,17},{2,10},{10... | collective-permute-start | bytes 393224 | tf_op jit(solution)/shard_map/attend/ppermute | solution.py:389

commit v6 on v5

--- a/solution.py
+++ b/solution.py
@@ -106,20 +106,17 @@
     refs[-1][...] = total.astype(jnp.bfloat16)
 
 
-def last_add_kernel(count, keep_in, got_ref, *refs):
-    total = (keep_in[...] + got_ref[...].astype(jnp.float32)).astype(jnp.bfloat16)
-    out_ref, swap_ref = refs[-2:]
-    out_ref[...] = total
-    swap_ref[0] = total
-    for i in range(count):
-        block = refs[i][...][: NBS * TOKEN_ROWS]
-        rest = jnp.zeros((total.shape[0] - block.shape[0], LANES), jnp.bfloat16)
-        swap_ref[1 + i] = jnp.concatenate([block, rest], axis=0)
+def last_add_kernel(keep_in, got_ref, first_ref, out_ref):
+    out_ref[...] = (keep_in[...] + got_ref[...].astype(jnp.float32)).astype(jnp.bfloat16)
+
+
+def cut_kernel(block_ref, first_ref, out_ref):
+    out_ref[...] = block_ref[: NBS * TOKEN_ROWS]
 
 
 def pair_kernel(own_ref, swapped_ref, out_ref):
     out_ref[0] = own_ref[...]
-    out_ref[1] = swapped_ref[0]
+    out_ref[1] = swapped_ref[...]
 
 
 def gate_kernel(*refs):
@@ -215,8 +212,8 @@
 
 
 def pack_kernel(evens, feats, q_gain_ref, k_gain_ref, gram_ref, *refs):
-    here, near = refs[: len(evens)], refs[len(evens)]
-    x_t_ref, x_ref, key_mask_ref, gain_ref, *row_refs, rows_t = refs[len(evens) + 1 :]
+    here, near = refs[: len(evens)], refs[len(evens) : 2 * len(evens)]
+    x_t_ref, x_ref, key_mask_ref, gain_ref, *row_refs, rows_t = refs[2 * len(evens) :]
     n_enc = 2 * len(evens)
     mine = lax.axis_index("enc")
     rows = n_enc * BLOCK
@@ -224,7 +221,7 @@
     extra = lax.broadcasted_iota(jnp.int32, (APAD - feats, BLOCK), 0)
     found = []
     blocks = [(at, here[i][...]) for i, at in enumerate(evens)]
-    blocks += [(at ^ 1, near[1 + i]) for i, at in enumerate(evens)]
+    blocks += [(at ^ 1, near[i][...]) for i, at in enumerate(evens)]
     for distance, block in blocks:
         source = mine ^ distance
         for b in range(NBS):
@@ -470,43 +467,14 @@
     with jax.named_scope("gram"):
         gram = call(gram_kernel, vmem(1) + after(1), [jax.ShapeDtypeStruct((2 * feats, feats), bf16)])(embed, keep)[0]
 
-    with jax.named_scope("fold_sum"):
-        for bit in range(log2(heads), log2(n_seq)):
-            got = exchange(send, "seq", n_seq, 1 << bit)
-            if bit + 1 < log2(n_seq):
-                keep, send = add(keep, [got], own_block)
-            else:
-                fresh, swap = call(
-                    functools.partial(last_add_kernel, len(blocks)),
-                    vmem(2 + len(blocks)) + after(1),
-                    [folds(bf16), folds(bf16, 1 + len(blocks))],
-                )(keep, got, *blocks, gram)
-
-    partners = [(far, k) for far in evens for k in range(heads) if far or k]
-    partners.sort(key=lambda p: (p[0].bit_count() + p[1].bit_count(), p[0]))
-    near_count = min(3, len(partners))
-    half = (len(partners) - near_count) // 2
-    assert len(partners) == near_count + 2 * half
-    neighbours = tuple(partners[:near_count])
-    lists = (tuple(partners[near_count : near_count + half]), tuple(partners[near_count + half :]))
-
-    def spread(x, partner_of):
-        pairs = []
-        for e in range(n_enc):
-            far, k = partner_of[e & 1]
-            pairs += [(e * n_seq + i, (e ^ far) * n_seq + (i ^ k)) for i in range(n_seq)]
-        return lax.ppermute(x, ("enc", "seq"), pairs)
-
-    with jax.named_scope("gather"):
-        singles = [spread(fresh, (partner, partner)) for partner in neighbours]
-        swapped = exchange(swap, "enc", n_enc, 1)
-        pair = call(pair_kernel, vmem(2), [folds(bf16, 2)])(fresh, swapped)[0]
-        got = [spread(pair, partner_of) for partner_of in zip(*lists)]
-
     with jax.named_scope("pack"):
+        cut = jax.ShapeDtypeStruct((NBS * TOKEN_ROWS, BLOCK), bf16)
+        near_blocks = [
+            exchange(call(cut_kernel, vmem(1) + after(1), [cut])(block, keep)[0], "enc", n_enc, 1) for block in blocks
+        ]
         *shared, own_rows, own_mask, far_rows, far_mask = call(
             functools.partial(pack_kernel, tuple(evens), feats),
-            vmem(4 + len(evens)),
+            vmem(3 + 2 * len(evens)),
             [
                 jax.ShapeDtypeStruct((APAD, rows), bf16),
                 jax.ShapeDtypeStruct((rows, LANES), bf16),
@@ -515,7 +483,36 @@
             ]
             + [jax.ShapeDtypeStruct((BLOCK, LANES), bf16)] * 4,
             [pltpu.VMEM((LANES, rows), f32)],
-        )(q_gain, k_gain, gram, *blocks, swapped)
+        )(q_gain, k_gain, gram, *blocks, *near_blocks)
+
+    with jax.named_scope("fold_sum"):
+        for bit in range(log2(heads), log2(n_seq)):
+            got = exchange(send, "seq", n_seq, 1 << bit)
+            if bit + 1 < log2(n_seq):
+                keep, send = add(keep, [got], own_block)
+            else:
+                (fresh,) = call(last_add_kernel, vmem(2) + after(1), [folds(bf16)])(keep, got, own_rows)
+
+    partners = [(far, k) for far in evens for k in range(heads) if far or k]
+    partners.sort(key=lambda p: (p[0].bit_count() + p[1].bit_count(), p[0]))
+    near_count = min(3, len(partners))
+    half = (len(partners) - near_count) // 2
+    assert len(partners) == near_count + 2 * half
+    neighbours = tuple(partners[:near_count])
+    lists = (tuple(partners[near_count : near_count + half]), tuple(partners[near_count + half :]))
+
+    def spread(x, partner_of):
+        pairs = []
+        for e in range(n_enc):
+            far, k = partner_of[e & 1]
+            pairs += [(e * n_seq + i, (e ^ far) * n_seq + (i ^ k)) for i in range(n_seq)]
+        return lax.ppermute(x, ("enc", "seq"), pairs)
+
+    with jax.named_scope("gather"):
+        singles = [spread(fresh, (partner, partner)) for partner in neighbours]
+        swapped = exchange(fresh, "enc", n_enc, 1)
+        pair = call(pair_kernel, vmem(2), [folds(bf16, 2)])(fresh, swapped)[0]
+        got = [spread(pair, partner_of) for partner_of in zip(*lists)]
 
     def attend(rows_here, groups, first=()):
         count = sum(group.size for group in groups) // ((3 * feats + TAIL) * LANES)

time: 29.9 us -> 30.2 us (1.010)
    ppermute x8 -> x10, waiting for transfers between devices: 2.64 us -> 1.37 us  [exchange(): return lax.ppermute(x, axis, [(i, i ^ k) for i in range(n)])]
    ppermute x5, waiting for transfers between devices: 1.86 us -> 3.05 us  [spread(): return lax.ppermute(x, ('enc', 'seq'), pairs)]
    ppermute x8 -> x10, starting transfers between devices: 9.65 us -> 10 us  [exchange(): return lax.ppermute(x, axis, [(i, i ^ k) for i in range(n)])]
    pallas_call x2 -> x4, Pallas kernels: 0.77 us -> 0.77 us  [the longest x1 0.74 us: on_device(): call(functools.partial(pack_kernel, tuple(evens), feats), vmem(3 + 2 * le...]
  transfers between devices with their start and end apart: 13 -> 15, of which waited for: 5 -> 7; matrix products, arithmetic and copies ran while one was open for 0% -> 0% of each run, Pallas kernels for 22% -> 22%
where the time goes in v6:
time: 30.2 us; the launch traced here: 30 us
  starting transfers between devices  16.3 us (54%)
  Pallas kernels  9.17 us (30%)
  waiting for transfers between devices  4.42 us (15%)
    ppermute x10, starting transfers between devices, exchange(): return lax.ppermute(x, axis, [(i, i ^ k) for i in range(n)])  10 us
    ppermute x5, starting transfers between devices, spread(): return lax.ppermute(x, ('enc', 'seq'), pairs)  6.26 us
    pallas_call x4, Pallas kernels, attend(): call(functools.partial(attend_kernel, len(groups)), vmem(6 + len(groups))...  3.49 us
    ppermute x5, waiting for transfers between devices, spread(): return lax.ppermute(x, ('enc', 'seq'), pairs)  3.05 us
    pallas_call x1, Pallas kernels, on_device(): call(functools.partial(fold_kernel, len(later)), hbm(4 + len(later)), [ja...  1.75 us
    pallas_call x1, Pallas kernels, on_device(): call(functools.partial(encode_kernel, caps), hbm(2) + vmem(2), [jax.Shape...  1.72 us
    ppermute x10, waiting for transfers between devices, exchange(): return lax.ppermute(x, axis, [(i, i ^ k) for i in range(n)])  1.37 us
    pallas_call x1, Pallas kernels, on_device(): pl.pallas_call(functools.partial(output_kernel, heads, neighbours, lists)...  0.91 us
  transfers between devices with their start and end apart: 15, of which 7 were waited for; matrix products, arithmetic and copies ran while one was open for 0% of the time, Pallas kernels for 22%

profile of v6, /device:TPU:0, one launch (start us, length us, event | category | flops | bytes accessed | tf_op | source)
XLA Modules:
  0.0 30.0 jit_solution(9148555003090972054)
XLA Ops:
  0.0 1.8 %fold.1 = (bf16[64,2048]{1,0:T(8,128)(2,1)S(1)}, bf16[1024,512]{1,0:T(8,128)(2,1)S(1)}, bf16[432,512]{1,0:T(8,128)(2,1)S(1)}, f32[1,128]{1,0:T(1,128)S(1)}, f32[...) custom-call(bf16[64,2048]{1,0:T(8,128)(2,1)} %embed_hbm.1, ...), custom_call_target="tpu_custom_call" | custom-call | flops 200000000 | bytes 1000000 | tf_op jit(solution)/shard_map/fold/pallas_call | solution.py:425
  1.8 4.0 %collective-permute-start = (bf16[200,128]{1,0:T(8,128)(2,1)S(1)}, bf16[200,128]{1,0:T(8,128)(2,1)S(1)}, u32[]{:S(2)}, u32[]{:S(2)}) collective-permute-start(bf16[200,128]{1,0:T(8,128)(2,1)S(1)} %get-tuple-element.28), channel_id=1, source_target_pairs={{0,3},{1,2},{2,1},{3,0},{4,7},{5,6},{6,5},{7,4},{8,11},{9,10},{10,... | collective-permute-start | bytes 153608 | tf_op jit(solution)/shard_map/fold_sum/ppermute | solution.py:386
  5.8 0.4 %collective-permute-start.1 = (bf16[200,128]{1,0:T(8,128)(2,1)S(1)}, bf16[200,128]{1,0:T(8,128)(2,1)S(1)}, u32[]{:S(2)}, u32[]{:S(2)}) collective-permute-start(bf16[200,128]{1,0:T(8,128)(2,1)S(1)} %get-tuple-element.29), channel_id=1, source_target_pairs={{0,2},{1,3},{2,0},{3,1},{4,6},{5,7},{6,4},{7,5},{8,10},{9,11},{10,... | collective-permute-start | bytes 153608 | tf_op jit(solution)/shard_map/fold_sum/ppermute | solution.py:386
  6.4 1.7 %encode.1.refs_3_.block_ref.refs_0_ = bf16[208,128]{1,0:T(8,128)(2,1)S(1)} custom-call(s32[1,1,3]{2,1,0:T(1,128)} %shape_hbm.1, s32[1,1,2,2]{3,2,1,0:T(2,128)} %plan_hbm.1, bf16[1024,512]{1,0:T(8,128)(2,1)S(1)} %get-tuple-element.31.feat_ref, bf16[432,512]{1,0:T(8,128)(2,1)S(1)} %get-tuple-element.32.conv_ref), custom_call_target="tpu_custom_call" | custom-call | flops 500000000 | bytes 2000000 | tf_op jit(solution)/shard_map/encode/pallas_call | solution.py:441
  8.2 1.9 %collective-permute-start.3 = (bf16[208,128]{1,0:T(8,128)(2,1)S(1)}, bf16[208,128]{1,0:T(8,128)(2,1)S(1)}, u32[]{:S(2)}, u32[]{:S(2)}) collective-permute-start(bf16[208,128]{1,0:T(8,128)(2,1)S(1)} %encode.1.refs_3_.block_ref.refs_0_), channel_id=1, source_target_pairs={{0,16},{8,24},{16,0},{24,8},{1,17},{9,25},{17,1},{25,9},{2,18},{10... | collective-permute-start | bytes 159752 | tf_op jit(solution)/shard_map/tokens/ppermute | solution.py:386
  10.1 0.3 collective-permute-done.2.refs_2_
  10.4 2.7 %collective-permute-start.6 = (bf16[200,128]{1,0:T(8,128)(2,1)S(1)}, bf16[200,128]{1,0:T(8,128)(2,1)S(1)}, u32[]{:S(2)}, u32[]{:S(2)}) collective-permute-start(bf16[200,128]{1,0:T(8,128)(2,1)S(1)} %get-tuple-element.40), channel_id=1, source_target_pairs={{0,4},{1,5},{2,6},{3,7},{4,0},{5,1},{6,2},{7,3},{8,12},{9,13},{10,... | collective-permute-start | bytes 153608 | tf_op jit(solution)/shard_map/fold_sum/ppermute | solution.py:386
  13.1 0.5 %collective-permute-start.5 = (bf16[160,128]{1,0:T(8,128)(2,1)S(1)}, bf16[160,128]{1,0:T(8,128)(2,1)S(1)}, u32[]{:S(2)}, u32[]{:S(2)}) collective-permute-start(bf16[160,128]{1,0:T(8,128)(2,1)S(1)} %pack.4), channel_id=1, source_target_pairs={{0,8},{8,0},{16,24},{24,16},{1,9},{9,1},{17,25},{25,17},{2,10},{10... | collective-permute-start | bytes 122888 | tf_op jit(solution)/shard_map/pack/ppermute | solution.py:386
  13.6 0.5 %gram.1.gram_ref = bf16[128,64]{1,0:T(8,128)(2,1)S(1)} custom-call(bf16[64,2048]{1,0:T(8,128)(2,1)S(1)} %get-tuple-element.26.embed_ref, f32[200,128]{1,0:T(8,128)S(1)} %get-tuple-element.33.first_ref.keep_in), custom_call_target="tpu_custom_call" | custom-call | flops 1000000 | bytes 1000000 | tf_op jit(solution)/shard_map/gram/pallas_call | solution.py:468
  14.4 0.7 %pack.5 = (bf16[72,512]{1,0:T(8,128)(2,1)S(1)}, bf16[512,128]{1,0:T(8,128)(2,1)S(1)}, bf16[128,512]{1,0:T(8,128)(2,1)S(1)}, f32[1,128]{1,0:T(1,128)S(1)}, bf16[1...) custom-call(f32[1,128]{1,0:T(1,128)S(1)} %get-tuple-element.24.q_gai, ...), custom_call_target="tpu_custom_call" | custom-call | flops 1000000 | bytes 1000000 | tf_op jit(solution)/shard_map/pack/pallas_call | solution.py:475
  15.2 0.3 collective-permute-done.6.got_ref
  15.6 1.5 %collective-permute-start.9 = (bf16[200,128]{1,0:T(8,128)(2,1)S(1)}, bf16[200,128]{1,0:T(8,128)(2,1)S(1)}, u32[]{:S(2)}, u32[]{:S(2)}) collective-permute-start(bf16[200,128]{1,0:T(8,128)(2,1)S(1)} %fold_sum.3.refs_6_.own_ref), channel_id=1, source_target_pairs={{0,16},{1,17},{2,18},{3,19},{4,20},{5,21},{6,22},{7,23},{8,24},{9,... | collective-permute-start | bytes 153608 | tf_op jit(solution)/shard_map/gather/ppermute | solution.py:509
  17.1 1.6 %collective-permute-start.8 = (bf16[200,128]{1,0:T(8,128)(2,1)S(1)}, bf16[200,128]{1,0:T(8,128)(2,1)S(1)}, u32[]{:S(2)}, u32[]{:S(2)}) collective-permute-start(bf16[200,128]{1,0:T(8,128)(2,1)S(1)} %fold_sum.3.refs_6_.own_ref), channel_id=1, source_target_pairs={{0,2},{1,3},{2,0},{3,1},{4,6},{5,7},{6,4},{7,5},{8,10},{9,11},{10,... | collective-permute-start | bytes 153608 | tf_op jit(solution)/shard_map/gather/ppermute | solution.py:509
  18.7 0.8 %collective-permute-start.7 = (bf16[200,128]{1,0:T(8,128)(2,1)S(1)}, bf16[200,128]{1,0:T(8,128)(2,1)S(1)}, u32[]{:S(2)}, u32[]{:S(2)}) collective-permute-start(bf16[200,128]{1,0:T(8,128)(2,1)S(1)} %fold_sum.3.refs_6_.own_ref), channel_id=1, source_target_pairs={{0,1},{1,0},{2,3},{3,2},{4,5},{5,4},{6,7},{7,6},{8,9},{9,8},{10,11... | collective-permute-start | bytes 153608 | tf_op jit(solution)/shard_map/gather/ppermute | solution.py:509
  19.5 1.2 %collective-permute-start.13 = (bf16[2,200,128]{2,1,0:T(8,128)(2,1)S(1)}, bf16[2,200,128]{2,1,0:T(8,128)(2,1)S(1)}, u32[]{:S(2)}, u32[]{:S(2)}) collective-permute-start(bf16[2,200,128]{2,1,0:T(8,128)(2,1)S(1)} %gather.1), channel_id=1, source_target_pairs={{0,17},{1,16},{2,19},{3,18},{4,21},{5,20},{6,23},{7,22},{8,27},{9,... | collective-permute-start | bytes 307208 | tf_op jit(solution)/shard_map/gather/ppermute | solution.py:509
  20.8 1.1 %collective-permute-start.12 = (bf16[2,200,128]{2,1,0:T(8,128)(2,1)S(1)}, bf16[2,200,128]{2,1,0:T(8,128)(2,1)S(1)}, u32[]{:S(2)}, u32[]{:S(2)}) collective-permute-start(bf16[2,200,128]{2,1,0:T(8,128)(2,1)S(1)} %gather.1), channel_id=1, source_target_pairs={{0,3},{1,2},{2,1},{3,0},{4,7},{5,6},{6,5},{7,4},{8,26},{9,27},{10,... | collective-permute-start | bytes 307208 | tf_op jit(solution)/shard_map/gather/ppermute | solution.py:509
  21.9 0.9 %collective-permute-done.7.refs_7_ = bf16[200,128]{1,0:T(8,128)(2,1)S(1)} collective-permute-done((bf16[200,128]{1,0:T(8,128)(2,1)S(1)}, bf16[200,128]{1,0:T(8,128)(2,1)S(1)}, u32[]{:S(2)}, u32[]{:S(2)}) %collective-permute-start.7) | collective-permute-done | bytes 51232 | tf_op jit(solution)/shard_map/gather/ppermute | solution.py:509
  22.8 0.9 %attend.6.refs_10_.refs_0_ = bf16[128,512]{1,0:T(8,128)(2,1)S(1)} custom-call(bf16[72,512]{1,0:T(8,128)(2,1)S(1)} %get-tuple-element.34.refs_0_, bf16[512,128]{1,0:T(8,128)(2,1)S(1)} %get-tuple-element.35.refs_1_, bf16[128,512]{1,0:T(8,128)(2,1)S(1)} %get-tuple-element.36.refs_2_, f32[1,128]{1,0:T(1,128)S(1)} %get-tuple-element.37.refs_3_, ...), custom_call_target="tpu_custom_call" | custom-call | flops 800000000 | bytes 1000000 | tf_op jit(solution)/shard_map/attend/pallas_call | solution.py:519
  23.7 0.9 %attend.7.refs_1_.refs_8_.own_early_ref = bf16[128,512]{1,0:T(8,128)(2,1)S(1)} custom-call(bf16[72,512]{1,0:T(8,128)(2,1)S(1)} %get-tuple-element.34.refs_0_, bf16[512,128]{1,0:T(8,128)(2,1)S(1)} %get-tuple-element.35.refs_1_, bf16[128,512]{1,0:T(8,128)(2,1)S(1)} %get-tuple-element.36.refs_2_, f32[1,128]{1,0:T(1,128)S(1)} %get-tuple-element.37.refs_3_, ...), custom_call_target="tpu_custom_call" | custom-call | flops 800000000 | bytes 1000000 | tf_op jit(solution)/shard_map/attend/pallas_call | solution.py:519
  24.7 2.1 %collective-permute-done.13.refs_7_ = bf16[2,200,128]{2,1,0:T(8,128)(2,1)S(1)} collective-permute-done((bf16[2,200,128]{2,1,0:T(8,128)(2,1)S(1)}, bf16[2,200,128]{2,1,0:T(8,128)(2,1)S(1)}, u32[]{:S(2)}, u32[]{:S(2)}) %collective-permute-start.13) | collective-permute-done | bytes 102432 | tf_op jit(solution)/shard_map/gather/ppermute | solution.py:509
  26.8 0.9 %attend.9 = bf16[128,512]{1,0:T(8,128)(2,1)S(1)} custom-call(bf16[72,512]{1,0:T(8,128)(2,1)S(1)} %get-tuple-element.34.refs_0_, bf16[512,128]{1,0:T(8,128)(2,1)S(1)} %get-tuple-element.35.refs_1_, bf16[128,512]{1,0:T(8,128)(2,1)S(1)} %get-tuple-element.36.refs_2_, f32[1,128]{1,0:T(1,128)S(1)} %get-tuple-element.37.refs_3_, ...), custom_call_target="tpu_custom_call" | custom-call | flops 800000000 | bytes 1000000 | tf_op jit(solution)/shard_map/attend/pallas_call | solution.py:519
  27.8 0.9 %attend.10.own_rest_ref = bf16[128,512]{1,0:T(8,128)(2,1)S(1)} custom-call(bf16[72,512]{1,0:T(8,128)(2,1)S(1)} %get-tuple-element.34.refs_0_, bf16[512,128]{1,0:T(8,128)(2,1)S(1)} %get-tuple-element.35.refs_1_, bf16[128,512]{1,0:T(8,128)(2,1)S(1)} %get-tuple-element.36.refs_2_, f32[1,128]{1,0:T(1,128)S(1)} %get-tuple-element.37.refs_3_, ...), custom_call_target="tpu_custom_call" | custom-call | flops 800000000 | bytes 1000000 | tf_op jit(solution)/shard_map/attend/pallas_call | solution.py:519
  28.6 0.4 %collective-permute-done.14.near_rest_ref = bf16[128,512]{1,0:T(8,128)(2,1)S(1)} collective-permute-done((bf16[128,512]{1,0:T(8,128)(2,1)S(1)}, bf16[128,512]{1,0:T(8,128)(2,1)S(1)}, u32[]{:S(2)}, u32[]{:S(2)}) %collective-permute-start.14) | collective-permute-done | bytes 131104 | tf_op jit(solution)/shard_map/attend/ppermute | solution.py:386
  29.1 0.9 %attend.11 = bf16[1,128,2048]{2,1,0:T(8,128)(2,1)} custom-call(bf16[128,512]{1,0:T(8,128)(2,1)S(1)} %collective-permute-done.10.near_early_ref, bf16[128,512]{1,0:T(8,128)(2,1)S(1)} %collective-permute-done.14.near_rest_ref, bf16[128,512]{1,0:T(8,128)(2,1)S(1)} %attend.7.refs_1_.refs_8_.own_early_ref, bf16[128,512]{1,0:T(8,128)(2,1)S(1)} %attend.10.own_rest_ref), custom_call_target="tpu_custom_call" | custom-call | tf_op jit(solution)/shard_map/attend/pallas_call | solution.py:534
  (21 shorter events, 1.0 us)
Async XLA Ops:
  1.8 8.3 %collective-permute-start = (bf16[200,128]{1,0:T(8,128)(2,1)S(1)}, bf16[200,128]{1,0:T(8,128)(2,1)S(1)}, u32[]{:S(2)}, u32[]{:S(2)}) collective-permute-start(bf16[200,128]{1,0:T(8,128)(2,1)S(1)} %get-tuple-element.28), channel_id=1, source_target_pairs={{0,3},{1,2},{2,1},{3,0},{4,7},{5,6},{6,5},{7,4},{8,11},{9,10},{10,... | collective-permute-start | bytes 153608 | tf_op jit(solution)/shard_map/fold_sum/ppermute | solution.py:386
  5.8 4.3 %collective-permute-start.1 = (bf16[200,128]{1,0:T(8,128)(2,1)S(1)}, bf16[200,128]{1,0:T(8,128)(2,1)S(1)}, u32[]{:S(2)}, u32[]{:S(2)}) collective-permute-start(bf16[200,128]{1,0:T(8,128)(2,1)S(1)} %get-tuple-element.29), channel_id=1, source_target_pairs={{0,2},{1,3},{2,0},{3,1},{4,6},{5,7},{6,4},{7,5},{8,10},{9,11},{10,... | collective-permute-start | bytes 153608 | tf_op jit(solution)/shard_map/fold_sum/ppermute | solution.py:386
  6.2 4.1 %collective-permute-start.2 = (bf16[200,128]{1,0:T(8,128)(2,1)S(1)}, bf16[200,128]{1,0:T(8,128)(2,1)S(1)}, u32[]{:S(2)}, u32[]{:S(2)}) collective-permute-start(bf16[200,128]{1,0:T(8,128)(2,1)S(1)} %get-tuple-element.30), channel_id=1, source_target_pairs={{0,1},{1,0},{2,3},{3,2},{4,5},{5,4},{6,7},{7,6},{8,9},{9,8},{10,11... | collective-permute-start | bytes 153608 | tf_op jit(solution)/shard_map/fold_sum/ppermute | solution.py:386
  8.2 4.9 %collective-permute-start.3 = (bf16[208,128]{1,0:T(8,128)(2,1)S(1)}, bf16[208,128]{1,0:T(8,128)(2,1)S(1)}, u32[]{:S(2)}, u32[]{:S(2)}) collective-permute-start(bf16[208,128]{1,0:T(8,128)(2,1)S(1)} %encode.1.refs_3_.block_ref.refs_0_), channel_id=1, source_target_pairs={{0,16},{8,24},{16,0},{24,8},{1,17},{9,25},{17,1},{25,9},{2,18},{10... | collective-permute-start | bytes 159752 | tf_op jit(solution)/shard_map/tokens/ppermute | solution.py:386
  10.4 5.1 %collective-permute-start.6 = (bf16[200,128]{1,0:T(8,128)(2,1)S(1)}, bf16[200,128]{1,0:T(8,128)(2,1)S(1)}, u32[]{:S(2)}, u32[]{:S(2)}) collective-permute-start(bf16[200,128]{1,0:T(8,128)(2,1)S(1)} %get-tuple-element.40), channel_id=1, source_target_pairs={{0,4},{1,5},{2,6},{3,7},{4,0},{5,1},{6,2},{7,3},{8,12},{9,13},{10,... | collective-permute-start | bytes 153608 | tf_op jit(solution)/shard_map/fold_sum/ppermute | solution.py:386
  13.0 1.2 %collective-permute-start.4 = (bf16[160,128]{1,0:T(8,128)(2,1)S(1)}, bf16[160,128]{1,0:T(8,128)(2,1)S(1)}, u32[]{:S(2)}, u32[]{:S(2)}) collective-permute-start(bf16[160,128]{1,0:T(8,128)(2,1)S(1)} %pack.3), channel_id=1, source_target_pairs={{0,8},{8,0},{16,24},{24,16},{1,9},{9,1},{17,25},{25,17},{2,10},{10... | collective-permute-start | bytes 122888 | tf_op jit(solution)/shard_map/pack/ppermute | solution.py:386
  13.1 1.4 %collective-permute-start.5 = (bf16[160,128]{1,0:T(8,128)(2,1)S(1)}, bf16[160,128]{1,0:T(8,128)(2,1)S(1)}, u32[]{:S(2)}, u32[]{:S(2)}) collective-permute-start(bf16[160,128]{1,0:T(8,128)(2,1)S(1)} %pack.4), channel_id=1, source_target_pairs={{0,8},{8,0},{16,24},{24,16},{1,9},{9,1},{17,25},{25,17},{2,10},{10... | collective-permute-start | bytes 122888 | tf_op jit(solution)/shard_map/pack/ppermute | solution.py:386
  15.5 4.1 %collective-permute-start.11 = (bf16[200,128]{1,0:T(8,128)(2,1)S(1)}, bf16[200,128]{1,0:T(8,128)(2,1)S(1)}, u32[]{:S(2)}, u32[]{:S(2)}) collective-permute-start(bf16[200,128]{1,0:T(8,128)(2,1)S(1)} %fold_sum.3.refs_6_.own_ref), channel_id=1, source_target_pairs={{0,8},{8,0},{16,24},{24,16},{1,9},{9,1},{17,25},{25,17},{2,10},{10... | collective-permute-start | bytes 153608 | tf_op jit(solution)/shard_map/gather/ppermute | solution.py:386
  15.6 6.3 %collective-permute-start.9 = (bf16[200,128]{1,0:T(8,128)(2,1)S(1)}, bf16[200,128]{1,0:T(8,128)(2,1)S(1)}, u32[]{:S(2)}, u32[]{:S(2)}) collective-permute-start(bf16[200,128]{1,0:T(8,128)(2,1)S(1)} %fold_sum.3.refs_6_.own_ref), channel_id=1, source_target_pairs={{0,16},{1,17},{2,18},{3,19},{4,20},{5,21},{6,22},{7,23},{8,24},{9,... | collective-permute-start | bytes 153608 | tf_op jit(solution)/shard_map/gather/ppermute | solution.py:509
  17.1 4.8 %collective-permute-start.8 = (bf16[200,128]{1,0:T(8,128)(2,1)S(1)}, bf16[200,128]{1,0:T(8,128)(2,1)S(1)}, u32[]{:S(2)}, u32[]{:S(2)}) collective-permute-start(bf16[200,128]{1,0:T(8,128)(2,1)S(1)} %fold_sum.3.refs_6_.own_ref), channel_id=1, source_target_pairs={{0,2},{1,3},{2,0},{3,1},{4,6},{5,7},{6,4},{7,5},{8,10},{9,11},{10,... | collective-permute-start | bytes 153608 | tf_op jit(solution)/shard_map/gather/ppermute | solution.py:509
  18.7 4.1 %collective-permute-start.7 = (bf16[200,128]{1,0:T(8,128)(2,1)S(1)}, bf16[200,128]{1,0:T(8,128)(2,1)S(1)}, u32[]{:S(2)}, u32[]{:S(2)}) collective-permute-start(bf16[200,128]{1,0:T(8,128)(2,1)S(1)} %fold_sum.3.refs_6_.own_ref), channel_id=1, source_target_pairs={{0,1},{1,0},{2,3},{3,2},{4,5},{5,4},{6,7},{7,6},{8,9},{9,8},{10,11... | collective-permute-start | bytes 153608 | tf_op jit(solution)/shard_map/gather/ppermute | solution.py:509
  19.5 7.3 %collective-permute-start.13 = (bf16[2,200,128]{2,1,0:T(8,128)(2,1)S(1)}, bf16[2,200,128]{2,1,0:T(8,128)(2,1)S(1)}, u32[]{:S(2)}, u32[]{:S(2)}) collective-permute-start(bf16[2,200,128]{2,1,0:T(8,128)(2,1)S(1)} %gather.1), channel_id=1, source_target_pairs={{0,17},{1,16},{2,19},{3,18},{4,21},{5,20},{6,23},{7,22},{8,27},{9,... | collective-permute-start | bytes 307208 | tf_op jit(solution)/shard_map/gather/ppermute | solution.py:509
  20.8 6.0 %collective-permute-start.12 = (bf16[2,200,128]{2,1,0:T(8,128)(2,1)S(1)}, bf16[2,200,128]{2,1,0:T(8,128)(2,1)S(1)}, u32[]{:S(2)}, u32[]{:S(2)}) collective-permute-start(bf16[2,200,128]{2,1,0:T(8,128)(2,1)S(1)} %gather.1), channel_id=1, source_target_pairs={{0,3},{1,2},{2,1},{3,0},{4,7},{5,6},{6,5},{7,4},{8,26},{9,27},{10,... | collective-permute-start | bytes 307208 | tf_op jit(solution)/shard_map/gather/ppermute | solution.py:509
  24.6 4.0 %collective-permute-start.10 = (bf16[128,512]{1,0:T(8,128)(2,1)S(1)}, bf16[128,512]{1,0:T(8,128)(2,1)S(1)}, u32[]{:S(2)}, u32[]{:S(2)}) collective-permute-start(bf16[128,512]{1,0:T(8,128)(2,1)S(1)} %attend.8), channel_id=1, source_target_pairs={{0,8},{8,0},{16,24},{24,16},{1,9},{9,1},{17,25},{25,17},{2,10},{10... | collective-permute-start | bytes 393224 | tf_op jit(solution)/shard_map/attend/ppermute | solution.py:386
  27.7 1.4 %collective-permute-start.14 = (bf16[128,512]{1,0:T(8,128)(2,1)S(1)}, bf16[128,512]{1,0:T(8,128)(2,1)S(1)}, u32[]{:S(2)}, u32[]{:S(2)}) collective-permute-start(bf16[128,512]{1,0:T(8,128)(2,1)S(1)} %attend.9), channel_id=1, source_target_pairs={{0,8},{8,0},{16,24},{24,16},{1,9},{9,1},{17,25},{25,17},{2,10},{10... | collective-permute-start | bytes 393224 | tf_op jit(solution)/shard_map/attend/ppermute | solution.py:386

commit v7 on v6

--- a/solution.py
+++ b/solution.py
@@ -318,7 +318,8 @@
     attend_heads(each_head(folds), place, *refs[:6])
 
 
-def output_kernel(heads, neighbours, lists, near_early_ref, near_rest_ref, own_early_ref, own_rest_ref, out_ref, sems):
+def output_kernel(heads, neighbours, lists, kinds, *refs):
+    out_ref, sems = refs[-2:]
     mine, slot = lax.axis_index("enc"), lax.axis_index("seq") & (heads - 1)
     copies = []
 
@@ -329,16 +330,16 @@
         copies.append(pltpu.make_async_copy(result, out_ref.at[0, :, column], sems.at[len(copies)]))
         copies[-1].start()
 
-    for early, rest, base in (
-        (near_early_ref, near_rest_ref, mine ^ 1),
-        (own_early_ref, own_rest_ref, mine),
-    ):
-        for at, partner in enumerate(((0, 0), *neighbours)):
-            put(early, at, base, *partner)
-        for i, pair in enumerate(zip(*lists)):
-            far, k = (jnp.where(base & 1 == 0, zero, one) for zero, one in zip(*pair))
-            put(rest, 2 * i, base, far, k)
-            put(rest, 2 * i + 1, base, far ^ 1, k)
+    for ref, (other, early) in zip(refs, kinds):
+        base = mine ^ other
+        if early:
+            for at, partner in enumerate(((0, 0), *neighbours)):
+                put(ref, at, base, *partner)
+        else:
+            for i, pair in enumerate(zip(*lists)):
+                far, k = (jnp.where(base & 1 == 0, zero, one) for zero, one in zip(*pair))
+                put(ref, 2 * i, base, far, k)
+                put(ref, 2 * i + 1, base, far ^ 1, k)
     for copy in copies:
         copy.wait()
 
@@ -523,22 +524,28 @@
             cost=(count * 200_000_000, 1_000_000),
         )(*shared, *rows_here, *groups, *first)[0]
 
+    def write(kinds, results, out):
+        olds = [] if out is None else [in_hbm(out)]
+        return pl.pallas_call(
+            functools.partial(output_kernel, heads, neighbours, lists, kinds),
+            in_specs=vmem(len(results)) + hbm(len(olds)),
+            out_specs=hbm(1)[0],
+            out_shape=jax.ShapeDtypeStruct((1, BLOCK, n_enc * cols), bf16),
+            scratch_shapes=[pltpu.SemaphoreType.DMA((n_enc * heads,))],
+            input_output_aliases={len(results): 0} if olds else {},
+            compiler_params=pltpu.CompilerParams(vmem_limit_bytes=VMEM_LIMIT),
+        )(*results, *olds)
+
     with jax.named_scope("attend"):
         own, other = (own_rows, own_mask), (far_rows, far_mask)
         early, rest = [fresh, *singles], got
         early_other = attend(other, early)
         early_own = attend(own, early, [early_other])
         near_early = exchange(gate(early_other, early_own), "enc", n_enc, 1)
-        near_rest = exchange(attend(other, rest, [early_own]), "enc", n_enc, 1)
+        out = write(((0, 1),), (early_own,), None)
+        near_rest = exchange(attend(other, rest, [in_hbm(out)]), "enc", n_enc, 1)
         rest_own = attend(own, rest)
-        return pl.pallas_call(
-            functools.partial(output_kernel, heads, neighbours, lists),
-            in_specs=vmem(4),
-            out_specs=hbm(1)[0],
-            out_shape=jax.ShapeDtypeStruct((1, BLOCK, n_enc * cols), bf16),
-            scratch_shapes=[pltpu.SemaphoreType.DMA((n_enc * heads,))],
-            compiler_params=pltpu.CompilerParams(vmem_limit_bytes=VMEM_LIMIT),
-        )(near_early, near_rest, early_own, rest_own)
+        return write(((1, 1), (1, 0), (0, 0)), (near_early, near_rest, rest_own), out)
 
 
 def solution(mesh):

time: 30.2 us -> 30.1 us (level)
  waiting for transfers between devices: 4.42 us -> 3.64 us
  Pallas kernels: 9.17 us -> 9.89 us
    ppermute x5, waiting for transfers between devices: 3.05 us -> 2.26 us  [spread(): return lax.ppermute(x, ('enc', 'seq'), pairs)]
    pallas_call x1 -> x2, Pallas kernels: 0.91 us -> 1.67 us  [write(): pl.pallas_call(functools.partial(output_kernel, heads, neighbours, lists,...]
  transfers between devices with their start and end apart: 15 -> 15, of which waited for: 7 -> 7; matrix products, arithmetic and copies ran while one was open for 0% -> 0% of each run, Pallas kernels for 22% -> 24%
where the time goes in v7:
time: 30.1 us; the launch traced here: 30 us
  starting transfers between devices  16.3 us (54%)
  Pallas kernels  9.89 us (33%)
  waiting for transfers between devices  3.64 us (12%)
    ppermute x10, starting transfers between devices, exchange(): return lax.ppermute(x, axis, [(i, i ^ k) for i in range(n)])  10 us
    ppermute x5, starting transfers between devices, spread(): return lax.ppermute(x, ('enc', 'seq'), pairs)  6.26 us
    pallas_call x4, Pallas kernels, attend(): call(functools.partial(attend_kernel, len(groups)), vmem(6 + len(groups))...  3.45 us
    ppermute x5, waiting for transfers between devices, spread(): return lax.ppermute(x, ('enc', 'seq'), pairs)  2.26 us
    pallas_call x1, Pallas kernels, on_device(): call(functools.partial(fold_kernel, len(later)), hbm(4 + len(later)), [ja...  1.75 us
    pallas_call x1, Pallas kernels, on_device(): call(functools.partial(encode_kernel, caps), hbm(2) + vmem(2), [jax.Shape...  1.72 us
    pallas_call x2, Pallas kernels, write(): pl.pallas_call(functools.partial(output_kernel, heads, neighbours, lists,...  1.67 us
    ppermute x10, waiting for transfers between devices, exchange(): return lax.ppermute(x, axis, [(i, i ^ k) for i in range(n)])  1.38 us
  transfers between devices with their start and end apart: 15, of which 7 were waited for; matrix products, arithmetic and copies ran while one was open for 0% of the time, Pallas kernels for 24%

profile of v7, /device:TPU:0, one launch (start us, length us, event | category | flops | bytes accessed | tf_op | source)
XLA Modules:
  0.0 30.0 jit_solution(1185559378960244378)
XLA Ops:
  0.0 1.8 %fold.1 = (bf16[64,2048]{1,0:T(8,128)(2,1)S(1)}, bf16[1024,512]{1,0:T(8,128)(2,1)S(1)}, bf16[432,512]{1,0:T(8,128)(2,1)S(1)}, f32[1,128]{1,0:T(1,128)S(1)}, f32[...) custom-call(bf16[64,2048]{1,0:T(8,128)(2,1)} %embed_hbm.1, ...), custom_call_target="tpu_custom_call" | custom-call | flops 200000000 | bytes 1000000 | tf_op jit(solution)/shard_map/fold/pallas_call | solution.py:426
  1.8 4.0 %collective-permute-start = (bf16[200,128]{1,0:T(8,128)(2,1)S(1)}, bf16[200,128]{1,0:T(8,128)(2,1)S(1)}, u32[]{:S(2)}, u32[]{:S(2)}) collective-permute-start(bf16[200,128]{1,0:T(8,128)(2,1)S(1)} %get-tuple-element.28), channel_id=1, source_target_pairs={{0,3},{1,2},{2,1},{3,0},{4,7},{5,6},{6,5},{7,4},{8,11},{9,10},{10,... | collective-permute-start | bytes 153608 | tf_op jit(solution)/shard_map/fold_sum/ppermute | solution.py:387
  5.8 0.4 %collective-permute-start.1 = (bf16[200,128]{1,0:T(8,128)(2,1)S(1)}, bf16[200,128]{1,0:T(8,128)(2,1)S(1)}, u32[]{:S(2)}, u32[]{:S(2)}) collective-permute-start(bf16[200,128]{1,0:T(8,128)(2,1)S(1)} %get-tuple-element.29), channel_id=1, source_target_pairs={{0,2},{1,3},{2,0},{3,1},{4,6},{5,7},{6,4},{7,5},{8,10},{9,11},{10,... | collective-permute-start | bytes 153608 | tf_op jit(solution)/shard_map/fold_sum/ppermute | solution.py:387
  6.4 1.7 %encode.1.refs_3_.block_ref.refs_0_ = bf16[208,128]{1,0:T(8,128)(2,1)S(1)} custom-call(s32[1,1,3]{2,1,0:T(1,128)} %shape_hbm.1, s32[1,1,2,2]{3,2,1,0:T(2,128)} %plan_hbm.1, bf16[1024,512]{1,0:T(8,128)(2,1)S(1)} %get-tuple-element.31.feat_ref, bf16[432,512]{1,0:T(8,128)(2,1)S(1)} %get-tuple-element.32.conv_ref), custom_call_target="tpu_custom_call" | custom-call | flops 500000000 | bytes 2000000 | tf_op jit(solution)/shard_map/encode/pallas_call | solution.py:442
  8.2 1.9 %collective-permute-start.3 = (bf16[208,128]{1,0:T(8,128)(2,1)S(1)}, bf16[208,128]{1,0:T(8,128)(2,1)S(1)}, u32[]{:S(2)}, u32[]{:S(2)}) collective-permute-start(bf16[208,128]{1,0:T(8,128)(2,1)S(1)} %encode.1.refs_3_.block_ref.refs_0_), channel_id=1, source_target_pairs={{0,16},{8,24},{16,0},{24,8},{1,17},{9,25},{17,1},{25,9},{2,18},{10... | collective-permute-start | bytes 159752 | tf_op jit(solution)/shard_map/tokens/ppermute | solution.py:387
  10.4 2.7 %collective-permute-start.6 = (bf16[200,128]{1,0:T(8,128)(2,1)S(1)}, bf16[200,128]{1,0:T(8,128)(2,1)S(1)}, u32[]{:S(2)}, u32[]{:S(2)}) collective-permute-start(bf16[200,128]{1,0:T(8,128)(2,1)S(1)} %get-tuple-element.40), channel_id=1, source_target_pairs={{0,4},{1,5},{2,6},{3,7},{4,0},{5,1},{6,2},{7,3},{8,12},{9,13},{10,... | collective-permute-start | bytes 153608 | tf_op jit(solution)/shard_map/fold_sum/ppermute | solution.py:387
  13.1 0.5 %collective-permute-start.5 = (bf16[160,128]{1,0:T(8,128)(2,1)S(1)}, bf16[160,128]{1,0:T(8,128)(2,1)S(1)}, u32[]{:S(2)}, u32[]{:S(2)}) collective-permute-start(bf16[160,128]{1,0:T(8,128)(2,1)S(1)} %pack.4), channel_id=1, source_target_pairs={{0,8},{8,0},{16,24},{24,16},{1,9},{9,1},{17,25},{25,17},{2,10},{10... | collective-permute-start | bytes 122888 | tf_op jit(solution)/shard_map/pack/ppermute | solution.py:387
  13.6 0.5 %gram.1.gram_ref = bf16[128,64]{1,0:T(8,128)(2,1)S(1)} custom-call(bf16[64,2048]{1,0:T(8,128)(2,1)S(1)} %get-tuple-element.26.embed_ref, f32[200,128]{1,0:T(8,128)S(1)} %get-tuple-element.33.first_ref.keep_in), custom_call_target="tpu_custom_call" | custom-call | flops 1000000 | bytes 1000000 | tf_op jit(solution)/shard_map/gram/pallas_call | solution.py:469
  14.4 0.7 %pack.5 = (bf16[72,512]{1,0:T(8,128)(2,1)S(1)}, bf16[512,128]{1,0:T(8,128)(2,1)S(1)}, bf16[128,512]{1,0:T(8,128)(2,1)S(1)}, f32[1,128]{1,0:T(1,128)S(1)}, bf16[1...) custom-call(f32[1,128]{1,0:T(1,128)S(1)} %get-tuple-element.24.q_gai, ...), custom_call_target="tpu_custom_call" | custom-call | flops 1000000 | bytes 1000000 | tf_op jit(solution)/shard_map/pack/pallas_call | solution.py:476
  15.2 0.3 collective-permute-done.6.got_ref
  15.6 1.5 %collective-permute-start.9 = (bf16[200,128]{1,0:T(8,128)(2,1)S(1)}, bf16[200,128]{1,0:T(8,128)(2,1)S(1)}, u32[]{:S(2)}, u32[]{:S(2)}) collective-permute-start(bf16[200,128]{1,0:T(8,128)(2,1)S(1)} %fold_sum.3.refs_6_.own_ref), channel_id=1, source_target_pairs={{0,16},{1,17},{2,18},{3,19},{4,20},{5,21},{6,22},{7,23},{8,24},{9,... | collective-permute-start | bytes 153608 | tf_op jit(solution)/shard_map/gather/ppermute | solution.py:510
  17.1 1.6 %collective-permute-start.8 = (bf16[200,128]{1,0:T(8,128)(2,1)S(1)}, bf16[200,128]{1,0:T(8,128)(2,1)S(1)}, u32[]{:S(2)}, u32[]{:S(2)}) collective-permute-start(bf16[200,128]{1,0:T(8,128)(2,1)S(1)} %fold_sum.3.refs_6_.own_ref), channel_id=1, source_target_pairs={{0,2},{1,3},{2,0},{3,1},{4,6},{5,7},{6,4},{7,5},{8,10},{9,11},{10,... | collective-permute-start | bytes 153608 | tf_op jit(solution)/shard_map/gather/ppermute | solution.py:510
  18.7 0.8 %collective-permute-start.7 = (bf16[200,128]{1,0:T(8,128)(2,1)S(1)}, bf16[200,128]{1,0:T(8,128)(2,1)S(1)}, u32[]{:S(2)}, u32[]{:S(2)}) collective-permute-start(bf16[200,128]{1,0:T(8,128)(2,1)S(1)} %fold_sum.3.refs_6_.own_ref), channel_id=1, source_target_pairs={{0,1},{1,0},{2,3},{3,2},{4,5},{5,4},{6,7},{7,6},{8,9},{9,8},{10,11... | collective-permute-start | bytes 153608 | tf_op jit(solution)/shard_map/gather/ppermute | solution.py:510
  19.5 1.2 %collective-permute-start.13 = (bf16[2,200,128]{2,1,0:T(8,128)(2,1)S(1)}, bf16[2,200,128]{2,1,0:T(8,128)(2,1)S(1)}, u32[]{:S(2)}, u32[]{:S(2)}) collective-permute-start(bf16[2,200,128]{2,1,0:T(8,128)(2,1)S(1)} %gather.1), channel_id=1, source_target_pairs={{0,17},{1,16},{2,19},{3,18},{4,21},{5,20},{6,23},{7,22},{8,27},{9,... | collective-permute-start | bytes 307208 | tf_op jit(solution)/shard_map/gather/ppermute | solution.py:510
  20.8 1.1 %collective-permute-start.12 = (bf16[2,200,128]{2,1,0:T(8,128)(2,1)S(1)}, bf16[2,200,128]{2,1,0:T(8,128)(2,1)S(1)}, u32[]{:S(2)}, u32[]{:S(2)}) collective-permute-start(bf16[2,200,128]{2,1,0:T(8,128)(2,1)S(1)} %gather.1), channel_id=1, source_target_pairs={{0,3},{1,2},{2,1},{3,0},{4,7},{5,6},{6,5},{7,4},{8,26},{9,27},{10,... | collective-permute-start | bytes 307208 | tf_op jit(solution)/shard_map/gather/ppermute | solution.py:510
  21.9 0.9 %collective-permute-done.7.refs_7_ = bf16[200,128]{1,0:T(8,128)(2,1)S(1)} collective-permute-done((bf16[200,128]{1,0:T(8,128)(2,1)S(1)}, bf16[200,128]{1,0:T(8,128)(2,1)S(1)}, u32[]{:S(2)}, u32[]{:S(2)}) %collective-permute-start.7) | collective-permute-done | bytes 51232 | tf_op jit(solution)/shard_map/gather/ppermute | solution.py:510
  22.8 0.9 %attend.7.refs_10_.refs_0_ = bf16[128,512]{1,0:T(8,128)(2,1)S(1)} custom-call(bf16[72,512]{1,0:T(8,128)(2,1)S(1)} %get-tuple-element.34.refs_0_, bf16[512,128]{1,0:T(8,128)(2,1)S(1)} %get-tuple-element.35.refs_1_, bf16[128,512]{1,0:T(8,128)(2,1)S(1)} %get-tuple-element.36.refs_2_, f32[1,128]{1,0:T(1,128)S(1)} %get-tuple-element.37.refs_3_, ...), custom_call_target="tpu_custom_call" | custom-call | flops 800000000 | bytes 1000000 | tf_op jit(solution)/shard_map/attend/pallas_call | solution.py:520
  23.7 0.9 %attend.8.refs_1_.refs_0_ = bf16[128,512]{1,0:T(8,128)(2,1)S(1)} custom-call(bf16[72,512]{1,0:T(8,128)(2,1)S(1)} %get-tuple-element.34.refs_0_, bf16[512,128]{1,0:T(8,128)(2,1)S(1)} %get-tuple-element.35.refs_1_, bf16[128,512]{1,0:T(8,128)(2,1)S(1)} %get-tuple-element.36.refs_2_, f32[1,128]{1,0:T(1,128)S(1)} %get-tuple-element.37.refs_3_, ...), custom_call_target="tpu_custom_call" | custom-call | flops 800000000 | bytes 1000000 | tf_op jit(solution)/shard_map/attend/pallas_call | solution.py:520
  24.6 0.8 %attend.10.refs_8_.refs_3_ = bf16[1,128,2048]{2,1,0:T(8,128)(2,1)} custom-call(bf16[128,512]{1,0:T(8,128)(2,1)S(1)} %attend.8.refs_1_.refs_0_), custom_call_target="tpu_custom_call" | custom-call | tf_op jit(solution)/shard_map/attend/pallas_call | solution.py:529
  25.5 1.3 %collective-permute-done.13.refs_7_ = bf16[2,200,128]{2,1,0:T(8,128)(2,1)S(1)} collective-permute-done((bf16[2,200,128]{2,1,0:T(8,128)(2,1)S(1)}, bf16[2,200,128]{2,1,0:T(8,128)(2,1)S(1)}, u32[]{:S(2)}, u32[]{:S(2)}) %collective-permute-start.13) | collective-permute-done | bytes 102432 | tf_op jit(solution)/shard_map/gather/ppermute | solution.py:510
  26.8 0.9 %attend.11 = bf16[128,512]{1,0:T(8,128)(2,1)S(1)} custom-call(bf16[72,512]{1,0:T(8,128)(2,1)S(1)} %get-tuple-element.34.refs_0_, bf16[512,128]{1,0:T(8,128)(2,1)S(1)} %get-tuple-element.35.refs_1_, bf16[128,512]{1,0:T(8,128)(2,1)S(1)} %get-tuple-element.36.refs_2_, f32[1,128]{1,0:T(1,128)S(1)} %get-tuple-element.37.refs_3_, ...), custom_call_target="tpu_custom_call" | custom-call | flops 800000000 | bytes 1000000 | tf_op jit(solution)/shard_map/attend/pallas_call | solution.py:520
  27.7 0.9 %attend.12.refs_2_ = bf16[128,512]{1,0:T(8,128)(2,1)S(1)} custom-call(bf16[72,512]{1,0:T(8,128)(2,1)S(1)} %get-tuple-element.34.refs_0_, bf16[512,128]{1,0:T(8,128)(2,1)S(1)} %get-tuple-element.35.refs_1_, bf16[128,512]{1,0:T(8,128)(2,1)S(1)} %get-tuple-element.36.refs_2_, f32[1,128]{1,0:T(1,128)S(1)} %get-tuple-element.37.refs_3_, ...), custom_call_target="tpu_custom_call" | custom-call | flops 800000000 | bytes 1000000 | tf_op jit(solution)/shard_map/attend/pallas_call | solution.py:520
  28.6 0.5 %collective-permute-done.14.refs_1_ = bf16[128,512]{1,0:T(8,128)(2,1)S(1)} collective-permute-done((bf16[128,512]{1,0:T(8,128)(2,1)S(1)}, bf16[128,512]{1,0:T(8,128)(2,1)S(1)}, u32[]{:S(2)}, u32[]{:S(2)}) %collective-permute-start.14) | collective-permute-done | bytes 131104 | tf_op jit(solution)/shard_map/attend/ppermute | solution.py:387
  29.1 0.9 %attend.13 = bf16[1,128,2048]{2,1,0:T(8,128)(2,1)} custom-call(bf16[128,512]{1,0:T(8,128)(2,1)S(1)} %collective-permute-done.10.refs_0_, bf16[128,512]{1,0:T(8,128)(2,1)S(1)} %collective-permute-done.14.refs_1_, bf16[128,512]{1,0:T(8,128)(2,1)S(1)} %attend.12.refs_2_, bf16[1,128,2048]{2,1,0:T(8,128)(2,1)} %attend.10.refs_8_.refs_3_), custom_call_target="tpu_custom_call", output_to_operand_aliasing={{}: (3, {})} | custom-call | tf_op jit(solution)/shard_map/attend/pallas_call | solution.py:529
  (22 shorter events, 1.2 us)
Async XLA Ops:
  1.8 8.3 %collective-permute-start = (bf16[200,128]{1,0:T(8,128)(2,1)S(1)}, bf16[200,128]{1,0:T(8,128)(2,1)S(1)}, u32[]{:S(2)}, u32[]{:S(2)}) collective-permute-start(bf16[200,128]{1,0:T(8,128)(2,1)S(1)} %get-tuple-element.28), channel_id=1, source_target_pairs={{0,3},{1,2},{2,1},{3,0},{4,7},{5,6},{6,5},{7,4},{8,11},{9,10},{10,... | collective-permute-start | bytes 153608 | tf_op jit(solution)/shard_map/fold_sum/ppermute | solution.py:387
  5.8 4.3 %collective-permute-start.1 = (bf16[200,128]{1,0:T(8,128)(2,1)S(1)}, bf16[200,128]{1,0:T(8,128)(2,1)S(1)}, u32[]{:S(2)}, u32[]{:S(2)}) collective-permute-start(bf16[200,128]{1,0:T(8,128)(2,1)S(1)} %get-tuple-element.29), channel_id=1, source_target_pairs={{0,2},{1,3},{2,0},{3,1},{4,6},{5,7},{6,4},{7,5},{8,10},{9,11},{10,... | collective-permute-start | bytes 153608 | tf_op jit(solution)/shard_map/fold_sum/ppermute | solution.py:387
  6.2 4.1 %collective-permute-start.2 = (bf16[200,128]{1,0:T(8,128)(2,1)S(1)}, bf16[200,128]{1,0:T(8,128)(2,1)S(1)}, u32[]{:S(2)}, u32[]{:S(2)}) collective-permute-start(bf16[200,128]{1,0:T(8,128)(2,1)S(1)} %get-tuple-element.30), channel_id=1, source_target_pairs={{0,1},{1,0},{2,3},{3,2},{4,5},{5,4},{6,7},{7,6},{8,9},{9,8},{10,11... | collective-permute-start | bytes 153608 | tf_op jit(solution)/shard_map/fold_sum/ppermute | solution.py:387
  8.2 4.9 %collective-permute-start.3 = (bf16[208,128]{1,0:T(8,128)(2,1)S(1)}, bf16[208,128]{1,0:T(8,128)(2,1)S(1)}, u32[]{:S(2)}, u32[]{:S(2)}) collective-permute-start(bf16[208,128]{1,0:T(8,128)(2,1)S(1)} %encode.1.refs_3_.block_ref.refs_0_), channel_id=1, source_target_pairs={{0,16},{8,24},{16,0},{24,8},{1,17},{9,25},{17,1},{25,9},{2,18},{10... | collective-permute-start | bytes 159752 | tf_op jit(solution)/shard_map/tokens/ppermute | solution.py:387
  10.4 5.1 %collective-permute-start.6 = (bf16[200,128]{1,0:T(8,128)(2,1)S(1)}, bf16[200,128]{1,0:T(8,128)(2,1)S(1)}, u32[]{:S(2)}, u32[]{:S(2)}) collective-permute-start(bf16[200,128]{1,0:T(8,128)(2,1)S(1)} %get-tuple-element.40), channel_id=1, source_target_pairs={{0,4},{1,5},{2,6},{3,7},{4,0},{5,1},{6,2},{7,3},{8,12},{9,13},{10,... | collective-permute-start | bytes 153608 | tf_op jit(solution)/shard_map/fold_sum/ppermute | solution.py:387
  13.0 1.2 %collective-permute-start.4 = (bf16[160,128]{1,0:T(8,128)(2,1)S(1)}, bf16[160,128]{1,0:T(8,128)(2,1)S(1)}, u32[]{:S(2)}, u32[]{:S(2)}) collective-permute-start(bf16[160,128]{1,0:T(8,128)(2,1)S(1)} %pack.3), channel_id=1, source_target_pairs={{0,8},{8,0},{16,24},{24,16},{1,9},{9,1},{17,25},{25,17},{2,10},{10... | collective-permute-start | bytes 122888 | tf_op jit(solution)/shard_map/pack/ppermute | solution.py:387
  13.1 1.4 %collective-permute-start.5 = (bf16[160,128]{1,0:T(8,128)(2,1)S(1)}, bf16[160,128]{1,0:T(8,128)(2,1)S(1)}, u32[]{:S(2)}, u32[]{:S(2)}) collective-permute-start(bf16[160,128]{1,0:T(8,128)(2,1)S(1)} %pack.4), channel_id=1, source_target_pairs={{0,8},{8,0},{16,24},{24,16},{1,9},{9,1},{17,25},{25,17},{2,10},{10... | collective-permute-start | bytes 122888 | tf_op jit(solution)/shard_map/pack/ppermute | solution.py:387
  15.5 4.1 %collective-permute-start.11 = (bf16[200,128]{1,0:T(8,128)(2,1)S(1)}, bf16[200,128]{1,0:T(8,128)(2,1)S(1)}, u32[]{:S(2)}, u32[]{:S(2)}) collective-permute-start(bf16[200,128]{1,0:T(8,128)(2,1)S(1)} %fold_sum.3.refs_6_.own_ref), channel_id=1, source_target_pairs={{0,8},{8,0},{16,24},{24,16},{1,9},{9,1},{17,25},{25,17},{2,10},{10... | collective-permute-start | bytes 153608 | tf_op jit(solution)/shard_map/gather/ppermute | solution.py:387
  15.6 6.3 %collective-permute-start.9 = (bf16[200,128]{1,0:T(8,128)(2,1)S(1)}, bf16[200,128]{1,0:T(8,128)(2,1)S(1)}, u32[]{:S(2)}, u32[]{:S(2)}) collective-permute-start(bf16[200,128]{1,0:T(8,128)(2,1)S(1)} %fold_sum.3.refs_6_.own_ref), channel_id=1, source_target_pairs={{0,16},{1,17},{2,18},{3,19},{4,20},{5,21},{6,22},{7,23},{8,24},{9,... | collective-permute-start | bytes 153608 | tf_op jit(solution)/shard_map/gather/ppermute | solution.py:510
  17.1 4.8 %collective-permute-start.8 = (bf16[200,128]{1,0:T(8,128)(2,1)S(1)}, bf16[200,128]{1,0:T(8,128)(2,1)S(1)}, u32[]{:S(2)}, u32[]{:S(2)}) collective-permute-start(bf16[200,128]{1,0:T(8,128)(2,1)S(1)} %fold_sum.3.refs_6_.own_ref), channel_id=1, source_target_pairs={{0,2},{1,3},{2,0},{3,1},{4,6},{5,7},{6,4},{7,5},{8,10},{9,11},{10,... | collective-permute-start | bytes 153608 | tf_op jit(solution)/shard_map/gather/ppermute | solution.py:510
  18.7 4.1 %collective-permute-start.7 = (bf16[200,128]{1,0:T(8,128)(2,1)S(1)}, bf16[200,128]{1,0:T(8,128)(2,1)S(1)}, u32[]{:S(2)}, u32[]{:S(2)}) collective-permute-start(bf16[200,128]{1,0:T(8,128)(2,1)S(1)} %fold_sum.3.refs_6_.own_ref), channel_id=1, source_target_pairs={{0,1},{1,0},{2,3},{3,2},{4,5},{5,4},{6,7},{7,6},{8,9},{9,8},{10,11... | collective-permute-start | bytes 153608 | tf_op jit(solution)/shard_map/gather/ppermute | solution.py:510
  19.5 7.3 %collective-permute-start.13 = (bf16[2,200,128]{2,1,0:T(8,128)(2,1)S(1)}, bf16[2,200,128]{2,1,0:T(8,128)(2,1)S(1)}, u32[]{:S(2)}, u32[]{:S(2)}) collective-permute-start(bf16[2,200,128]{2,1,0:T(8,128)(2,1)S(1)} %gather.1), channel_id=1, source_target_pairs={{0,17},{1,16},{2,19},{3,18},{4,21},{5,20},{6,23},{7,22},{8,27},{9,... | collective-permute-start | bytes 307208 | tf_op jit(solution)/shard_map/gather/ppermute | solution.py:510
  20.8 6.0 %collective-permute-start.12 = (bf16[2,200,128]{2,1,0:T(8,128)(2,1)S(1)}, bf16[2,200,128]{2,1,0:T(8,128)(2,1)S(1)}, u32[]{:S(2)}, u32[]{:S(2)}) collective-permute-start(bf16[2,200,128]{2,1,0:T(8,128)(2,1)S(1)} %gather.1), channel_id=1, source_target_pairs={{0,3},{1,2},{2,1},{3,0},{4,7},{5,6},{6,5},{7,4},{8,26},{9,27},{10,... | collective-permute-start | bytes 307208 | tf_op jit(solution)/shard_map/gather/ppermute | solution.py:510
  25.4 3.2 %collective-permute-start.10 = (bf16[128,512]{1,0:T(8,128)(2,1)S(1)}, bf16[128,512]{1,0:T(8,128)(2,1)S(1)}, u32[]{:S(2)}, u32[]{:S(2)}) collective-permute-start(bf16[128,512]{1,0:T(8,128)(2,1)S(1)} %attend.9), channel_id=1, source_target_pairs={{0,8},{8,0},{16,24},{24,16},{1,9},{9,1},{17,25},{25,17},{2,10},{10... | collective-permute-start | bytes 393224 | tf_op jit(solution)/shard_map/attend/ppermute | solution.py:387
  27.7 1.4 %collective-permute-start.14 = (bf16[128,512]{1,0:T(8,128)(2,1)S(1)}, bf16[128,512]{1,0:T(8,128)(2,1)S(1)}, u32[]{:S(2)}, u32[]{:S(2)}) collective-permute-start(bf16[128,512]{1,0:T(8,128)(2,1)S(1)} %attend.11), channel_id=1, source_target_pairs={{0,8},{8,0},{16,24},{24,16},{1,9},{9,1},{17,25},{25,17},{2,10},{10... | collective-permute-start | bytes 393224 | tf_op jit(solution)/shard_map/attend/ppermute | solution.py:387

commit v8 on v4

--- a/solution.py
+++ b/solution.py
@@ -495,7 +495,8 @@
         return lax.ppermute(x, ("enc", "seq"), pairs)
 
     with jax.named_scope("gather"):
-        singles = [spread(fresh, (partner, partner)) for partner in neighbours]
+        sent = {partner: spread(fresh, (partner, partner)) for partner in (neighbours[0], *neighbours[:0:-1])}
+        singles = [sent[partner] for partner in neighbours]
         swapped = exchange(swap, "enc", n_enc, 1)
         pair = call(pair_kernel, vmem(2), [folds(bf16, 2)])(fresh, swapped)[0]
         got = [spread(pair, partner_of) for partner_of in zip(*lists)]

time: 29.9 us -> 29.9 us (level)
  no operation moved by 1% of the time
where the time goes in v8:
time: 29.9 us; the launch traced here: 29.8 us
  starting transfers between devices  16.1 us (54%)
  Pallas kernels  9.16 us (31%)
  waiting for transfers between devices  4.36 us (15%)
    ppermute x8, starting transfers between devices, exchange(): return lax.ppermute(x, axis, [(i, i ^ k) for i in range(n)])  9.78 us
    ppermute x5, starting transfers between devices, spread(): return lax.ppermute(x, ('enc', 'seq'), pairs)  6.33 us
    pallas_call x4, Pallas kernels, attend(): call(functools.partial(attend_kernel, len(groups)), vmem(6 + len(groups))...  3.47 us
    ppermute x8, waiting for transfers between devices, exchange(): return lax.ppermute(x, axis, [(i, i ^ k) for i in range(n)])  3.14 us
    pallas_call x1, Pallas kernels, on_device(): call(functools.partial(fold_kernel, len(later)), hbm(4 + len(later)), [ja...  1.75 us
    pallas_call x1, Pallas kernels, on_device(): call(functools.partial(encode_kernel, caps), hbm(2) + vmem(2), [jax.Shape...  1.72 us
    ppermute x5, waiting for transfers between devices, spread(): return lax.ppermute(x, ('enc', 'seq'), pairs)  1.22 us
    pallas_call x1, Pallas kernels, on_device(): pl.pallas_call(functools.partial(output_kernel, heads, neighbours, lists)...  0.91 us
  transfers between devices with their start and end apart: 13, of which 4 were waited for; matrix products, arithmetic and copies ran while one was open for 0% of the time, Pallas kernels for 22%

profile of v8, /device:TPU:0, one launch (start us, length us, event | category | flops | bytes accessed | tf_op | source)
XLA Modules:
  0.0 29.8 jit_solution(3774481109328521407)
XLA Ops:
  0.0 1.8 %fold.1 = (bf16[64,2048]{1,0:T(8,128)(2,1)S(1)}, bf16[1024,512]{1,0:T(8,128)(2,1)S(1)}, bf16[432,512]{1,0:T(8,128)(2,1)S(1)}, f32[1,128]{1,0:T(1,128)S(1)}, f32[...) custom-call(bf16[64,2048]{1,0:T(8,128)(2,1)} %embed_hbm.1, ...), custom_call_target="tpu_custom_call" | custom-call | flops 200000000 | bytes 1000000 | tf_op jit(solution)/shard_map/fold/pallas_call | solution.py:428
  1.8 4.0 %collective-permute-start = (bf16[200,128]{1,0:T(8,128)(2,1)S(1)}, bf16[200,128]{1,0:T(8,128)(2,1)S(1)}, u32[]{:S(2)}, u32[]{:S(2)}) collective-permute-start(bf16[200,128]{1,0:T(8,128)(2,1)S(1)} %get-tuple-element.30), channel_id=1, source_target_pairs={{0,3},{1,2},{2,1},{3,0},{4,7},{5,6},{6,5},{7,4},{8,11},{9,10},{10,... | collective-permute-start | bytes 153608 | tf_op jit(solution)/shard_map/fold_sum/ppermute | solution.py:389
  5.8 0.4 %collective-permute-start.1 = (bf16[200,128]{1,0:T(8,128)(2,1)S(1)}, bf16[200,128]{1,0:T(8,128)(2,1)S(1)}, u32[]{:S(2)}, u32[]{:S(2)}) collective-permute-start(bf16[200,128]{1,0:T(8,128)(2,1)S(1)} %get-tuple-element.31), channel_id=1, source_target_pairs={{0,2},{1,3},{2,0},{3,1},{4,6},{5,7},{6,4},{7,5},{8,10},{9,11},{10,... | collective-permute-start | bytes 153608 | tf_op jit(solution)/shard_map/fold_sum/ppermute | solution.py:389
  6.2 0.2 collective-permute-start.2
  6.4 1.7 %encode.1.refs_3_.refs_0_ = bf16[208,128]{1,0:T(8,128)(2,1)S(1)} custom-call(s32[1,1,3]{2,1,0:T(1,128)} %shape_hbm.1, s32[1,1,2,2]{3,2,1,0:T(2,128)} %plan_hbm.1, bf16[1024,512]{1,0:T(8,128)(2,1)S(1)} %get-tuple-element.33.feat_ref, bf16[432,512]{1,0:T(8,128)(2,1)S(1)} %get-tuple-element.34.conv_ref), custom_call_target="tpu_custom_call" | custom-call | flops 500000000 | bytes 2000000 | tf_op jit(solution)/shard_map/encode/pallas_call | solution.py:444
  8.2 1.9 %collective-permute-start.4 = (bf16[208,128]{1,0:T(8,128)(2,1)S(1)}, bf16[208,128]{1,0:T(8,128)(2,1)S(1)}, u32[]{:S(2)}, u32[]{:S(2)}) collective-permute-start(bf16[208,128]{1,0:T(8,128)(2,1)S(1)} %encode.1.refs_3_.refs_0_), channel_id=1, source_target_pairs={{0,16},{8,24},{16,0},{24,8},{1,17},{9,25},{17,1},{25,9},{2,18},{10... | collective-permute-start | bytes 159752 | tf_op jit(solution)/shard_map/tokens/ppermute | solution.py:389
  10.1 0.3 collective-permute-done.2.refs_2_
  10.4 2.7 %collective-permute-start.3 = (bf16[200,128]{1,0:T(8,128)(2,1)S(1)}, bf16[200,128]{1,0:T(8,128)(2,1)S(1)}, u32[]{:S(2)}, u32[]{:S(2)}) collective-permute-start(bf16[200,128]{1,0:T(8,128)(2,1)S(1)} %get-tuple-element.36), channel_id=1, source_target_pairs={{0,4},{1,5},{2,6},{3,7},{4,0},{5,1},{6,2},{7,3},{8,12},{9,13},{10,... | collective-permute-start | bytes 153608 | tf_op jit(solution)/shard_map/fold_sum/ppermute | solution.py:389
  13.0 2.4 %collective-permute-done.3.got_ref = bf16[200,128]{1,0:T(8,128)(2,1)S(1)} collective-permute-done((bf16[200,128]{1,0:T(8,128)(2,1)S(1)}, bf16[200,128]{1,0:T(8,128)(2,1)S(1)}, u32[]{:S(2)}, u32[]{:S(2)}) %collective-permute-start.3) | collective-permute-done | bytes 51232 | tf_op jit(solution)/shard_map/fold_sum/ppermute | solution.py:389
  15.6 1.6 %collective-permute-start.8 = (bf16[200,128]{1,0:T(8,128)(2,1)S(1)}, bf16[200,128]{1,0:T(8,128)(2,1)S(1)}, u32[]{:S(2)}, u32[]{:S(2)}) collective-permute-start(bf16[200,128]{1,0:T(8,128)(2,1)S(1)} %get-tuple-element.37.own_ref.refs_6_), channel_id=1, source_target_pairs={{0,16},{1,17},{2,18},{3,19},{4,20},{5,21},{6,22},{7,23},{8,24},{9,... | collective-permute-start | bytes 153608 | tf_op jit(solution)/shard_map/gather/ppermute | solution.py:495
  17.1 1.6 %collective-permute-start.7 = (bf16[200,128]{1,0:T(8,128)(2,1)S(1)}, bf16[200,128]{1,0:T(8,128)(2,1)S(1)}, u32[]{:S(2)}, u32[]{:S(2)}) collective-permute-start(bf16[200,128]{1,0:T(8,128)(2,1)S(1)} %get-tuple-element.37.own_ref.refs_6_), channel_id=1, source_target_pairs={{0,2},{1,3},{2,0},{3,1},{4,6},{5,7},{6,4},{7,5},{8,10},{9,11},{10,... | collective-permute-start | bytes 153608 | tf_op jit(solution)/shard_map/gather/ppermute | solution.py:495
  18.7 0.5 %collective-permute-start.6 = (bf16[200,128]{1,0:T(8,128)(2,1)S(1)}, bf16[200,128]{1,0:T(8,128)(2,1)S(1)}, u32[]{:S(2)}, u32[]{:S(2)}) collective-permute-start(bf16[200,128]{1,0:T(8,128)(2,1)S(1)} %get-tuple-element.37.own_ref.refs_6_), channel_id=1, source_target_pairs={{0,1},{1,0},{2,3},{3,2},{4,5},{5,4},{6,7},{7,6},{8,9},{9,8},{10,11... | collective-permute-start | bytes 153608 | tf_op jit(solution)/shard_map/gather/ppermute | solution.py:495
  19.3 1.5 %collective-permute-start.11 = (bf16[2,200,128]{2,1,0:T(8,128)(2,1)S(1)}, bf16[2,200,128]{2,1,0:T(8,128)(2,1)S(1)}, u32[]{:S(2)}, u32[]{:S(2)}) collective-permute-start(bf16[2,200,128]{2,1,0:T(8,128)(2,1)S(1)} %gather.1.first_ref), channel_id=1, source_target_pairs={{0,17},{1,16},{2,19},{3,18},{4,21},{5,20},{6,23},{7,22},{8,27},{9,... | collective-permute-start | bytes 307208 | tf_op jit(solution)/shard_map/gather/ppermute | solution.py:495
  20.8 1.1 %collective-permute-start.10 = (bf16[2,200,128]{2,1,0:T(8,128)(2,1)S(1)}, bf16[2,200,128]{2,1,0:T(8,128)(2,1)S(1)}, u32[]{:S(2)}, u32[]{:S(2)}) collective-permute-start(bf16[2,200,128]{2,1,0:T(8,128)(2,1)S(1)} %gather.1.first_ref), channel_id=1, source_target_pairs={{0,3},{1,2},{2,1},{3,0},{4,7},{5,6},{6,5},{7,4},{8,26},{9,27},{10,... | collective-permute-start | bytes 307208 | tf_op jit(solution)/shard_map/gather/ppermute | solution.py:495
  21.9 0.5 %gram.1.gram_ref = bf16[128,64]{1,0:T(8,128)(2,1)S(1)} custom-call(bf16[64,2048]{1,0:T(8,128)(2,1)S(1)} %get-tuple-element.28.embed_ref, bf16[2,200,128]{2,1,0:T(8,128)(2,1)S(1)} %gather.1.first_ref), custom_call_target="tpu_custom_call" | custom-call | flops 1000000 | bytes 1000000 | tf_op jit(solution)/shard_map/gram/pallas_call | solution.py:505
  22.4 0.7 %pack.1 = (bf16[72,512]{1,0:T(8,128)(2,1)S(1)}, bf16[512,128]{1,0:T(8,128)(2,1)S(1)}, bf16[128,512]{1,0:T(8,128)(2,1)S(1)}, f32[1,128]{1,0:T(1,128)S(1)}, bf16[1...) custom-call(f32[1,128]{1,0:T(1,128)S(1)} %get-tuple-element.26.q_gai, ...), custom_call_target="tpu_custom_call" | custom-call | flops 1000000 | bytes 1000000 | tf_op jit(solution)/shard_map/pack/pallas_call | solution.py:508
  23.2 0.9 %attend.6.refs_10_.refs_0_ = bf16[128,512]{1,0:T(8,128)(2,1)S(1)} custom-call(bf16[72,512]{1,0:T(8,128)(2,1)S(1)} %get-tuple-element.39.refs_0_, bf16[512,128]{1,0:T(8,128)(2,1)S(1)} %get-tuple-element.40.refs_1_, bf16[128,512]{1,0:T(8,128)(2,1)S(1)} %get-tuple-element.41.refs_2_, f32[1,128]{1,0:T(1,128)S(1)} %get-tuple-element.42.refs_3_, ...), custom_call_target="tpu_custom_call" | custom-call | flops 800000000 | bytes 1000000 | tf_op jit(solution)/shard_map/attend/pallas_call | solution.py:523
  24.1 0.9 %attend.7.refs_1_.refs_8_.own_early_ref = bf16[128,512]{1,0:T(8,128)(2,1)S(1)} custom-call(bf16[72,512]{1,0:T(8,128)(2,1)S(1)} %get-tuple-element.39.refs_0_, bf16[512,128]{1,0:T(8,128)(2,1)S(1)} %get-tuple-element.40.refs_1_, bf16[128,512]{1,0:T(8,128)(2,1)S(1)} %get-tuple-element.41.refs_2_, f32[1,128]{1,0:T(1,128)S(1)} %get-tuple-element.42.refs_3_, ...), custom_call_target="tpu_custom_call" | custom-call | flops 800000000 | bytes 1000000 | tf_op jit(solution)/shard_map/attend/pallas_call | solution.py:523
  24.9 0.4 %collective-permute-start.9 = (bf16[128,512]{1,0:T(8,128)(2,1)S(1)}, bf16[128,512]{1,0:T(8,128)(2,1)S(1)}, u32[]{:S(2)}, u32[]{:S(2)}) collective-permute-start(bf16[128,512]{1,0:T(8,128)(2,1)S(1)} %attend.8), channel_id=1, source_target_pairs={{0,8},{8,0},{16,24},{24,16},{1,9},{9,1},{17,25},{25,17},{2,10},{10... | collective-permute-start | bytes 393224 | tf_op jit(solution)/shard_map/attend/ppermute | solution.py:389
  25.3 1.2 %collective-permute-done.11.refs_7_ = bf16[2,200,128]{2,1,0:T(8,128)(2,1)S(1)} collective-permute-done((bf16[2,200,128]{2,1,0:T(8,128)(2,1)S(1)}, bf16[2,200,128]{2,1,0:T(8,128)(2,1)S(1)}, u32[]{:S(2)}, u32[]{:S(2)}) %collective-permute-start.11) | collective-permute-done | bytes 102432 | tf_op jit(solution)/shard_map/gather/ppermute | solution.py:495
  26.6 0.9 %attend.9 = bf16[128,512]{1,0:T(8,128)(2,1)S(1)} custom-call(bf16[72,512]{1,0:T(8,128)(2,1)S(1)} %get-tuple-element.39.refs_0_, bf16[512,128]{1,0:T(8,128)(2,1)S(1)} %get-tuple-element.40.refs_1_, bf16[128,512]{1,0:T(8,128)(2,1)S(1)} %get-tuple-element.41.refs_2_, f32[1,128]{1,0:T(1,128)S(1)} %get-tuple-element.42.refs_3_, ...), custom_call_target="tpu_custom_call" | custom-call | flops 800000000 | bytes 1000000 | tf_op jit(solution)/shard_map/attend/pallas_call | solution.py:523
  27.5 0.9 %attend.10.own_rest_ref = bf16[128,512]{1,0:T(8,128)(2,1)S(1)} custom-call(bf16[72,512]{1,0:T(8,128)(2,1)S(1)} %get-tuple-element.39.refs_0_, bf16[512,128]{1,0:T(8,128)(2,1)S(1)} %get-tuple-element.40.refs_1_, bf16[128,512]{1,0:T(8,128)(2,1)S(1)} %get-tuple-element.41.refs_2_, f32[1,128]{1,0:T(1,128)S(1)} %get-tuple-element.42.refs_3_, ...), custom_call_target="tpu_custom_call" | custom-call | flops 800000000 | bytes 1000000 | tf_op jit(solution)/shard_map/attend/pallas_call | solution.py:523
  28.4 0.5 %collective-permute-done.12.near_rest_ref = bf16[128,512]{1,0:T(8,128)(2,1)S(1)} collective-permute-done((bf16[128,512]{1,0:T(8,128)(2,1)S(1)}, bf16[128,512]{1,0:T(8,128)(2,1)S(1)}, u32[]{:S(2)}, u32[]{:S(2)}) %collective-permute-start.12) | collective-permute-done | bytes 131104 | tf_op jit(solution)/shard_map/attend/ppermute | solution.py:389
  28.8 0.9 %attend.11 = bf16[1,128,2048]{2,1,0:T(8,128)(2,1)} custom-call(bf16[128,512]{1,0:T(8,128)(2,1)S(1)} %collective-permute-done.9.near_early_ref, bf16[128,512]{1,0:T(8,128)(2,1)S(1)} %collective-permute-done.12.near_rest_ref, bf16[128,512]{1,0:T(8,128)(2,1)S(1)} %attend.7.refs_1_.refs_8_.own_early_ref, bf16[128,512]{1,0:T(8,128)(2,1)S(1)} %attend.10.own_rest_ref), custom_call_target="tpu_custom_call" | custom-call | tf_op jit(solution)/shard_map/attend/pallas_call | solution.py:538
  (15 shorter events, 0.3 us)
Async XLA Ops:
  1.8 8.3 %collective-permute-start = (bf16[200,128]{1,0:T(8,128)(2,1)S(1)}, bf16[200,128]{1,0:T(8,128)(2,1)S(1)}, u32[]{:S(2)}, u32[]{:S(2)}) collective-permute-start(bf16[200,128]{1,0:T(8,128)(2,1)S(1)} %get-tuple-element.30), channel_id=1, source_target_pairs={{0,3},{1,2},{2,1},{3,0},{4,7},{5,6},{6,5},{7,4},{8,11},{9,10},{10,... | collective-permute-start | bytes 153608 | tf_op jit(solution)/shard_map/fold_sum/ppermute | solution.py:389
  5.8 4.3 %collective-permute-start.1 = (bf16[200,128]{1,0:T(8,128)(2,1)S(1)}, bf16[200,128]{1,0:T(8,128)(2,1)S(1)}, u32[]{:S(2)}, u32[]{:S(2)}) collective-permute-start(bf16[200,128]{1,0:T(8,128)(2,1)S(1)} %get-tuple-element.31), channel_id=1, source_target_pairs={{0,2},{1,3},{2,0},{3,1},{4,6},{5,7},{6,4},{7,5},{8,10},{9,11},{10,... | collective-permute-start | bytes 153608 | tf_op jit(solution)/shard_map/fold_sum/ppermute | solution.py:389
  6.2 4.1 %collective-permute-start.2 = (bf16[200,128]{1,0:T(8,128)(2,1)S(1)}, bf16[200,128]{1,0:T(8,128)(2,1)S(1)}, u32[]{:S(2)}, u32[]{:S(2)}) collective-permute-start(bf16[200,128]{1,0:T(8,128)(2,1)S(1)} %get-tuple-element.32), channel_id=1, source_target_pairs={{0,1},{1,0},{2,3},{3,2},{4,5},{5,4},{6,7},{7,6},{8,9},{9,8},{10,11... | collective-permute-start | bytes 153608 | tf_op jit(solution)/shard_map/fold_sum/ppermute | solution.py:389
  8.2 4.9 %collective-permute-start.4 = (bf16[208,128]{1,0:T(8,128)(2,1)S(1)}, bf16[208,128]{1,0:T(8,128)(2,1)S(1)}, u32[]{:S(2)}, u32[]{:S(2)}) collective-permute-start(bf16[208,128]{1,0:T(8,128)(2,1)S(1)} %encode.1.refs_3_.refs_0_), channel_id=1, source_target_pairs={{0,16},{8,24},{16,0},{24,8},{1,17},{9,25},{17,1},{25,9},{2,18},{10... | collective-permute-start | bytes 159752 | tf_op jit(solution)/shard_map/tokens/ppermute | solution.py:389
  10.4 5.1 %collective-permute-start.3 = (bf16[200,128]{1,0:T(8,128)(2,1)S(1)}, bf16[200,128]{1,0:T(8,128)(2,1)S(1)}, u32[]{:S(2)}, u32[]{:S(2)}) collective-permute-start(bf16[200,128]{1,0:T(8,128)(2,1)S(1)} %get-tuple-element.36), channel_id=1, source_target_pairs={{0,4},{1,5},{2,6},{3,7},{4,0},{5,1},{6,2},{7,3},{8,12},{9,13},{10,... | collective-permute-start | bytes 153608 | tf_op jit(solution)/shard_map/fold_sum/ppermute | solution.py:389
  15.5 3.8 %collective-permute-start.5 = (bf16[3,200,128]{2,1,0:T(8,128)(2,1)S(1)}, bf16[3,200,128]{2,1,0:T(8,128)(2,1)S(1)}, u32[]{:S(2)}, u32[]{:S(2)}) collective-permute-start(bf16[3,200,128]{2,1,0:T(8,128)(2,1)S(1)} %get-tuple-element.38), channel_id=1, source_target_pairs={{0,8},{8,0},{16,24},{24,16},{1,9},{9,1},{17,25},{25,17},{2,10},{10... | collective-permute-start | bytes 460808 | tf_op jit(solution)/shard_map/gather/ppermute | solution.py:389
  15.6 7.6 %collective-permute-start.8 = (bf16[200,128]{1,0:T(8,128)(2,1)S(1)}, bf16[200,128]{1,0:T(8,128)(2,1)S(1)}, u32[]{:S(2)}, u32[]{:S(2)}) collective-permute-start(bf16[200,128]{1,0:T(8,128)(2,1)S(1)} %get-tuple-element.37.own_ref.refs_6_), channel_id=1, source_target_pairs={{0,16},{1,17},{2,18},{3,19},{4,20},{5,21},{6,22},{7,23},{8,24},{9,... | collective-permute-start | bytes 153608 | tf_op jit(solution)/shard_map/gather/ppermute | solution.py:495
  17.1 6.0 %collective-permute-start.7 = (bf16[200,128]{1,0:T(8,128)(2,1)S(1)}, bf16[200,128]{1,0:T(8,128)(2,1)S(1)}, u32[]{:S(2)}, u32[]{:S(2)}) collective-permute-start(bf16[200,128]{1,0:T(8,128)(2,1)S(1)} %get-tuple-element.37.own_ref.refs_6_), channel_id=1, source_target_pairs={{0,2},{1,3},{2,0},{3,1},{4,6},{5,7},{6,4},{7,5},{8,10},{9,11},{10,... | collective-permute-start | bytes 153608 | tf_op jit(solution)/shard_map/gather/ppermute | solution.py:495
  18.7 4.5 %collective-permute-start.6 = (bf16[200,128]{1,0:T(8,128)(2,1)S(1)}, bf16[200,128]{1,0:T(8,128)(2,1)S(1)}, u32[]{:S(2)}, u32[]{:S(2)}) collective-permute-start(bf16[200,128]{1,0:T(8,128)(2,1)S(1)} %get-tuple-element.37.own_ref.refs_6_), channel_id=1, source_target_pairs={{0,1},{1,0},{2,3},{3,2},{4,5},{5,4},{6,7},{7,6},{8,9},{9,8},{10,11... | collective-permute-start | bytes 153608 | tf_op jit(solution)/shard_map/gather/ppermute | solution.py:495
  19.3 7.2 %collective-permute-start.11 = (bf16[2,200,128]{2,1,0:T(8,128)(2,1)S(1)}, bf16[2,200,128]{2,1,0:T(8,128)(2,1)S(1)}, u32[]{:S(2)}, u32[]{:S(2)}) collective-permute-start(bf16[2,200,128]{2,1,0:T(8,128)(2,1)S(1)} %gather.1.first_ref), channel_id=1, source_target_pairs={{0,17},{1,16},{2,19},{3,18},{4,21},{5,20},{6,23},{7,22},{8,27},{9,... | collective-permute-start | bytes 307208 | tf_op jit(solution)/shard_map/gather/ppermute | solution.py:495
  20.8 5.8 %collective-permute-start.10 = (bf16[2,200,128]{2,1,0:T(8,128)(2,1)S(1)}, bf16[2,200,128]{2,1,0:T(8,128)(2,1)S(1)}, u32[]{:S(2)}, u32[]{:S(2)}) collective-permute-start(bf16[2,200,128]{2,1,0:T(8,128)(2,1)S(1)} %gather.1.first_ref), channel_id=1, source_target_pairs={{0,3},{1,2},{2,1},{3,0},{4,7},{5,6},{6,5},{7,4},{8,26},{9,27},{10,... | collective-permute-start | bytes 307208 | tf_op jit(solution)/shard_map/gather/ppermute | solution.py:495
  24.9 3.4 %collective-permute-start.9 = (bf16[128,512]{1,0:T(8,128)(2,1)S(1)}, bf16[128,512]{1,0:T(8,128)(2,1)S(1)}, u32[]{:S(2)}, u32[]{:S(2)}) collective-permute-start(bf16[128,512]{1,0:T(8,128)(2,1)S(1)} %attend.8), channel_id=1, source_target_pairs={{0,8},{8,0},{16,24},{24,16},{1,9},{9,1},{17,25},{25,17},{2,10},{10... | collective-permute-start | bytes 393224 | tf_op jit(solution)/shard_map/attend/ppermute | solution.py:389
  27.4 1.4 %collective-permute-start.12 = (bf16[128,512]{1,0:T(8,128)(2,1)S(1)}, bf16[128,512]{1,0:T(8,128)(2,1)S(1)}, u32[]{:S(2)}, u32[]{:S(2)}) collective-permute-start(bf16[128,512]{1,0:T(8,128)(2,1)S(1)} %attend.9), channel_id=1, source_target_pairs={{0,8},{8,0},{16,24},{24,16},{1,9},{9,1},{17,25},{25,17},{2,10},{10... | collective-permute-start | bytes 393224 | tf_op jit(solution)/shard_map/attend/ppermute | solution.py:389
